TPU v7x, 32 devices: a whole 2x2x4 slice. The times are simulated.
32 devices in a mesh: groups: 2 (over y), ctx: 4 (over z), head: 4 (over x, core).
Axes of the slice: x: 2, y: 2, z: 4, core: 2. Of those that a mesh axis runs over, the one named last changes fastest.
Arguments:
- queries: bfloat16 [1024, 32, 128], P(('groups', 'ctx'), 'head'), parts along dimension 0, may hold values from -16 to 16
- positions: int32 [1024], P(('groups', 'ctx')), parts along dimension 0, may hold values from 4096 to 6143
- key_codes: bfloat16 [4, 4096, 128], P('groups', 'ctx'), parts along dimension 0, may hold values from -16 to 16
- value_codes: bfloat16 [4, 4096, 128], P('groups', 'ctx'), parts along dimension 0, may hold values from -8 to 8
- scale_index: int32 [4, 2, 32], P('groups', None, 'ctx'), parts along dimension 0, may hold values from 0 to 15
- scale_table: float32 [2, 16], replicated, may hold values from 0.5 to 2
- block_lists: int32 [64, 4, 8], P(('groups', 'head')), parts along dimension 0, may hold values from 0 to 31, as said below
Outputs:
- attended: bfloat16 [1024, 4096], P(('groups', 'ctx', 'head')), parts along dimension 0
There are 2 independent parts, one for each index of `groups`. A program takes and returns all parts, laid end to end along the dimension named above; an argument that names none is the same for every part. Nothing has to cross between parts.
Inputs may be any that keep to these rules, and one draw needn't show every extreme that they name: For query head h and query block b, block_lists[h, b, :] names 8 different key blocks. Call the rows of b's index of ctx (a run of 128 rows) its shard c; every listed block lies on a key shard (a run of 1024 keys) at most 1 shards from c counted around the closed cycle of key shards in either direction, and at least one listed block lies exactly 1 shards away.
All inputs are finite; a program needn't handle non-finite values.
Results may differ from a plain program's by a relative error of at most 0.0065.
The roundings to bfloat16 on the way count: a program that leaves them out, or rounds other values in their place, can miss the bound.
Values may be sent and summed in bfloat16 or wider, within the bound.
No kernel may reach another device: no remote copies, remote signals or barrier semaphores. Data moves between devices by JAX's collectives and lax.ppermute only.
A program may use at most 64 MiB of HBM per device.

v0:
```python
import math

import jax
import jax.numpy as jnp
from jax import lax
from jax.sharding import PartitionSpec as P

GROUP = 16
BLOCK = 128


ROPE_BASE = 500000.0
FLOOR_VALUE = -1e30


def shifted(x, axis, by):
    count = lax.axis_size(axis)
    return lax.ppermute(x, axis, [(i, (i + by) % count) for i in range(count)])


def rotate(queries, positions):
    halves = queries.shape[2] // 2
    frequency = ROPE_BASE ** (-2.0 * jnp.arange(halves, dtype=jnp.float32) / queries.shape[2])
    angles = positions.astype(jnp.float32)[:, None] * frequency[None, :]
    cosine = jnp.cos(angles)[:, None, :]
    sine_value = jnp.sin(angles)[:, None, :]
    paired = queries.astype(jnp.float32).reshape(queries.shape[0], queries.shape[1], halves, 2)
    even_part = paired[..., 0]
    odd_part = paired[..., 1]
    turned = jnp.stack(
        [even_part * cosine - odd_part * sine_value, even_part * sine_value + odd_part * cosine],
        axis=-1,
    )
    return turned.reshape(queries.shape).astype(jnp.bfloat16)


def scale_pair(key_codes, value_codes, scale_index, scale_table, kv_head):
    key_rows = lax.dynamic_index_in_dim(key_codes, kv_head, 0, keepdims=False)
    value_rows = lax.dynamic_index_in_dim(value_codes, kv_head, 0, keepdims=False)
    index_rows = lax.dynamic_index_in_dim(scale_index, kv_head, 1, keepdims=False)
    matches = (
        index_rows[:, :, None] == jnp.arange(scale_table.shape[1], dtype=jnp.int32)[None, None, :]
    )
    picked = jnp.sum(jnp.where(matches, scale_table[:, None, :], 0.0), axis=2)
    keys_dev, head_width = key_rows.shape
    stacked = jnp.stack([key_rows, value_rows]).astype(jnp.float32)
    blocks = stacked.reshape(2, keys_dev // BLOCK, BLOCK, head_width) * picked[:, :, None, None]
    return blocks.reshape(2, keys_dev, head_width).astype(jnp.bfloat16)


def block_partial(rotated, lists_rows, scaled_pair, key_shard):
    rows_dev, heads_dev, head_width = rotated.shape
    keys_dev = scaled_pair.shape[1]
    query_blocks = rows_dev // BLOCK
    key_blocks = keys_dev // BLOCK
    targets = key_shard * key_blocks + jnp.arange(key_blocks, dtype=jnp.int32)
    block_mask = jnp.any(lists_rows[:, :, :, None] == targets[None, None, None, :], axis=2)
    scores = jnp.einsum(
        "rhd,kd->hrk", rotated, scaled_pair[0], preferred_element_type=jnp.float32
    ) / math.sqrt(head_width)
    scores = scores.reshape(heads_dev, query_blocks, BLOCK, key_blocks, BLOCK)
    allowed = block_mask[:, :, None, :, None]
    local_max = jnp.max(jnp.where(allowed, scores, FLOOR_VALUE), axis=(3, 4))
    weights = jnp.where(allowed, jnp.exp(scores - local_max[:, :, :, None, None]), 0.0)
    local_sum = jnp.sum(weights, axis=(3, 4)).reshape(heads_dev, rows_dev)
    weights_low = weights.astype(jnp.bfloat16).reshape(heads_dev, rows_dev, keys_dev)
    local_out = jnp.einsum(
        "hrk,kd->rhd", weights_low, scaled_pair[1], preferred_element_type=jnp.float32
    )
    return (local_max.reshape(heads_dev, rows_dev), local_sum, local_out)


def combine(earlier, arrived):
    joined_max = jnp.maximum(earlier[0], arrived[0])
    first_factor = jnp.exp(earlier[0] - joined_max)
    second_factor = jnp.exp(arrived[0] - joined_max)
    joined_sum = first_factor * earlier[1] + second_factor * arrived[1]
    joined_out = first_factor.T[:, :, None] * earlier[2] + second_factor.T[:, :, None] * arrived[2]
    return (joined_max, joined_sum, joined_out)


def on_device(queries, positions, key_codes, value_codes, scale_index, scale_table, block_lists):
    cycle_size = lax.axis_size("ctx")
    cycle_place = lax.axis_index("ctx")
    head_place = lax.axis_index("head")
    reach_hops = min(3, (cycle_size - 1) // 2)
    rows_dev, heads_dev, head_width = queries.shape
    blocks_held = rows_dev // BLOCK
    kv_head = head_place * heads_dev // GROUP
    scaled_pair = scale_pair(key_codes, value_codes, scale_index, scale_table, kv_head)
    rotated = rotate(queries, positions)

    def visit_shard(held_rows, home_shard, pair_here, key_shard):
        lists_rows = lax.dynamic_slice_in_dim(block_lists, home_shard * blocks_held, blocks_held, 1)
        return block_partial(held_rows, lists_rows, pair_here, key_shard)

    running = visit_shard(rotated, cycle_place, scaled_pair, cycle_place)
    ahead_pair = scaled_pair
    behind_pair = scaled_pair
    for offset in range(1, reach_hops + 1):
        ahead_pair = shifted(ahead_pair, "ctx", 1)
        running = combine(
            running,
            visit_shard(
                rotated, cycle_place, ahead_pair, jnp.mod(cycle_place - offset, cycle_size)
            ),
        )
        behind_pair = shifted(behind_pair, "ctx", -1)
        running = combine(
            running,
            visit_shard(
                rotated, cycle_place, behind_pair, jnp.mod(cycle_place + offset, cycle_size)
            ),
        )
    joined_max, joined_sum, joined_out = running
    normalized = (
        (joined_out / joined_sum.T[:, :, None])
        .astype(jnp.bfloat16)
        .reshape(rows_dev, heads_dev * head_width)
    )
    return lax.all_to_all(normalized, "head", split_axis=0, concat_axis=1, tiled=True)


def solution(mesh):
    placed = (
        P(("groups", "ctx"), "head", None),
        P(("groups", "ctx")),
        P("groups", "ctx", None),
        P("groups", "ctx", None),
        P("groups", None, "ctx"),
        P(),
        P(("groups", "head"), None, None),
    )
    return jax.shard_map(
        on_device,
        mesh=mesh,
        in_specs=placed,
        out_specs=P(("groups", "ctx", "head"), None),
        check_vma=False,
    )
```

profile of v0, /device:TPU:0, one launch (start us, length us, event | category | flops | bytes accessed | tf_op | source)
XLA Modules:
  0.0 53.1 jit_solution(6652843286546882741)
XLA Ops:
  0.0 0.7 %constant_dynamic-slice_fusion = s32[2,1,8]{2,1,0:T(1,128)S(1)} fusion(s32[2,2,8]{2,1,0:T(2,128)} %param.11, s32[]{:T(128)S(6)} %select_n.76), kind=kLoop, calls=%fused_computation.78 | loop fusion | bytes 132 | tf_op jit(solution)/shard_map/jit(dynamic_index_in_dim)/dynamic_slice | solution.py:40
  0.7 0.8 %select_reduce_fusion = f32[2,8]{1,0:T(2,128)S(1)} fusion(f32[2,16]{1,0:T(2,128)} %param.12, s32[2,8]{1,0:T(2,128)S(1)} %bitcast.203), kind=kLoop, calls=%fused_computation.60 | loop fusion | flops 752 | bytes 256 | tf_op jit(solution)/shard_map/reduce_sum | solution.py:44
  1.6 1.1 %constant_dynamic-slice_fusion.1 = (bf16[1,1024,128]{2,1,0:T(8,128)(2,1)S(1)}, bf16[1,1024,128]{2,1,0:T(8,128)(2,1)S(1)}) fusion(bf16[2,1024,128]{2,1,0:T(8,128)(2,1)} %param.10, s32[]{:T(128)S(6)} %select_n.76, bf16[2,1024,128]{2,1,0:T(8,128)(2,1)} %param.9), kind=kLoop, calls=%fused_computation.79 | loop fusion | bytes 1048580 | tf_op jit(solution)/shard_map/jit(dynamic_index_in_dim)/dynamic_slice | solution.py:39
  2.7 0.3 multiply_convert_fusion
  3.0 5.1 %collective-permute-start.1 = (bf16[2,1024,128]{2,1,0:T(8,128)(2,1)S(1)}, bf16[2,1024,128]{2,1,0:T(8,128)(2,1)S(1)}, u32[]{:S(2)}, u32[]{:S(2)}) collective-permute-start(bf16[2,1024,128]{2,1,0:T(8,128)(2,1)S(1)} %multiply_convert_fusion), channel_id=1, source_target_pairs={{0,12},{4,0},{8,4},{12,8},{1,13},{5,1},{9,5},{13,9},{2,14},{6,2},{... | collective-permute-start | bytes 1572872 | tf_op jit(solution)/shard_map/ppermute | solution.py:18
  8.2 0.7 %convert_element_type.53 = f32[128]{0:T(128)S(1)} convert(s32[128]{0:T(128)} %param.8) | non-fusion elementwise | flops 128 | bytes 1024 | tf_op jit(solution)/shard_map/convert_element_type | solution.py:24
  8.9 0.1 compare_reduce_fusion.2
  9.4 1.2 %copy.45 = bf16[128,8,128]{0,1,2:T(8,128)(2,1)S(1)} copy(bf16[128,8,128]{2,1,0:T(8,128)(2,1)} %param.7) | data formatting | bytes 524288 | tf_op args[0]
  10.6 0.2 multiply_cosine_fusion
  11.0 0.2 copy.46
  11.2 1.2 %fusion.6 = (f32[8,128]{1,0:T(8,128)S(1)}, f32[1024,128,8]{1,0,2:T(8,128)S(1)}) fusion(pred[8,1024]{1,0:T(8,128)(4,1)S(1)} %broadcast_bitcast_fusion.2, bf16[128,8,128]{2,0,1:T(8,128)(2,1)S(1)} %copy.46, bf16[2,1024,128]{2,1,0:T(8,128)(2,1)S(1)} %multiply_convert_fusion), kind=kOutput, calls=%fused_computation.12 | convolution fusion | flops 271580160 | bytes 4730880 | tf_op jit(solution)/shard_map/rhd,kd->hrk/dot_general | solution.py:58
  12.5 2.4 %fusion.9 = f32[8,128]{1,0:T(8,128)S(1)} fusion(f32[1024,128,8]{1,0,2:T(8,128)S(1)} %get-tuple-element.22, f32[8,128]{1,0:T(8,128)S(1)} %get-tuple-element.21, pred[8,1024]{1,0:T(8,128)(4,1)S(1)} %broadcast_bitcast_fusion.2), kind=kLoop, calls=%fused_computation.15 | loop fusion | flops 4193280 | bytes 4210688 | tf_op jit(solution)/shard_map/reduce_sum | solution.py:65
  14.9 16.6 %collective-permute-done = bf16[2,1024,128]{2,1,0:T(8,128)(2,1)S(1)} collective-permute-done((bf16[2,1024,128]{2,1,0:T(8,128)(2,1)S(1)}, bf16[2,1024,128]{2,1,0:T(8,128)(2,1)S(1)}, u32[]{:S(2)}, u32[]{:S(2)}) %collective-permute-start) | collective-permute-done | bytes 524320 | tf_op jit(solution)/shard_map/ppermute | solution.py:18
  31.5 1.2 %fusion.3 = (f32[8,128]{1,0:T(8,128)S(1)}, f32[1024,128,8]{1,0,2:T(8,128)S(1)}) fusion(pred[8,1024]{1,0:T(8,128)(4,1)S(1)} %broadcast_bitcast_fusion.1, bf16[128,8,128]{2,0,1:T(8,128)(2,1)S(1)} %copy.46, bf16[2,1024,128]{2,1,0:T(8,128)(2,1)S(1)} %collective-permute-done), kind=kOutput, calls=%fused_computation.7 | convolution fusion | flops 271580160 | bytes 4730880 | tf_op jit(solution)/shard_map/rhd,kd->hrk/dot_general | solution.py:58
  32.7 2.4 %fusion.11 = f32[8,128]{1,0:T(8,128)S(1)} fusion(f32[1024,128,8]{1,0,2:T(8,128)S(1)} %get-tuple-element.20, f32[8,128]{1,0:T(8,128)S(1)} %get-tuple-element.19, pred[8,1024]{1,0:T(8,128)(4,1)S(1)} %broadcast_bitcast_fusion.1), kind=kLoop, calls=%fused_computation.17 | loop fusion | flops 4193280 | bytes 4210688 | tf_op jit(solution)/shard_map/reduce_sum | solution.py:65
  35.1 1.2 %fusion = (f32[8,128]{1,0:T(8,128)S(1)}, f32[1024,128,8]{1,0,2:T(8,128)S(1)}) fusion(pred[8,1024]{1,0:T(8,128)(4,1)S(1)} %broadcast_bitcast_fusion, bf16[128,8,128]{2,0,1:T(8,128)(2,1)S(1)} %copy.46, bf16[2,1024,128]{2,1,0:T(8,128)(2,1)S(1)} %collective-permute-done.1), kind=kOutput, calls=%fused_computation.2 | convolution fusion | flops 271580160 | bytes 4730880 | tf_op jit(solution)/shard_map/rhd,kd->hrk/dot_general | solution.py:58
  36.3 2.4 %fusion.13 = f32[8,128]{1,0:T(8,128)S(1)} fusion(f32[1024,128,8]{1,0,2:T(8,128)S(1)} %get-tuple-element.18, f32[8,128]{1,0:T(8,128)S(1)} %get-tuple-element.17, pred[8,1024]{1,0:T(8,128)(4,1)S(1)} %broadcast_bitcast_fusion), kind=kLoop, calls=%fused_computation.19 | loop fusion | flops 4193280 | bytes 4210688 | tf_op jit(solution)/shard_map/reduce_sum | solution.py:65
  38.7 1.4 %fusion.39 = f32[128,8,128]{0,2,1:T(8,128)S(1)} fusion(f32[1024,128,8]{1,0,2:T(8,128)S(1)} %get-tuple-element.22, f32[8,128]{1,0:T(8,128)S(1)} %get-tuple-element.21, pred[8,1024]{1,0:T(8,128)(4,1)S(1)} %broadcast_bitcast_fusion.2, bf16[2,1024,128]{2,1,0:T(8,128)(2,1)S(1)} %multiply_convert_fusion, f32[128,8]{0,1:T(8,128)S(1)} %get-tuple-element.11), kind=kOutput, calls=%fused_computation.32 | convolution fusion | flops 272760832 | bytes 4997120 | tf_op jit(solution)/shard_map/hrk,kd->rhd/dot_general | solution.py:67
  40.2 1.5 %fusion.33 = f32[128,8,128]{0,2,1:T(8,128)S(1)} fusion(f32[1024,128,8]{1,0,2:T(8,128)S(1)} %get-tuple-element.18, f32[8,128]{1,0:T(8,128)S(1)} %get-tuple-element.17, pred[8,1024]{1,0:T(8,128)(4,1)S(1)} %broadcast_bitcast_fusion, bf16[2,1024,128]{2,1,0:T(8,128)(2,1)S(1)} %collective-permute-done.1, f32[128,8]{0,1:T(8,128)S(1)} %get-tuple-element.12), kind=kOutput, calls=%fused_computation.30 | convolution fusion | flops 272760832 | bytes 4997120 | tf_op jit(solution)/shard_map/hrk,kd->rhd/dot_general | solution.py:67
  41.6 1.8 %fusion.54 = bf16[128,8,128]{0,2,1:T(8,128)(2,1)S(1)} fusion(f32[128,8,128]{0,2,1:T(8,128)S(1)} %fusion.33, f32[128,8,128]{0,2,1:T(8,128)S(1)} %fusion.39, f32[1024,128,8]{1,0,2:T(8,128)S(1)} %get-tuple-element.20, f32[8,128]{1,0:T(8,128)S(1)} %get-tuple-element.19, pred[8,1024]{1,0:T(8,128)(4,1)S(1)} %broadcast_bitcast_fusion.1, ...), kind=kOutput, calls=%fused_computation.38 | convolution fusion | flops 273416192 | bytes 5791744 | tf_op jit(solution)/shard_map/hrk,kd->rhd/dot_general | solution.py:67
  43.5 0.2 copy.57
  43.6 0.1 all_to_all.14
  43.8 8.6 %all_to_all.19 = bf16[4,32,1024]{2,1,0:T(8,128)(2,1)S(1)} all-to-all(bf16[4,32,1024]{2,1,0:T(8,128)(2,1)S(1)} %all_to_all.14), channel_id=1, replica_groups=mesh['groups'=2,'ctx'=4,'head'=4] {'head'}, dimensions={0} | all-to-all | bytes 524288 | tf_op jit(solution)/shard_map/all_to_all | solution.py:121
  52.4 0.7 %copy.69 = bf16[4,4,8,1024]{3,2,0,1:T(8,128)(2,1)} copy(bf16[4,4,8,1024]{3,2,1,0:T(8,128)(2,1)S(1)} %bitcast.200) | data formatting | bytes 524288 | tf_op jit(solution)/shard_map/all_to_all | solution.py:121
  (20 shorter events, 0.8 us)
Async XLA Ops:
  0.0 8.8 %copy-start = (s32[8,4,8]{2,1,0:T(4,128)S(1)}, s32[8,4,8]{2,1,0:T(4,128)}, u32[]{:S(2)}) copy-start(s32[8,4,8]{2,1,0:T(4,128)} %param.13) | copy-start | bytes 3076
  3.0 32.0 %collective-permute-start.1 = (bf16[2,1024,128]{2,1,0:T(8,128)(2,1)S(1)}, bf16[2,1024,128]{2,1,0:T(8,128)(2,1)S(1)}, u32[]{:S(2)}, u32[]{:S(2)}) collective-permute-start(bf16[2,1024,128]{2,1,0:T(8,128)(2,1)S(1)} %multiply_convert_fusion), channel_id=1, source_target_pairs={{0,12},{4,0},{8,4},{12,8},{1,13},{5,1},{9,5},{13,9},{2,14},{6,2},{... | collective-permute-start | bytes 1572872 | tf_op jit(solution)/shard_map/ppermute | solution.py:18
  8.1 23.3 %collective-permute-start = (bf16[2,1024,128]{2,1,0:T(8,128)(2,1)S(1)}, bf16[2,1024,128]{2,1,0:T(8,128)(2,1)S(1)}, u32[]{:S(2)}, u32[]{:S(2)}) collective-permute-start(bf16[2,1024,128]{2,1,0:T(8,128)(2,1)S(1)} %multiply_convert_fusion), channel_id=1, source_target_pairs={{0,4},{4,8},{8,12},{12,0},{1,5},{5,9},{9,13},{13,1},{2,6},{6,10},{... | collective-permute-start | bytes 1572872 | tf_op jit(solution)/shard_map/ppermute | solution.py:18
where the time goes:
time: 53.4 us; the launch traced here: 53.1 us
  waiting for transfers between devices  16.6 us (31%)
  other arithmetic  9.48 us (18%)
  blocking collectives  8.6 us (16%)
  matrix products  8.34 us (16%)
  starting transfers between devices  5.1 us (10%)
  local copies, waits for them, and re-layouts  4.81 us (9%)
    ppermute x2, waiting for transfers between devices, shifted(): return lax.ppermute(x, axis, [(i, (i + by) % count) for i in range(count)])  16.6 us
    all_to_all x1, blocking collectives, on_device(): lax.all_to_all(normalized, 'head', split_axis=0, concat_axis=1, tiled=True)  8.6 us
    reduce_sum x3, other arithmetic, block_partial(): local_sum = jnp.sum(weights, axis=(3, 4)).reshape(heads_dev, rows_dev)  7.15 us
    ppermute x2, starting transfers between devices, shifted(): return lax.ppermute(x, axis, [(i, (i + by) % count) for i in range(count)])  5.1 us
    dot_general x3, matrix products, block_partial(): jnp.einsum('hrk,kd->rhd', weights_low, scaled_pair[1], preferred_element_...  4.73 us
    dot_general x3, matrix products, block_partial(): jnp.einsum('rhd,kd->hrk', rotated, scaled_pair[0], preferred_element_type...  3.61 us
    unnamed x5, local copies, waits for them, and re-layouts  1.3 us
  transfers between devices with their start and end apart: 2, of which 1 were waited for; matrix products, arithmetic and copies ran while one was open for 19% of the time, Pallas kernels for 0%

commit v1 on v0

v1 whole, which is shorter than its diff:
```python
import functools
import math

import jax
import jax.numpy as jnp
from jax import lax
from jax.experimental import pallas as pl
from jax.experimental.pallas import tpu as pltpu
from jax.sharding import PartitionSpec as P

GROUP = 16
BLOCK = 128
ROPE_BASE = 500000.0
VMEM_GRANT = 16 * 2**20

in_vmem = pl.BlockSpec(memory_space=pltpu.VMEM)
in_smem = pl.BlockSpec(memory_space=pltpu.SMEM)
in_hbm = pl.BlockSpec(memory_space=pltpu.HBM)
granted = pltpu.CompilerParams(vmem_limit_bytes=VMEM_GRANT)


def shifted(x, axis, by):
    count = lax.axis_size(axis)
    return lax.ppermute(x, axis, [(i, (i + by) % count) for i in range(count)])


def swapped(x, axis, mask):
    count = lax.axis_size(axis)
    return lax.ppermute(x, axis, [(i, i ^ mask) for i in range(count)])


def scale_kernel(
    index_ref, table_ref, codes_ref, full_ref, send_ref, held, arrived, *, row, transposed, share, heads_dev
):
    place = lax.axis_index("head")
    kv_head = place * heads_dev // GROUP
    part = lax.rem(place, share)
    copy = pltpu.make_async_copy(codes_ref.at[kv_head], held, arrived)
    copy.start()
    copy.wait()
    blocks = full_ref.shape[0]
    for block in range(blocks):
        scale = table_ref[row, index_ref[row, kv_head, block]]
        scaled = held[block * BLOCK : (block + 1) * BLOCK, :].astype(jnp.float32) * scale
        if transposed:
            scaled = scaled.T
        full_ref[block] = scaled.astype(jnp.bfloat16)
    per_part = send_ref.shape[0]
    send_ref[...] = full_ref[pl.ds(part * per_part, per_part)]


def scale_blocks(codes, scale_index, scale_table, row, transposed, share, heads_dev):
    _, keys_dev, width = codes.shape
    blocks = keys_dev // BLOCK
    return pl.pallas_call(
        functools.partial(
            scale_kernel, row=row, transposed=transposed, share=share, heads_dev=heads_dev
        ),
        in_specs=[in_smem, in_smem, in_hbm],
        out_specs=[in_vmem, in_vmem],
        out_shape=[
            jax.ShapeDtypeStruct((blocks, BLOCK, width), jnp.bfloat16),
            jax.ShapeDtypeStruct((blocks // share, BLOCK, width), jnp.bfloat16),
        ],
        scratch_shapes=[pltpu.VMEM((keys_dev, width), codes.dtype), pltpu.SemaphoreType.DMA(())],
        compiler_params=granted,
        name="scale_keys" if transposed else "scale_values",
    )(scale_index, scale_table, codes)


def gather_parts(parts, store):
    at = 0
    for part in parts:
        store[at : at + part.shape[0]] = part[...]
        at += part.shape[0]


def score_kernel(slots_ref, queries_ref, cosine_ref, sine_ref, *rest):
    *parts, weights_ref, total_ref, store = rest
    heads, rows, width = queries_ref.shape
    picks = slots_ref.shape[1]
    factor = math.log2(math.e) / math.sqrt(width)
    gather_parts(parts, store)
    cosine = cosine_ref[...]
    sine = sine_ref[...]
    even = lax.rem(lax.broadcasted_iota(jnp.int32, (rows, width), 1), 2) == 0
    for head in range(heads):
        plain = queries_ref[head].astype(jnp.float32)
        other = jnp.where(even, pltpu.roll(plain, width - 1, 1), pltpu.roll(plain, 1, 1))
        turned = (plain * cosine + other * sine).astype(jnp.bfloat16)
        scores = [
            jnp.dot(turned, store[slots_ref[head, i]], preferred_element_type=jnp.float32)
            for i in range(picks)
        ]
        top = scores[0]
        for i in range(1, picks):
            top = jnp.maximum(top, scores[i])
        top = jnp.max(top, axis=1, keepdims=True)
        total = jnp.zeros((rows, BLOCK), jnp.float32)
        for i in range(picks):
            weight = jnp.exp2((scores[i] - top) * factor)
            total = total + weight
            weights_ref[head, :, i * BLOCK : (i + 1) * BLOCK] = weight.astype(jnp.bfloat16)
        total = jnp.sum(total, axis=1, keepdims=True)
        total_ref[head] = jnp.broadcast_to(total, (rows, width))


def block_weights(slots, queries, cosine, sine, parts):
    heads, rows, width = queries.shape
    picks = slots.shape[1]
    blocks = sum(part.shape[0] for part in parts)
    return pl.pallas_call(
        score_kernel,
        in_specs=[in_smem] + [in_vmem] * (3 + len(parts)),
        out_specs=[in_vmem, in_vmem],
        out_shape=[
            jax.ShapeDtypeStruct((heads, rows, picks * BLOCK), jnp.bfloat16),
            jax.ShapeDtypeStruct((heads, rows, width), jnp.float32),
        ],
        scratch_shapes=[pltpu.VMEM((blocks, width, BLOCK), jnp.bfloat16)],
        compiler_params=granted,
        name="block_weights",
    )(slots, queries, cosine, sine, *parts)


def value_kernel(slots_ref, weights_ref, total_ref, *rest, inputs):
    parts = rest[:inputs]
    pieces = rest[inputs:-1]
    store = rest[-1]
    heads = weights_ref.shape[0]
    width = total_ref.shape[2]
    picks = slots_ref.shape[1]
    rows = pieces[0].shape[0]
    gather_parts(parts, store)
    for head in range(heads):
        picked = jnp.concatenate([store[slots_ref[head, i]] for i in range(picks)], axis=0)
        out = jnp.dot(weights_ref[head], picked, preferred_element_type=jnp.float32)
        out = out / total_ref[head]
        for n, piece in enumerate(pieces):
            piece[:, head * width : (head + 1) * width] = out[n * rows : (n + 1) * rows].astype(
                jnp.bfloat16
            )


def block_outputs(slots, weights, total, parts, pieces):
    heads, rows, width = total.shape
    blocks = sum(part.shape[0] for part in parts)
    piece = jax.ShapeDtypeStruct((rows // pieces, heads * width), jnp.bfloat16)
    return pl.pallas_call(
        functools.partial(value_kernel, inputs=len(parts)),
        in_specs=[in_smem] + [in_vmem] * (2 + len(parts)),
        out_specs=[in_vmem] * pieces,
        out_shape=[piece] * pieces,
        scratch_shapes=[pltpu.VMEM((blocks, BLOCK, width), jnp.bfloat16)],
        compiler_params=granted,
        name="block_outputs",
    )(slots, weights, total, *parts)


def join_kernel(*refs):
    *pieces, out_ref = refs
    place = lax.axis_index("head")
    width = pieces[0].shape[1]
    for mask, piece in enumerate(pieces):
        column = pl.multiple_of(jnp.bitwise_xor(place, mask) * width, width)
        out_ref[:, pl.ds(column, width)] = piece[...]


def join_pieces(pieces):
    rows, width = pieces[0].shape
    return pl.pallas_call(
        join_kernel,
        in_specs=[in_vmem] * len(pieces),
        out_specs=in_vmem,
        out_shape=jax.ShapeDtypeStruct((rows, width * len(pieces)), jnp.bfloat16),
        compiler_params=granted,
        name="join_pieces",
    )(*pieces)


def on_device(queries, positions, key_codes, value_codes, scale_index, scale_table, block_lists):
    cycle_size = lax.axis_size("ctx")
    cycle_place = lax.axis_index("ctx")
    head_count = lax.axis_size("head")
    head_place = lax.axis_index("head")
    reach_hops = min(3, (cycle_size - 1) // 2)
    rows_dev, heads_dev, head_width = queries.shape
    key_blocks = key_codes.shape[1] // BLOCK
    share = GROUP // heads_dev

    def spread(codes, row):
        full, own = scale_blocks(
            codes, scale_index, scale_table, row, row == 0, share, heads_dev
        )
        parts = [full]
        ahead = behind = own
        for _ in range(reach_hops):
            ahead = shifted(ahead, "ctx", 1)
            behind = shifted(behind, "ctx", -1)
            for arrived in (ahead, behind):
                parts.append(arrived)
                for mask in range(1, share):
                    parts.append(swapped(arrived, "head", mask))
        return parts

    key_parts = spread(key_codes, 0)
    value_parts = spread(value_codes, 1)

    lists = lax.dynamic_index_in_dim(block_lists, cycle_place, 1, keepdims=False)
    offset = jnp.mod(lists // key_blocks - cycle_place, cycle_size)
    behind = cycle_size - offset
    inner = lists % key_blocks
    per_part = key_blocks // share
    mixed = jnp.bitwise_xor(inner // per_part, head_place % share) * per_part + inner % per_part
    slots = jnp.where(
        offset == 0,
        inner,
        mixed
        + key_blocks * jnp.where(offset <= reach_hops, 2 * offset, 2 * behind - 1),
    )

    frequency = ROPE_BASE ** (
        -2.0 * (jnp.arange(head_width) // 2).astype(jnp.float32) / head_width
    )
    angles = positions.astype(jnp.float32)[:, None] * frequency[None, :]
    signs = jnp.where(jnp.arange(head_width) % 2 == 0, -1.0, 1.0)
    cosine = jnp.cos(angles)
    sine = jnp.sin(angles) * signs[None, :]

    rows_piece = rows_dev // head_count

    def reordered(x):
        shape = x.shape
        cut = x.reshape((head_count, rows_piece) + shape[1:])
        taken = [
            lax.dynamic_index_in_dim(cut, jnp.bitwise_xor(head_place, mask), 0, keepdims=False)
            for mask in range(head_count)
        ]
        return jnp.concatenate(taken, axis=0)

    turned_rows = jnp.transpose(reordered(queries), (1, 0, 2))
    weights, total = block_weights(
        slots, turned_rows, reordered(cosine), reordered(sine), key_parts
    )
    pieces = block_outputs(slots, weights, total, value_parts, head_count)
    moved = [pieces[0]] + [swapped(pieces[mask], "head", mask) for mask in range(1, head_count)]
    return join_pieces(moved)


def solution(mesh):
    placed = (
        P(("groups", "ctx"), "head", None),
        P(("groups", "ctx")),
        P("groups", "ctx", None),
        P("groups", "ctx", None),
        P("groups", None, "ctx"),
        P(),
        P(("groups", "head"), None, None),
    )
    return jax.shard_map(
        on_device,
        mesh=mesh,
        in_specs=placed,
        out_specs=P(("groups", "ctx", "head"), None),
        check_vma=False,
    )
```

time: 53.4 us -> 30.3 us (0.57)
  waiting for transfers between devices: 16.6 us -> 6.85 us
  blocking collectives: 8.6 us -> 0 us
  other arithmetic: 9.48 us -> 1.04 us
  matrix products: 8.34 us -> 0 us
  starting transfers between devices: 5.1 us -> 11.8 us
  Pallas kernels: 0 us -> 5.58 us
    ppermute x2 -> x4, waiting for transfers between devices: 16.6 us -> 2.88 us  [shifted(): return lax.ppermute(x, axis, [(i, (i + by) % count) for i in range(count)])]
    all_to_all x1 -> x0, blocking collectives: 8.6 us -> none  [on_device(): lax.all_to_all(normalized, 'head', split_axis=0, concat_axis=1, tiled=True)]
    dot_general x6 -> x0, matrix products: 8.34 us -> none  [the longest x3 4.73 us: block_partial(): jnp.einsum('hrk,kd->rhd', weights_low, scaled_pair[1], preferred_element_...]
    reduce_sum x4 -> x0, other arithmetic: 7.98 us -> none  [the longest x3 7.15 us: block_partial(): local_sum = jnp.sum(weights, axis=(3, 4)).reshape(heads_dev, rows_dev)]
    pallas_call x0 -> x5, Pallas kernels: none -> 5.58 us  [the longest x1 2.02 us: block_weights(): pl.pallas_call(score_kernel, in_specs=[in_smem] + [in_vmem] * (3 + len(pa...]
    ppermute x0 -> x7, waiting for transfers between devices: none -> 3.97 us  [swapped(): return lax.ppermute(x, axis, [(i, i ^ mask) for i in range(count)])]
    ppermute x2 -> x4, starting transfers between devices: 5.1 us -> 9.04 us  [shifted(): return lax.ppermute(x, axis, [(i, (i + by) % count) for i in range(count)])]
    ppermute x0 -> x7, starting transfers between devices: none -> 2.77 us  [swapped(): return lax.ppermute(x, axis, [(i, i ^ mask) for i in range(count)])]
  transfers between devices with their start and end apart: 2 -> 11, of which waited for: 1 -> 4; matrix products, arithmetic and copies ran while one was open for 19% -> 7% of each run, Pallas kernels for 0% -> 9%
where the time goes in v1:
time: 30.3 us; the launch traced here: 30.1 us
  starting transfers between devices  11.8 us (39%)
  waiting for transfers between devices  6.85 us (23%)
  Pallas kernels  5.58 us (18%)
  local copies, waits for them, and re-layouts  4.6 us (15%)
  other arithmetic  1.04 us (3%)
    ppermute x4, starting transfers between devices, shifted(): return lax.ppermute(x, axis, [(i, (i + by) % count) for i in range(count)])  9.04 us
    ppermute x7, waiting for transfers between devices, swapped(): return lax.ppermute(x, axis, [(i, i ^ mask) for i in range(count)])  3.97 us
    unnamed x10, local copies, waits for them, and re-layouts  3.46 us
    ppermute x4, waiting for transfers between devices, shifted(): return lax.ppermute(x, axis, [(i, (i + by) % count) for i in range(count)])  2.88 us
    ppermute x7, starting transfers between devices, swapped(): return lax.ppermute(x, axis, [(i, i ^ mask) for i in range(count)])  2.77 us
    pallas_call x1, Pallas kernels, block_weights(): pl.pallas_call(score_kernel, in_specs=[in_smem] + [in_vmem] * (3 + len(pa...  2.02 us
    pallas_call x2, Pallas kernels, scale_blocks(): pl.pallas_call(functools.partial(scale_kernel, row=row, transposed=transp...  1.46 us
    pallas_call x1, Pallas kernels, block_outputs(): pl.pallas_call(functools.partial(value_kernel, inputs=len(parts)), in_spe...  1.37 us
  transfers between devices with their start and end apart: 11, of which 4 were waited for; matrix products, arithmetic and copies ran while one was open for 7% of the time, Pallas kernels for 9%

profile of v1, /device:TPU:0, one launch (start us, length us, event | category | flops | bytes accessed | tf_op | source)
XLA Modules:
  0.0 30.1 jit_solution(13917771999586668809)
XLA Ops:
  0.0 1.1 %copy-done.1 = bf16[2,1024,128]{2,1,0:T(8,128)(2,1)S(1)} copy-done((bf16[2,1024,128]{2,1,0:T(8,128)(2,1)S(1)}, bf16[2,1024,128]{2,1,0:T(8,128)(2,1)}, u32[]{:S(2)}) %copy-start.1) | copy-done | bytes 524312
  1.1 0.7 %copy-done.3 = s32[2,2,8]{2,1,0:T(2,128)S(1)} copy-done((s32[2,2,8]{2,1,0:T(2,128)S(1)}, s32[2,2,8]{2,1,0:T(2,128)}, u32[]{:S(2)}) %copy-start.3) | copy-done | bytes 152
  1.7 0.7 %copy-done.4 = f32[2,16]{1,0:T(2,128)S(1)} copy-done((f32[2,16]{1,0:T(2,128)S(1)}, f32[2,16]{1,0:T(2,128)}, u32[]{:S(2)}) %copy-start.4) | copy-done | bytes 152
  2.4 0.8 %scale_keys.1 = (bf16[8,128,128]{2,1,0:T(8,128)(2,1)S(1)}, bf16[4,128,128]{2,1,0:T(8,128)(2,1)S(1)}) custom-call(s32[2,2,8]{2,1,0:T(2,128)S(1)} %copy-done.3, f32[2,16]{1,0:T(2,128)S(1)} %copy-done.4, bf16[2,1024,128]{2,1,0:T(8,128)(2,1)S(1)} %copy-done.1), custom_call_target="tpu_custom_call" | custom-call | tf_op jit(solution)/shard_map/scale_keys/pallas_call | solution.py:55
  3.2 3.1 %collective-permute-start = (bf16[4,128,128]{2,1,0:T(8,128)(2,1)S(1)}, bf16[4,128,128]{2,1,0:T(8,128)(2,1)S(1)}, u32[]{:S(2)}, u32[]{:S(2)}) collective-permute-start(bf16[4,128,128]{2,1,0:T(8,128)(2,1)S(1)} %get-tuple-element.16), channel_id=1, source_target_pairs={{0,4},{4,8},{8,12},{12,0},{1,5},{5,9},{9,13},{13,1},{2,6},{6,10},{... | collective-permute-start | bytes 393224 | tf_op jit(solution)/shard_map/ppermute | solution.py:24
  6.3 2.1 %collective-permute-start.2 = (bf16[4,128,128]{2,1,0:T(8,128)(2,1)S(1)}, bf16[4,128,128]{2,1,0:T(8,128)(2,1)S(1)}, u32[]{:S(2)}, u32[]{:S(2)}) collective-permute-start(bf16[4,128,128]{2,1,0:T(8,128)(2,1)S(1)} %get-tuple-element.16), channel_id=1, source_target_pairs={{0,12},{4,0},{8,4},{12,8},{1,13},{5,1},{9,5},{13,9},{2,14},{6,2},{... | collective-permute-start | bytes 393224 | tf_op jit(solution)/shard_map/ppermute | solution.py:24
  8.4 1.0 %copy-done.2 = bf16[2,1024,128]{2,1,0:T(8,128)(2,1)S(1)} copy-done((bf16[2,1024,128]{2,1,0:T(8,128)(2,1)S(1)}, bf16[2,1024,128]{2,1,0:T(8,128)(2,1)}, u32[]{:S(2)}) %copy-start.2) | copy-done | bytes 524312
  9.4 0.7 %scale_values.1 = (bf16[8,128,128]{2,1,0:T(8,128)(2,1)S(1)}, bf16[4,128,128]{2,1,0:T(8,128)(2,1)S(1)}) custom-call(s32[2,2,8]{2,1,0:T(2,128)S(1)} %copy-done.3, f32[2,16]{1,0:T(2,128)S(1)} %copy-done.4, bf16[2,1024,128]{2,1,0:T(8,128)(2,1)S(1)} %copy-done.2), custom_call_target="tpu_custom_call" | custom-call | tf_op jit(solution)/shard_map/scale_values/pallas_call | solution.py:55
  10.2 3.8 %collective-permute-start.6 = (bf16[4,128,128]{2,1,0:T(8,128)(2,1)S(1)}, bf16[4,128,128]{2,1,0:T(8,128)(2,1)S(1)}, u32[]{:S(2)}, u32[]{:S(2)}) collective-permute-start(bf16[4,128,128]{2,1,0:T(8,128)(2,1)S(1)} %get-tuple-element.20), channel_id=1, source_target_pairs={{0,12},{4,0},{8,4},{12,8},{1,13},{5,1},{9,5},{13,9},{2,14},{6,2},{... | collective-permute-start | bytes 393224 | tf_op jit(solution)/shard_map/ppermute | solution.py:24
  14.0 0.7 %convert_element_type.10 = f32[128]{0:T(128)S(1)} convert(s32[128]{0:T(128)} %param.8) | non-fusion elementwise | flops 128 | bytes 1024 | tf_op jit(solution)/shard_map/convert_element_type | solution.py:225
  14.7 0.1 mul.46
  14.7 0.3 %fusion = (f32[4,32,128]{2,1,0:T(8,128)S(1)}, f32[4,32,128]{2,1,0:T(8,128)S(1)}) fusion(f32[128]{0:T(128)S(1)} %get-tuple-element.39, f32[128]{0:T(128)S(1)} %get-tuple-element.40, f32[4,32]{1,0:T(4,128)S(1)} %mul.46), kind=kLoop, calls=%fused_computation.3 | loop fusion | flops 32768 | bytes 132608 | tf_op jit(solution)/shard_map/mul | solution.py:228
  15.1 1.0 %constant_dynamic-slice_fusion.3 = (bf16[1,32,8,128]{3,2,1,0:T(8,128)(2,1)S(1)}, bf16[1,32,8,128]{3,2,1,0:T(8,128)(2,1)S(1)}, bf16[1,32,8,128]{3,2,1,0:T(8,128)(2,1)S(1)}, bf16[1,32,8,128]{3,2,1,0:T(8,128)(2,1)S(1)}) fusion(bf16[4,32,8,128]{3,2,1,0:T(8,128)(2,1)} %bitcast.30, s32[]{:T(128)S(6)} %select_n.97, s32[]{:T(128)S(6)} %select_n.99, ...), kind=kLoop, calls=%fused_computation.47 | loop fusion | bytes 524304 | tf_op jit(solution)/shard_map/jit(dynamic_index_in_dim)/dynamic_slice | solution.py:236
  16.2 0.1 collective-permute-start.1
  16.3 0.5 %collective-permute-start.3 = (bf16[4,128,128]{2,1,0:T(8,128)(2,1)S(1)}, bf16[4,128,128]{2,1,0:T(8,128)(2,1)S(1)}, u32[]{:S(2)}, u32[]{:S(2)}) collective-permute-start(bf16[4,128,128]{2,1,0:T(8,128)(2,1)S(1)} %collective-permute-done.2.rest_3_), channel_id=1, source_target_pairs={{0,1},{1,0},{2,3},{3,2},{4,5},{5,4},{6,7},{7,6},{8,9},{9,8},{10,11... | collective-permute-start | bytes 393224 | tf_op jit(solution)/shard_map/ppermute | solution.py:29
  16.8 1.6 %collective-permute-done.4.rest_1_ = bf16[4,128,128]{2,1,0:T(8,128)(2,1)S(1)} collective-permute-done((bf16[4,128,128]{2,1,0:T(8,128)(2,1)S(1)}, bf16[4,128,128]{2,1,0:T(8,128)(2,1)S(1)}, u32[]{:S(2)}, u32[]{:S(2)}) %collective-permute-start.4) | collective-permute-done | bytes 131104 | tf_op jit(solution)/shard_map/ppermute | solution.py:24
  18.4 1.3 %collective-permute-done.6.rest_3_ = bf16[4,128,128]{2,1,0:T(8,128)(2,1)S(1)} collective-permute-done((bf16[4,128,128]{2,1,0:T(8,128)(2,1)S(1)}, bf16[4,128,128]{2,1,0:T(8,128)(2,1)S(1)}, u32[]{:S(2)}, u32[]{:S(2)}) %collective-permute-start.6) | collective-permute-done | bytes 131104 | tf_op jit(solution)/shard_map/ppermute | solution.py:24
  19.7 2.0 %block_weights.1 = (bf16[8,128,1024]{2,1,0:T(8,128)(2,1)S(1)}, f32[8,128,128]{2,1,0:T(8,128)S(1)}) custom-call(s32[8,8]{1,0:T(8,128)S(1)} %fusion.7.slots_ref, bf16[8,128,128]{2,1,0:T(8,128)(2,1)S(1)} %maximum_bitcast_fusion.queries_ref, f32[128,128]{1,0:T(8,128)S(1)} %pad_maximum_fusion.cosine_ref, f32[128,128]{1,0:T(8,128)S(1)} %pad_maximum_fusion.1.sine_ref, ...), custom_call_target="tpu_custom_call" | custom-call | tf_op jit(solution)/shard_map/block_weights/pallas_call | solution.py:112
  21.8 1.4 %block_outputs.1 = (bf16[32,1024]{1,0:T(8,128)(2,1)S(1)}, bf16[32,1024]{1,0:T(8,128)(2,1)S(1)}, bf16[32,1024]{1,0:T(8,128)(2,1)S(1)}, bf16[32,1024]{1,0:T(8,128)(2,1)S(1)}) custom-call(s32[8,8]{1,0:T(8,128)S(1)} %fusion.7.slots_ref, bf16[8,128,1024]{2,1,0:T(8,128)(2,1)S(1)} %get-tuple-element.17.weights_ref, f32[8,128,128]{2,1,0:T(8,128)S(1)} %get-tuple-element.18.total_ref, ...), custom_call_target="tpu_custom_call" | custom-call | tf_op jit(solution)/shard_map/block_outputs/pallas_call | solution.py:149
  23.2 1.7 %collective-permute-start.10 = (bf16[32,1024]{1,0:T(8,128)(2,1)S(1)}, bf16[32,1024]{1,0:T(8,128)(2,1)S(1)}, u32[]{:S(2)}, u32[]{:S(2)}) collective-permute-start(bf16[32,1024]{1,0:T(8,128)(2,1)S(1)} %get-tuple-element.24), channel_id=1, source_target_pairs={{0,3},{1,2},{2,1},{3,0},{4,7},{5,6},{6,5},{7,4},{8,11},{9,10},{10,... | collective-permute-start | bytes 196616 | tf_op jit(solution)/shard_map/ppermute | solution.py:29
  24.8 0.5 %collective-permute-start.9 = (bf16[32,1024]{1,0:T(8,128)(2,1)S(1)}, bf16[32,1024]{1,0:T(8,128)(2,1)S(1)}, u32[]{:S(2)}, u32[]{:S(2)}) collective-permute-start(bf16[32,1024]{1,0:T(8,128)(2,1)S(1)} %get-tuple-element.23), channel_id=1, source_target_pairs={{0,2},{1,3},{2,0},{3,1},{4,6},{5,7},{6,4},{7,5},{8,10},{9,11},{10,... | collective-permute-start | bytes 196616 | tf_op jit(solution)/shard_map/ppermute | solution.py:29
  25.4 1.9 %collective-permute-done.10.refs_3_ = bf16[32,1024]{1,0:T(8,128)(2,1)S(1)} collective-permute-done((bf16[32,1024]{1,0:T(8,128)(2,1)S(1)}, bf16[32,1024]{1,0:T(8,128)(2,1)S(1)}, u32[]{:S(2)}, u32[]{:S(2)}) %collective-permute-start.10) | collective-permute-done | bytes 65568 | tf_op jit(solution)/shard_map/ppermute | solution.py:29
  27.3 2.1 %collective-permute-done.9.refs_2_ = bf16[32,1024]{1,0:T(8,128)(2,1)S(1)} collective-permute-done((bf16[32,1024]{1,0:T(8,128)(2,1)S(1)}, bf16[32,1024]{1,0:T(8,128)(2,1)S(1)}, u32[]{:S(2)}, u32[]{:S(2)}) %collective-permute-start.9) | collective-permute-done | bytes 65568 | tf_op jit(solution)/shard_map/ppermute | solution.py:29
  29.3 0.7 %join_pieces.1 = bf16[32,4096]{1,0:T(8,128)(2,1)} custom-call(bf16[32,1024]{1,0:T(8,128)(2,1)S(1)} %get-tuple-element.21.refs_0_, bf16[32,1024]{1,0:T(8,128)(2,1)S(1)} %collective-permute-done.8.refs_1_, bf16[32,1024]{1,0:T(8,128)(2,1)S(1)} %collective-permute-done.9.refs_2_, bf16[32,1024]{1,0:T(8,128)(2,1)S(1)} %collective-permute-done.10.refs_3_), custom_call_target="tpu_custom_call" | custom-call | tf_op jit(solution)/shard_map/join_pieces/pallas_call | solution.py:171
  (27 shorter events, 0.3 us)
Async XLA Ops:
  0.0 16.1 %copy-start = (s32[8,4,8]{2,1,0:T(4,128)S(1)}, s32[8,4,8]{2,1,0:T(4,128)}, u32[]{:S(2)}) copy-start(s32[8,4,8]{2,1,0:T(4,128)} %param.13) | copy-start | bytes 3076
  0.0 1.1 %copy-start.1 = (bf16[2,1024,128]{2,1,0:T(8,128)(2,1)S(1)}, bf16[2,1024,128]{2,1,0:T(8,128)(2,1)}, u32[]{:S(2)}) copy-start(bf16[2,1024,128]{2,1,0:T(8,128)(2,1)} %codes_ref.2) | copy-start | bytes 1572868
  1.1 0.7 %copy-start.3 = (s32[2,2,8]{2,1,0:T(2,128)S(1)}, s32[2,2,8]{2,1,0:T(2,128)}, u32[]{:S(2)}) copy-start(s32[2,2,8]{2,1,0:T(2,128)} %index_ref.3) | copy-start | bytes 388
  1.7 0.7 %copy-start.4 = (f32[2,16]{1,0:T(2,128)S(1)}, f32[2,16]{1,0:T(2,128)}, u32[]{:S(2)}) copy-start(f32[2,16]{1,0:T(2,128)} %table_ref.3) | copy-start | bytes 388
  3.2 13.0 %collective-permute-start = (bf16[4,128,128]{2,1,0:T(8,128)(2,1)S(1)}, bf16[4,128,128]{2,1,0:T(8,128)(2,1)S(1)}, u32[]{:S(2)}, u32[]{:S(2)}) collective-permute-start(bf16[4,128,128]{2,1,0:T(8,128)(2,1)S(1)} %get-tuple-element.16), channel_id=1, source_target_pairs={{0,4},{4,8},{8,12},{12,0},{1,5},{5,9},{9,13},{13,1},{2,6},{6,10},{... | collective-permute-start | bytes 393224 | tf_op jit(solution)/shard_map/ppermute | solution.py:24
  6.3 10.0 %collective-permute-start.2 = (bf16[4,128,128]{2,1,0:T(8,128)(2,1)S(1)}, bf16[4,128,128]{2,1,0:T(8,128)(2,1)S(1)}, u32[]{:S(2)}, u32[]{:S(2)}) collective-permute-start(bf16[4,128,128]{2,1,0:T(8,128)(2,1)S(1)} %get-tuple-element.16), channel_id=1, source_target_pairs={{0,12},{4,0},{8,4},{12,8},{1,13},{5,1},{9,5},{13,9},{2,14},{6,2},{... | collective-permute-start | bytes 393224 | tf_op jit(solution)/shard_map/ppermute | solution.py:24
  8.4 1.0 %copy-start.2 = (bf16[2,1024,128]{2,1,0:T(8,128)(2,1)S(1)}, bf16[2,1024,128]{2,1,0:T(8,128)(2,1)}, u32[]{:S(2)}) copy-start(bf16[2,1024,128]{2,1,0:T(8,128)(2,1)} %codes_ref.3) | copy-start | bytes 1572868
  10.1 8.3 %collective-permute-start.4 = (bf16[4,128,128]{2,1,0:T(8,128)(2,1)S(1)}, bf16[4,128,128]{2,1,0:T(8,128)(2,1)S(1)}, u32[]{:S(2)}, u32[]{:S(2)}) collective-permute-start(bf16[4,128,128]{2,1,0:T(8,128)(2,1)S(1)} %get-tuple-element.20), channel_id=1, source_target_pairs={{0,4},{4,8},{8,12},{12,0},{1,5},{5,9},{9,13},{13,1},{2,6},{6,10},{... | collective-permute-start | bytes 393224 | tf_op jit(solution)/shard_map/ppermute | solution.py:24
  10.2 9.5 %collective-permute-start.6 = (bf16[4,128,128]{2,1,0:T(8,128)(2,1)S(1)}, bf16[4,128,128]{2,1,0:T(8,128)(2,1)S(1)}, u32[]{:S(2)}, u32[]{:S(2)}) collective-permute-start(bf16[4,128,128]{2,1,0:T(8,128)(2,1)S(1)} %get-tuple-element.20), channel_id=1, source_target_pairs={{0,12},{4,0},{8,4},{12,8},{1,13},{5,1},{9,5},{13,9},{2,14},{6,2},{... | collective-permute-start | bytes 393224 | tf_op jit(solution)/shard_map/ppermute | solution.py:24
  16.2 3.5 %collective-permute-start.1 = (bf16[4,128,128]{2,1,0:T(8,128)(2,1)S(1)}, bf16[4,128,128]{2,1,0:T(8,128)(2,1)S(1)}, u32[]{:S(2)}, u32[]{:S(2)}) collective-permute-start(bf16[4,128,128]{2,1,0:T(8,128)(2,1)S(1)} %collective-permute-done.rest_1_), channel_id=1, source_target_pairs={{0,1},{1,0},{2,3},{3,2},{4,5},{5,4},{6,7},{7,6},{8,9},{9,8},{10,11... | collective-permute-start | bytes 393224 | tf_op jit(solution)/shard_map/ppermute | solution.py:29
  16.3 3.4 %collective-permute-start.3 = (bf16[4,128,128]{2,1,0:T(8,128)(2,1)S(1)}, bf16[4,128,128]{2,1,0:T(8,128)(2,1)S(1)}, u32[]{:S(2)}, u32[]{:S(2)}) collective-permute-start(bf16[4,128,128]{2,1,0:T(8,128)(2,1)S(1)} %collective-permute-done.2.rest_3_), channel_id=1, source_target_pairs={{0,1},{1,0},{2,3},{3,2},{4,5},{5,4},{6,7},{7,6},{8,9},{9,8},{10,11... | collective-permute-start | bytes 393224 | tf_op jit(solution)/shard_map/ppermute | solution.py:29
  18.4 3.3 %collective-permute-start.5 = (bf16[4,128,128]{2,1,0:T(8,128)(2,1)S(1)}, bf16[4,128,128]{2,1,0:T(8,128)(2,1)S(1)}, u32[]{:S(2)}, u32[]{:S(2)}) collective-permute-start(bf16[4,128,128]{2,1,0:T(8,128)(2,1)S(1)} %collective-permute-done.4.rest_1_), channel_id=1, source_target_pairs={{0,1},{1,0},{2,3},{3,2},{4,5},{5,4},{6,7},{7,6},{8,9},{9,8},{10,11... | collective-permute-start | bytes 393224 | tf_op jit(solution)/shard_map/ppermute | solution.py:29
  19.7 2.1 %collective-permute-start.7 = (bf16[4,128,128]{2,1,0:T(8,128)(2,1)S(1)}, bf16[4,128,128]{2,1,0:T(8,128)(2,1)S(1)}, u32[]{:S(2)}, u32[]{:S(2)}) collective-permute-start(bf16[4,128,128]{2,1,0:T(8,128)(2,1)S(1)} %collective-permute-done.6.rest_3_), channel_id=1, source_target_pairs={{0,1},{1,0},{2,3},{3,2},{4,5},{5,4},{6,7},{7,6},{8,9},{9,8},{10,11... | collective-permute-start | bytes 393224 | tf_op jit(solution)/shard_map/ppermute | solution.py:29
  23.2 4.1 %collective-permute-start.10 = (bf16[32,1024]{1,0:T(8,128)(2,1)S(1)}, bf16[32,1024]{1,0:T(8,128)(2,1)S(1)}, u32[]{:S(2)}, u32[]{:S(2)}) collective-permute-start(bf16[32,1024]{1,0:T(8,128)(2,1)S(1)} %get-tuple-element.24), channel_id=1, source_target_pairs={{0,3},{1,2},{2,1},{3,0},{4,7},{5,6},{6,5},{7,4},{8,11},{9,10},{10,... | collective-permute-start | bytes 196616 | tf_op jit(solution)/shard_map/ppermute | solution.py:29
  24.8 2.4 %collective-permute-start.8 = (bf16[32,1024]{1,0:T(8,128)(2,1)S(1)}, bf16[32,1024]{1,0:T(8,128)(2,1)S(1)}, u32[]{:S(2)}, u32[]{:S(2)}) collective-permute-start(bf16[32,1024]{1,0:T(8,128)(2,1)S(1)} %get-tuple-element.22), channel_id=1, source_target_pairs={{0,1},{1,0},{2,3},{3,2},{4,5},{5,4},{6,7},{7,6},{8,9},{9,8},{10,11... | collective-permute-start | bytes 196616 | tf_op jit(solution)/shard_map/ppermute | solution.py:29
  24.8 4.5 %collective-permute-start.9 = (bf16[32,1024]{1,0:T(8,128)(2,1)S(1)}, bf16[32,1024]{1,0:T(8,128)(2,1)S(1)}, u32[]{:S(2)}, u32[]{:S(2)}) collective-permute-start(bf16[32,1024]{1,0:T(8,128)(2,1)S(1)} %get-tuple-element.23), channel_id=1, source_target_pairs={{0,2},{1,3},{2,0},{3,1},{4,6},{5,7},{6,4},{7,5},{8,10},{9,11},{10,... | collective-permute-start | bytes 196616 | tf_op jit(solution)/shard_map/ppermute | solution.py:29

commit v2 on v1

v2 whole, which is shorter than its diff:
```python
import functools
import math

import jax
import jax.numpy as jnp
from jax import lax
from jax.experimental import pallas as pl
from jax.experimental.pallas import tpu as pltpu
from jax.sharding import PartitionSpec as P

GROUP = 16
BLOCK = 128
ROPE_BASE = 500000.0
VMEM_GRANT = 16 * 2**20

in_vmem = pl.BlockSpec(memory_space=pltpu.VMEM)
granted = pltpu.CompilerParams(vmem_limit_bytes=VMEM_GRANT)


def sent(x, hop, share):
    cycle = lax.axis_size("ctx")
    heads = lax.axis_size("head")
    pairs = []
    for place in range(cycle):
        for head in range(heads):
            by = hop if head % share == 0 else -hop
            pairs.append((place * heads + head, (place + by) % cycle * heads + head))
    return lax.ppermute(x, ("ctx", "head"), pairs)


def swapped(x, mask):
    return lax.ppermute(x, "head", [(i, i ^ mask) for i in range(lax.axis_size("head"))])


def scale_kernel(scales_ref, codes_ref, _, out_ref, *, row):
    scales = scales_ref[...]
    for block in range(out_ref.shape[0]):
        codes = codes_ref[block * BLOCK : (block + 1) * BLOCK, :].astype(jnp.float32)
        out_ref[block] = (codes * scales[row, block]).astype(jnp.bfloat16)


def scale_blocks(scales, codes, before, row):
    keys_dev, width = codes.shape
    return pl.pallas_call(
        functools.partial(scale_kernel, row=row),
        in_specs=[in_vmem, in_vmem, pl.BlockSpec(memory_space=pl.ANY)],
        out_specs=in_vmem,
        out_shape=jax.ShapeDtypeStruct((keys_dev // BLOCK, BLOCK, width), jnp.bfloat16),
        compiler_params=granted,
        name="scale_values",
    )(scales, codes, before)


def scaled_keys(codes_ref, scales, blocks, store, at):
    for block in range(blocks):
        codes = codes_ref[block * BLOCK : (block + 1) * BLOCK, :].astype(jnp.float32)
        store[at + block] = (codes * scales[0, block]).T.astype(jnp.bfloat16)


def turn_kernel(queries_ref, cosine_ref, sine_ref, codes_ref, scales_ref, *outs):
    own_ref, sibling_ref, keys_ref = outs
    heads_dev, rows, width = own_ref.shape
    cosine = cosine_ref[...]
    sine = sine_ref[...]
    even = lax.rem(lax.broadcasted_iota(jnp.int32, cosine.shape, 1), 2) == 0
    for head in range(heads_dev):
        plain = queries_ref[head].astype(jnp.float32)
        other = jnp.where(even, pltpu.roll(plain, width - 1, 1), pltpu.roll(plain, 1, 1))
        turned = (plain * cosine + other * sine).astype(jnp.bfloat16)
        own_ref[head] = turned[:rows]
        sibling_ref[head] = turned[rows:]
    scaled_keys(codes_ref, scales_ref[...], keys_ref.shape[0], keys_ref, 0)


def turn_queries(queries, cosine, sine, codes, scales):
    heads_dev, rows, width = queries.shape
    half = jax.ShapeDtypeStruct((heads_dev, rows // 2, width), jnp.bfloat16)
    return pl.pallas_call(
        turn_kernel,
        in_specs=[in_vmem] * 5,
        out_specs=[in_vmem] * 3,
        out_shape=[
            half,
            half,
            jax.ShapeDtypeStruct((codes.shape[0] // BLOCK, width, BLOCK), jnp.bfloat16),
        ],
        compiler_params=granted,
        name="turn_queries",
    )(queries, cosine, sine, codes, scales)


def score_kernel(slots_ref, own_ref, sibling_ref, near_ref, table_ref, *rest):
    *parts, weights_ref, total_ref, store = rest
    heads_dev, rows, width = own_ref.shape
    heads = slots_ref.shape[0]
    picks = slots_ref.shape[1]
    slots = slots_ref[...]
    factor = math.log2(math.e) / math.sqrt(width)
    blocks = near_ref.shape[0]
    store[:blocks] = near_ref[...]
    table = table_ref[...]
    entries = lax.broadcasted_iota(jnp.int32, (table.shape[0], width), 0).astype(jnp.float32)
    for n, part in enumerate(parts):
        index = part[blocks * BLOCK :, :].astype(jnp.float32)
        scales = jnp.sum(jnp.where(index == entries, table, 0.0), axis=0, keepdims=True)
        scaled_keys(part, scales, blocks, store, (n + 1) * blocks)
    for head in range(heads):
        turned = (own_ref if head < heads_dev else sibling_ref)[head % heads_dev]
        scores = [
            jnp.dot(turned, store[slots[head, i]], preferred_element_type=jnp.float32)
            for i in range(picks)
        ]
        top = scores[0]
        for i in range(1, picks):
            top = jnp.maximum(top, scores[i])
        top = jnp.max(top, axis=1, keepdims=True)
        total = jnp.zeros((rows, BLOCK), jnp.float32)
        for i in range(picks):
            weight = jnp.exp2((scores[i] - top) * factor)
            total = total + weight
            weights_ref[head, :, i * BLOCK : (i + 1) * BLOCK] = weight.astype(jnp.bfloat16)
        total = jnp.sum(total, axis=1, keepdims=True)
        total_ref[head] = jnp.broadcast_to(total, (rows, width))


def block_weights(slots, own, sibling, near, table, parts):
    _, rows, width = own.shape
    heads, picks = slots.shape
    blocks = near.shape[0] * (1 + len(parts))
    return pl.pallas_call(
        score_kernel,
        in_specs=[in_vmem] * (5 + len(parts)),
        out_specs=[in_vmem, in_vmem],
        out_shape=[
            jax.ShapeDtypeStruct((heads, rows, picks * BLOCK), jnp.bfloat16),
            jax.ShapeDtypeStruct((heads, rows, width), jnp.float32),
        ],
        scratch_shapes=[pltpu.VMEM((blocks, width, BLOCK), jnp.bfloat16)],
        compiler_params=granted,
        name="block_weights",
    )(slots, own, sibling, near, table, *parts)


def value_kernel(slots_ref, weights_ref, total_ref, *rest, inputs):
    parts = rest[:inputs]
    pieces = rest[inputs:-1]
    store = rest[-1]
    heads, _, width = total_ref.shape
    picks = slots_ref.shape[1]
    rows = pieces[0].shape[0]
    slots = slots_ref[...]
    at = 0
    for part in parts:
        store[at : at + part.shape[0]] = part[...]
        at += part.shape[0]
    for head in range(heads):
        picked = jnp.concatenate([store[slots[head, i]] for i in range(picks)], axis=0)
        out = jnp.dot(weights_ref[head], picked, preferred_element_type=jnp.float32)
        out = out / total_ref[head]
        for n, piece in enumerate(pieces):
            piece[:, head * width : (head + 1) * width] = out[n * rows : (n + 1) * rows].astype(
                jnp.bfloat16
            )


def block_outputs(slots, weights, total, parts, pieces):
    heads, rows, width = total.shape
    blocks = sum(part.shape[0] for part in parts)
    piece = jax.ShapeDtypeStruct((rows // pieces, heads * width), jnp.bfloat16)
    return pl.pallas_call(
        functools.partial(value_kernel, inputs=len(parts)),
        in_specs=[in_vmem] * (3 + len(parts)),
        out_specs=[in_vmem] * pieces,
        out_shape=[piece] * pieces,
        scratch_shapes=[pltpu.VMEM((blocks, BLOCK, width), jnp.bfloat16)],
        compiler_params=granted,
        name="block_outputs",
    )(slots, weights, total, *parts)


def join_kernel(*refs, share):
    *pieces, out_ref = refs
    place = lax.axis_index("head")
    width = pieces[0].shape[1] // share
    for n, piece in enumerate(pieces):
        for part in range(share):
            column = pl.multiple_of(jnp.bitwise_xor(place, n * share + part) * width, width)
            out_ref[:, pl.ds(column, width)] = piece[:, part * width : (part + 1) * width]


def join_pieces(pieces, share):
    rows, width = pieces[0].shape
    return pl.pallas_call(
        functools.partial(join_kernel, share=share),
        in_specs=[in_vmem] * len(pieces),
        out_specs=in_vmem,
        out_shape=jax.ShapeDtypeStruct((rows, width * len(pieces)), jnp.bfloat16),
        compiler_params=granted,
        name="join_pieces",
    )(*pieces)


def on_device(queries, positions, key_codes, value_codes, scale_index, scale_table, block_lists):
    cycle_size = lax.axis_size("ctx")
    cycle_place = lax.axis_index("ctx")
    head_count = lax.axis_size("head")
    head_place = lax.axis_index("head")
    reach_hops = min(3, (cycle_size - 1) // 2)
    rows_dev, heads_dev, head_width = queries.shape
    key_blocks = key_codes.shape[1] // BLOCK
    share = GROUP // heads_dev
    assert share == 2 and rows_dev == BLOCK
    core = head_place % share
    group = head_place // share
    groups = head_count // share
    kv_head = head_place * heads_dev // GROUP

    key_rows = lax.dynamic_index_in_dim(key_codes, kv_head, 0, keepdims=False)
    (
        key_rows,
        queries,
        positions,
        value_codes,
        scale_index,
        scale_table,
        block_lists,
    ) = lax.optimization_barrier(
        (key_rows, queries, positions, value_codes, scale_index, scale_table, block_lists)
    )
    value_rows = lax.dynamic_index_in_dim(value_codes, kv_head, 0, keepdims=False)
    index_rows = lax.dynamic_index_in_dim(scale_index, kv_head, 1, keepdims=False)
    matches = index_rows[:, :, None] == jnp.arange(scale_table.shape[1], dtype=jnp.int32)
    scales = jnp.sum(jnp.where(matches, scale_table[:, None, :], 0.0), axis=2)

    entries = scale_table.shape[1]
    labels = jnp.pad(
        jnp.broadcast_to(index_rows[0].astype(jnp.bfloat16), (entries, key_blocks)),
        ((0, 0), (0, head_width - key_blocks)),
    )
    far_keys = jnp.concatenate([key_rows, labels], axis=0)
    key_parts = []
    for _ in range(reach_hops):
        far_keys = sent(far_keys, 1, share)
        key_parts += [far_keys, swapped(far_keys, 1)]

    own_lists = lax.dynamic_index_in_dim(block_lists, cycle_place, 1, keepdims=False)
    lists = jnp.concatenate([own_lists, swapped(own_lists, 1)], axis=0)
    offset = jnp.mod(lists // key_blocks - cycle_place, cycle_size)
    above = offset <= reach_hops
    hops = jnp.where(above, offset, cycle_size - offset)
    place = 2 * hops - jnp.where(above == (core == 1), 1, 0)
    slots = lists % key_blocks + key_blocks * jnp.where(offset == 0, 0, place)

    def ordered(x):
        cut = x.reshape((groups, share, rows_dev // head_count) + x.shape[1:])
        taken = [
            lax.dynamic_slice(
                cut,
                (jnp.bitwise_xor(group, n), jnp.bitwise_xor(core, part)) + (0,) * x.ndim,
                (1, 1) + cut.shape[2:],
            )
            for part in range(share)
            for n in range(groups)
        ]
        return jnp.concatenate(taken, axis=0).reshape(x.shape)

    frequency = ROPE_BASE ** (
        -2.0 * (jnp.arange(head_width) // 2).astype(jnp.float32) / head_width
    )
    angles = ordered(positions).astype(jnp.float32)[:, None] * frequency[None, :]
    signs = jnp.where(jnp.arange(head_width) % 2 == 0, -1.0, 1.0)
    cosine = jnp.cos(angles)
    sine = jnp.sin(angles) * signs[None, :]

    own, sibling, near = turn_queries(
        jnp.transpose(ordered(queries), (1, 0, 2)), cosine, sine, key_rows, scales
    )
    values = scale_blocks(scales, value_rows, own, 1)
    value_steps = []
    far_values = values
    for _ in range(reach_hops):
        far_values = sent(far_values, 1, share)
        value_steps.append(far_values)
    weights, total = block_weights(
        slots, own, swapped(sibling, 1), near, scale_table[0][:, None], key_parts
    )

    *value_steps, weights = lax.optimization_barrier((*value_steps, weights))
    value_parts = [values]
    for step in value_steps:
        value_parts += [step, swapped(step, 1)]
    pieces = block_outputs(slots, weights, total, value_parts, groups)
    moved = [pieces[0]] + [swapped(pieces[n], n * share) for n in range(1, groups)]
    return join_pieces(moved, share)


def solution(mesh):
    placed = (
        P(("groups", "ctx"), "head", None),
        P(("groups", "ctx")),
        P("groups", "ctx", None),
        P("groups", "ctx", None),
        P("groups", None, "ctx"),
        P(),
        P(("groups", "head"), None, None),
    )
    return jax.shard_map(
        on_device,
        mesh=mesh,
        in_specs=placed,
        out_specs=P(("groups", "ctx", "head"), None),
        check_vma=False,
    )
```

time: 30.3 us -> 28.7 us (0.947)
  waiting for transfers between devices: 6.85 us -> 12 us
  starting transfers between devices: 11.8 us -> 6.84 us
  Pallas kernels: 5.58 us -> 4.45 us
  local copies, waits for them, and re-layouts: 4.6 us -> 3.72 us
    ppermute x11 -> x7, waiting for transfers between devices: 6.85 us -> 12 us  [the longest x5 6.99 us: swapped(): lax.ppermute(x, 'head', [(i, i ^ mask) for i in range(lax.axis_size('head...]
    ppermute x11 -> x7, starting transfers between devices: 11.8 us -> 6.84 us  [the longest x2 3.52 us: sent(): return lax.ppermute(x, ('ctx', 'head'), pairs)]
    unnamed x10 -> x12, local copies, waits for them, and re-layouts: 3.46 us -> 1.1 us
    reshape x0 -> x1, local copies, waits for them, and re-layouts: none -> 0.74 us  [ordered(): cut = x.reshape((groups, share, rows_dev // head_count) + x.shape[1:])]
    pallas_call x4, Pallas kernels: 4.21 us -> 3.49 us  [the longest x1 2.17 us: block_weights(): pl.pallas_call(score_kernel, in_specs=[in_vmem] * (5 + len(parts)), out_s...]
    dynamic_slice x2 -> x3, local copies, waits for them, and re-layouts: 0.98 us -> 1.65 us  [the longest x2 0.96 us: ordered(): lax.dynamic_slice(cut, (jnp.bitwise_xor(group, n), jnp.bitwise_xor(core,...]
    pallas_call x1, Pallas kernels: 1.37 us -> 0.96 us  [block_outputs(): pl.pallas_call(functools.partial(value_kernel, inputs=len(parts)), in_spe...]
    convert_element_type x1 -> x2, other arithmetic: 0.66 us -> 0.71 us  [the longest x1 0.69 us: on_device(): index_rows[0].astype(jnp.bfloat16)]
  transfers between devices with their start and end apart: 11 -> 7, of which waited for: 4 -> 5; matrix products, arithmetic and copies ran while one was open for 7% -> 11% of each run, Pallas kernels for 9% -> 10%
where the time goes in v2:
time: 28.7 us; the launch traced here: 28.5 us
  waiting for transfers between devices  12 us (42%)
  starting transfers between devices  6.84 us (24%)
  Pallas kernels  4.45 us (16%)
  local copies, waits for them, and re-layouts  3.72 us (13%)
  other arithmetic  1.27 us (4%)
    ppermute x5, waiting for transfers between devices, swapped(): lax.ppermute(x, 'head', [(i, i ^ mask) for i in range(lax.axis_size('head...  6.99 us
    ppermute x2, waiting for transfers between devices, sent(): return lax.ppermute(x, ('ctx', 'head'), pairs)  5.06 us
    ppermute x2, starting transfers between devices, sent(): return lax.ppermute(x, ('ctx', 'head'), pairs)  3.52 us
    ppermute x5, starting transfers between devices, swapped(): lax.ppermute(x, 'head', [(i, i ^ mask) for i in range(lax.axis_size('head...  3.32 us
    pallas_call x1, Pallas kernels, block_weights(): pl.pallas_call(score_kernel, in_specs=[in_vmem] * (5 + len(parts)), out_s...  2.17 us
    unnamed x12, local copies, waits for them, and re-layouts  1.1 us
    dynamic_slice x2, local copies, waits for them, and re-layouts, ordered(): lax.dynamic_slice(cut, (jnp.bitwise_xor(group, n), jnp.bitwise_xor(core,...  0.96 us
    pallas_call x1, Pallas kernels, block_outputs(): pl.pallas_call(functools.partial(value_kernel, inputs=len(parts)), in_spe...  0.96 us
  transfers between devices with their start and end apart: 7, of which 5 were waited for; matrix products, arithmetic and copies ran while one was open for 11% of the time, Pallas kernels for 10%

profile of v2, /device:TPU:0, one launch (start us, length us, event | category | flops | bytes accessed | tf_op | source)
XLA Modules:
  0.0 28.5 jit_solution(366754497844786106)
XLA Ops:
  0.0 1.0 %copy-done = bf16[2,1024,128]{2,1,0:T(8,128)(2,1)S(1)} copy-done((bf16[2,1024,128]{2,1,0:T(8,128)(2,1)S(1)}, bf16[2,1024,128]{2,1,0:T(8,128)(2,1)}, u32[]{:S(2)}) %copy-start) | copy-done | bytes 524312
  1.1 0.7 %fusion.15 = bf16[8]{0:T(256)(128)(2,1)S(1)} fusion(s32[2,2,8]{2,1,0:T(2,128)} %param.11, s32[]{:T(128)S(6)} %select_n.107), kind=kLoop, calls=%fused_computation.53 | loop fusion | flops 8 | bytes 52 | tf_op jit(solution)/shard_map/convert_element_type | solution.py:237
  1.8 3.1 %collective-permute-start.3 = (bf16[1040,128]{1,0:T(8,128)(2,1)S(1)}, bf16[1040,128]{1,0:T(8,128)(2,1)S(1)}, u32[]{:S(2)}, u32[]{:S(2)}) collective-permute-start(bf16[1040,128]{1,0:T(8,128)(2,1)S(1)} %pad_maximum_fusion), channel_id=1, source_target_pairs={{0,4},{1,13},{2,6},{3,15},{4,8},{5,1},{6,10},{7,3},{8,12},{9,5},{1... | collective-permute-start | bytes 798728 | tf_op jit(solution)/shard_map/ppermute | solution.py:28
  4.9 0.7 %constant_dynamic-slice_fusion.9 = s32[2,1,8]{2,1,0:T(1,128)S(1)} fusion(s32[2,2,8]{2,1,0:T(2,128)} %param.11, s32[]{:T(128)S(6)} %select_n.107), kind=kLoop, calls=%fused_computation.40 | loop fusion | bytes 132 | tf_op jit(solution)/shard_map/jit(dynamic_index_in_dim)/dynamic_slice | solution.py:231
  5.6 0.7 %reshape.51 = s32[2,2,32]{2,1,0:T(2,128)S(1)} reshape(s32[128]{0:T(128)} %param.8) | data formatting | bytes 1024 | tf_op jit(solution)/shard_map/reshape | solution.py:255
  6.4 0.1 convert_element_type.24
  6.5 1.0 %constant_dynamic-slice_fusion.8 = (bf16[1,1,32,8,128]{4,3,2,1,0:T(8,128)(2,1)S(1)}, bf16[1,1,32,8,128]{4,3,2,1,0:T(8,128)(2,1)S(1)}, bf16[1,1,32,8,128]{4,3,2,1,0:T(8,128)(2,1)S(1)}, bf16[1,1,32,8,128]{4,3,2,1,0:T(8,128)(2,1)S(1)}) fusion(bf16[2,2,32,8,128]{4,3,2,1,0:T(8,128)(2,1)} %bitcast.16, s32[]{:T(128)S(6)} %select_n.118, s32[]{:T(128)S(6)} %select_n.119, ...), kind=kLoop, calls=%fused_computation.39 | loop fusion | bytes 524304 | tf_op jit(solution)/shard_map/dynamic_slice | solution.py:257
  7.5 0.3 %fusion = (f32[128,128]{1,0:T(8,128)S(1)}, f32[128,128]{1,0:T(8,128)S(1)}) fusion(f32[128]{0:T(128)S(1)} %get-tuple-element.47, f32[128]{0:T(128)S(1)} %get-tuple-element.48, f32[128]{0:T(128)S(1)} %convert_element_type.24), kind=kLoop, calls=%fused_computation.6 | loop fusion | flops 32768 | bytes 132608 | tf_op jit(solution)/shard_map/mul | solution.py:273
  7.9 0.2 select_reduce_fusion.scales_ref
  8.0 0.5 %turn_queries.1 = (bf16[8,64,128]{2,1,0:T(8,128)(2,1)S(1)}, bf16[8,64,128]{2,1,0:T(8,128)(2,1)S(1)}, bf16[8,128,128]{2,1,0:T(8,128)(2,1)S(1)}) custom-call(bf16[8,128,128]{2,1,0:T(8,128)(2,1)S(1)} %bitcast.15, f32[128,128]{1,0:T(8,128)S(1)} %get-tuple-element.46.cosine_ref, f32[128,128]{1,0:T(8,128)S(1)} %get-tuple-element.45.sine_ref, ...), custom_call_target="tpu_custom_call" | custom-call | tf_op jit(solution)/shard_map/turn_queries/pallas_call | solution.py:78
  8.5 1.6 %collective-permute-start.2 = (bf16[8,64,128]{2,1,0:T(8,128)(2,1)S(1)}, bf16[8,64,128]{2,1,0:T(8,128)(2,1)S(1)}, u32[]{:S(2)}, u32[]{:S(2)}) collective-permute-start(bf16[8,64,128]{2,1,0:T(8,128)(2,1)S(1)} %get-tuple-element.29), channel_id=1, source_target_pairs={{0,1},{1,0},{2,3},{3,2},{4,5},{5,4},{6,7},{7,6},{8,9},{9,8},{10,11... | collective-permute-start | bytes 393224 | tf_op jit(solution)/shard_map/ppermute | solution.py:32
  10.1 0.1 collective-permute-start
  10.3 0.1 scale_values.1.rest_0_
  10.4 0.4 %collective-permute-start.1 = (bf16[8,128,128]{2,1,0:T(8,128)(2,1)S(1)}, bf16[8,128,128]{2,1,0:T(8,128)(2,1)S(1)}, u32[]{:S(2)}, u32[]{:S(2)}) collective-permute-start(bf16[8,128,128]{2,1,0:T(8,128)(2,1)S(1)} %scale_values.1.rest_0_), channel_id=1, source_target_pairs={{0,4},{1,13},{2,6},{3,15},{4,8},{5,1},{6,10},{7,3},{8,12},{9,5},{1... | collective-permute-start | bytes 786440 | tf_op jit(solution)/shard_map/ppermute | solution.py:28
  10.9 2.7 %collective-permute-done.3.rest_0_ = bf16[1040,128]{1,0:T(8,128)(2,1)S(1)} collective-permute-done((bf16[1040,128]{1,0:T(8,128)(2,1)S(1)}, bf16[1040,128]{1,0:T(8,128)(2,1)S(1)}, u32[]{:S(2)}, u32[]{:S(2)}) %collective-permute-start.3) | collective-permute-done | bytes 266272 | tf_op jit(solution)/shard_map/ppermute | solution.py:28
  13.5 0.1 copy.19.table_ref
  13.7 1.4 %collective-permute-done.4.rest_1_ = bf16[1040,128]{1,0:T(8,128)(2,1)S(1)} collective-permute-done((bf16[1040,128]{1,0:T(8,128)(2,1)S(1)}, bf16[1040,128]{1,0:T(8,128)(2,1)S(1)}, u32[]{:S(2)}, u32[]{:S(2)}) %collective-permute-start.4) | collective-permute-done | bytes 266272 | tf_op jit(solution)/shard_map/ppermute | solution.py:32
  15.1 2.2 %block_weights.1 = (bf16[16,64,1024]{2,1,0:T(8,128)(2,1)S(1)}, f32[16,64,128]{2,1,0:T(8,128)S(1)}) custom-call(s32[16,8]{1,0:T(8,128)S(1)} %fusion.1.slots_ref, bf16[8,64,128]{2,1,0:T(8,128)(2,1)S(1)} %get-tuple-element.28._.own_ref, bf16[8,64,128]{2,1,0:T(8,128)(2,1)S(1)} %collective-permute-done.2.sibling_ref, ...), custom_call_target="tpu_custom_call" | custom-call | tf_op jit(solution)/shard_map/block_weights/pallas_call | solution.py:130
  17.2 2.4 %collective-permute-done.1.rest_1_ = bf16[8,128,128]{2,1,0:T(8,128)(2,1)S(1)} collective-permute-done((bf16[8,128,128]{2,1,0:T(8,128)(2,1)S(1)}, bf16[8,128,128]{2,1,0:T(8,128)(2,1)S(1)}, u32[]{:S(2)}, u32[]{:S(2)}) %collective-permute-start.1) | collective-permute-done | bytes 262176 | tf_op jit(solution)/shard_map/ppermute | solution.py:28
  19.6 1.5 %collective-permute-done.5.rest_2_ = bf16[8,128,128]{2,1,0:T(8,128)(2,1)S(1)} collective-permute-done((bf16[8,128,128]{2,1,0:T(8,128)(2,1)S(1)}, bf16[8,128,128]{2,1,0:T(8,128)(2,1)S(1)}, u32[]{:S(2)}, u32[]{:S(2)}) %collective-permute-start.5) | collective-permute-done | bytes 262176 | tf_op jit(solution)/shard_map/ppermute | solution.py:32
  21.2 1.0 %block_outputs.1 = (bf16[32,2048]{1,0:T(8,128)(2,1)S(1)}, bf16[32,2048]{1,0:T(8,128)(2,1)S(1)}) custom-call(s32[16,8]{1,0:T(8,128)S(1)} %fusion.1.slots_ref, bf16[16,64,1024]{2,1,0:T(8,128)(2,1)S(1)} %get-tuple-element.32.weights_ref, f32[16,64,128]{2,1,0:T(8,128)S(1)} %get-tuple-element.33.total_ref, bf16[8,128,128]{2,1,0:T(8,128)(2,1)S(1)} %scale_values.1.rest_0_, ...), custom_call_target="tpu_custom_call" | custom-call | tf_op jit(solution)/shard_map/block_outputs/pallas_call | solution.py:170
  22.1 1.6 %collective-permute-start.6 = (bf16[32,2048]{1,0:T(8,128)(2,1)S(1)}, bf16[32,2048]{1,0:T(8,128)(2,1)S(1)}, u32[]{:S(2)}, u32[]{:S(2)}) collective-permute-start(bf16[32,2048]{1,0:T(8,128)(2,1)S(1)} %get-tuple-element.36), channel_id=1, source_target_pairs={{0,2},{1,3},{2,0},{3,1},{4,6},{5,7},{6,4},{7,5},{8,10},{9,11},{10,... | collective-permute-start | bytes 393224 | tf_op jit(solution)/shard_map/ppermute | solution.py:32
  23.7 4.0 %collective-permute-done.6.refs_1_ = bf16[32,2048]{1,0:T(8,128)(2,1)S(1)} collective-permute-done((bf16[32,2048]{1,0:T(8,128)(2,1)S(1)}, bf16[32,2048]{1,0:T(8,128)(2,1)S(1)}, u32[]{:S(2)}, u32[]{:S(2)}) %collective-permute-start.6) | collective-permute-done | bytes 131104 | tf_op jit(solution)/shard_map/ppermute | solution.py:32
  27.7 0.7 %join_pieces.1 = bf16[32,4096]{1,0:T(8,128)(2,1)} custom-call(bf16[32,2048]{1,0:T(8,128)(2,1)S(1)} %get-tuple-element.35.refs_0_, bf16[32,2048]{1,0:T(8,128)(2,1)S(1)} %collective-permute-done.6.refs_1_), custom_call_target="tpu_custom_call" | custom-call | tf_op jit(solution)/shard_map/join_pieces/pallas_call | solution.py:193
  (28 shorter events, 0.2 us)
Async XLA Ops:
  0.0 1.1 %copy-start = (bf16[2,1024,128]{2,1,0:T(8,128)(2,1)S(1)}, bf16[2,1024,128]{2,1,0:T(8,128)(2,1)}, u32[]{:S(2)}) copy-start(bf16[2,1024,128]{2,1,0:T(8,128)(2,1)} %param.9) | copy-start | bytes 1572868
  0.0 10.2 %copy-start.1 = (bf16[2,1024,128]{2,1,0:T(8,128)(2,1)S(1)}, bf16[2,1024,128]{2,1,0:T(8,128)(2,1)}, u32[]{:S(2)}) copy-start(bf16[2,1024,128]{2,1,0:T(8,128)(2,1)} %param.10) | copy-start | bytes 1572868
  0.0 7.8 %copy-start.3 = (f32[2,16]{1,0:T(2,128)S(1)}, f32[2,16]{1,0:T(2,128)}, u32[]{:S(2)}) copy-start(f32[2,16]{1,0:T(2,128)} %param.12) | copy-start | bytes 388
  0.0 10.1 %copy-start.2 = (s32[8,4,8]{2,1,0:T(4,128)S(1)}, s32[8,4,8]{2,1,0:T(4,128)}, u32[]{:S(2)}) copy-start(s32[8,4,8]{2,1,0:T(4,128)} %param.13) | copy-start | bytes 3076
  1.8 11.7 %collective-permute-start.3 = (bf16[1040,128]{1,0:T(8,128)(2,1)S(1)}, bf16[1040,128]{1,0:T(8,128)(2,1)S(1)}, u32[]{:S(2)}, u32[]{:S(2)}) collective-permute-start(bf16[1040,128]{1,0:T(8,128)(2,1)S(1)} %pad_maximum_fusion), channel_id=1, source_target_pairs={{0,4},{1,13},{2,6},{3,15},{4,8},{5,1},{6,10},{7,3},{8,12},{9,5},{1... | collective-permute-start | bytes 798728 | tf_op jit(solution)/shard_map/ppermute | solution.py:28
  8.5 5.2 %collective-permute-start.2 = (bf16[8,64,128]{2,1,0:T(8,128)(2,1)S(1)}, bf16[8,64,128]{2,1,0:T(8,128)(2,1)S(1)}, u32[]{:S(2)}, u32[]{:S(2)}) collective-permute-start(bf16[8,64,128]{2,1,0:T(8,128)(2,1)S(1)} %get-tuple-element.29), channel_id=1, source_target_pairs={{0,1},{1,0},{2,3},{3,2},{4,5},{5,4},{6,7},{7,6},{8,9},{9,8},{10,11... | collective-permute-start | bytes 393224 | tf_op jit(solution)/shard_map/ppermute | solution.py:32
  10.1 3.5 %collective-permute-start = (s32[8,8]{1,0:T(8,128)S(1)}, s32[8,8]{1,0:T(8,128)S(1)}, u32[]{:S(2)}, u32[]{:S(2)}) collective-permute-start(s32[8,8]{1,0:T(8,128)S(1)} %dynamic-slice_bitcast_fusion.2), channel_id=1, source_target_pairs={{0,1},{1,0},{2,3},{3,2},{4,5},{5,4},{6,7},{7,6},{8,9},{9,8},{10,11... | collective-permute-start | bytes 776 | tf_op jit(solution)/shard_map/ppermute | solution.py:32
  10.4 9.2 %collective-permute-start.1 = (bf16[8,128,128]{2,1,0:T(8,128)(2,1)S(1)}, bf16[8,128,128]{2,1,0:T(8,128)(2,1)S(1)}, u32[]{:S(2)}, u32[]{:S(2)}) collective-permute-start(bf16[8,128,128]{2,1,0:T(8,128)(2,1)S(1)} %scale_values.1.rest_0_), channel_id=1, source_target_pairs={{0,4},{1,13},{2,6},{3,15},{4,8},{5,1},{6,10},{7,3},{8,12},{9,5},{1... | collective-permute-start | bytes 786440 | tf_op jit(solution)/shard_map/ppermute | solution.py:28
  13.5 1.5 %collective-permute-start.4 = (bf16[1040,128]{1,0:T(8,128)(2,1)S(1)}, bf16[1040,128]{1,0:T(8,128)(2,1)S(1)}, u32[]{:S(2)}, u32[]{:S(2)}) collective-permute-start(bf16[1040,128]{1,0:T(8,128)(2,1)S(1)} %collective-permute-done.3.rest_0_), channel_id=1, source_target_pairs={{0,1},{1,0},{2,3},{3,2},{4,5},{5,4},{6,7},{7,6},{8,9},{9,8},{10,11... | collective-permute-start | bytes 798728 | tf_op jit(solution)/shard_map/ppermute | solution.py:32
  19.6 1.5 %collective-permute-start.5 = (bf16[8,128,128]{2,1,0:T(8,128)(2,1)S(1)}, bf16[8,128,128]{2,1,0:T(8,128)(2,1)S(1)}, u32[]{:S(2)}, u32[]{:S(2)}) collective-permute-start(bf16[8,128,128]{2,1,0:T(8,128)(2,1)S(1)} %collective-permute-done.1.rest_1_), channel_id=1, source_target_pairs={{0,1},{1,0},{2,3},{3,2},{4,5},{5,4},{6,7},{7,6},{8,9},{9,8},{10,11... | collective-permute-start | bytes 786440 | tf_op jit(solution)/shard_map/ppermute | solution.py:32
  22.1 5.6 %collective-permute-start.6 = (bf16[32,2048]{1,0:T(8,128)(2,1)S(1)}, bf16[32,2048]{1,0:T(8,128)(2,1)S(1)}, u32[]{:S(2)}, u32[]{:S(2)}) collective-permute-start(bf16[32,2048]{1,0:T(8,128)(2,1)S(1)} %get-tuple-element.36), channel_id=1, source_target_pairs={{0,2},{1,3},{2,0},{3,1},{4,6},{5,7},{6,4},{7,5},{8,10},{9,11},{10,... | collective-permute-start | bytes 393224 | tf_op jit(solution)/shard_map/ppermute | solution.py:32

commit v3 on v2

--- a/solution.py
+++ b/solution.py
@@ -82,7 +82,7 @@
         out_shape=[
             half,
             half,
-            jax.ShapeDtypeStruct((codes.shape[0] // BLOCK, width, BLOCK), jnp.bfloat16),
+            jax.ShapeDtypeStruct((scales.shape[1], width, BLOCK), jnp.bfloat16),
         ],
         compiler_params=granted,
         name="turn_queries",
@@ -215,33 +215,30 @@
     groups = head_count // share
     kv_head = head_place * heads_dev // GROUP
 
-    key_rows = lax.dynamic_index_in_dim(key_codes, kv_head, 0, keepdims=False)
-    (
-        key_rows,
-        queries,
-        positions,
-        value_codes,
-        scale_index,
-        scale_table,
-        block_lists,
-    ) = lax.optimization_barrier(
-        (key_rows, queries, positions, value_codes, scale_index, scale_table, block_lists)
-    )
-    value_rows = lax.dynamic_index_in_dim(value_codes, kv_head, 0, keepdims=False)
     index_rows = lax.dynamic_index_in_dim(scale_index, kv_head, 1, keepdims=False)
-    matches = index_rows[:, :, None] == jnp.arange(scale_table.shape[1], dtype=jnp.int32)
-    scales = jnp.sum(jnp.where(matches, scale_table[:, None, :], 0.0), axis=2)
-
     entries = scale_table.shape[1]
     labels = jnp.pad(
         jnp.broadcast_to(index_rows[0].astype(jnp.bfloat16), (entries, key_blocks)),
         ((0, 0), (0, head_width - key_blocks)),
     )
-    far_keys = jnp.concatenate([key_rows, labels], axis=0)
+    labels, key_codes = lax.optimization_barrier((labels, key_codes))
+    key_rows = lax.dynamic_index_in_dim(key_codes, kv_head, 0, keepdims=False)
+    near_keys = jnp.concatenate([key_rows, labels], axis=0)
+    near_keys, queries, positions, value_codes, scale_index, scale_table, block_lists = (
+        lax.optimization_barrier(
+            (near_keys, queries, positions, value_codes, scale_index, scale_table, block_lists)
+        )
+    )
+    index_rows = lax.dynamic_index_in_dim(scale_index, kv_head, 1, keepdims=False)
+    far_keys = near_keys
     key_parts = []
     for _ in range(reach_hops):
         far_keys = sent(far_keys, 1, share)
         key_parts += [far_keys, swapped(far_keys, 1)]
+
+    value_rows = lax.dynamic_index_in_dim(value_codes, kv_head, 0, keepdims=False)
+    matches = index_rows[:, :, None] == jnp.arange(entries, dtype=jnp.int32)
+    scales = jnp.sum(jnp.where(matches, scale_table[:, None, :], 0.0), axis=2)
 
     own_lists = lax.dynamic_index_in_dim(block_lists, cycle_place, 1, keepdims=False)
     lists = jnp.concatenate([own_lists, swapped(own_lists, 1)], axis=0)
@@ -273,9 +270,9 @@
     sine = jnp.sin(angles) * signs[None, :]
 
     own, sibling, near = turn_queries(
-        jnp.transpose(ordered(queries), (1, 0, 2)), cosine, sine, key_rows, scales
-    )
-    values = scale_blocks(scales, value_rows, own, 1)
+        jnp.transpose(ordered(queries), (1, 0, 2)), cosine, sine, near_keys, scales
+    )
+    values = scale_blocks(scales, value_rows, near_keys, 1)
     value_steps = []
     far_values = values
     for _ in range(reach_hops):

time: 28.7 us -> 27.4 us (0.955)
  local copies, waits for them, and re-layouts: 3.72 us -> 2.27 us
    unnamed x12 -> x14, local copies, waits for them, and re-layouts: 1.1 us -> 0.32 us
    dynamic_slice x1, local copies, waits for them, and re-layouts: 0.69 us -> 0.01 us  [on_device(): lax.dynamic_index_in_dim(scale_index, kv_head, 1, keepdims=False)]
  transfers between devices with their start and end apart: 7 -> 7, of which waited for: 5 -> 5; matrix products, arithmetic and copies ran while one was open for 11% -> 9% of each run, Pallas kernels for 10% -> 10%
where the time goes in v3:
time: 27.4 us; the launch traced here: 27.2 us
  waiting for transfers between devices  12.2 us (45%)
  starting transfers between devices  6.86 us (25%)
  Pallas kernels  4.45 us (16%)
  local copies, waits for them, and re-layouts  2.27 us (8%)
  other arithmetic  1.35 us (5%)
    ppermute x5, waiting for transfers between devices, swapped(): lax.ppermute(x, 'head', [(i, i ^ mask) for i in range(lax.axis_size('head...  6.97 us
    ppermute x2, waiting for transfers between devices, sent(): return lax.ppermute(x, ('ctx', 'head'), pairs)  5.18 us
    ppermute x2, starting transfers between devices, sent(): return lax.ppermute(x, ('ctx', 'head'), pairs)  3.52 us
    ppermute x5, starting transfers between devices, swapped(): lax.ppermute(x, 'head', [(i, i ^ mask) for i in range(lax.axis_size('head...  3.34 us
    pallas_call x1, Pallas kernels, block_weights(): pl.pallas_call(score_kernel, in_specs=[in_vmem] * (5 + len(parts)), out_s...  2.17 us
    dynamic_slice x2, local copies, waits for them, and re-layouts, ordered(): lax.dynamic_slice(cut, (jnp.bitwise_xor(group, n), jnp.bitwise_xor(core,...  0.96 us
    pallas_call x1, Pallas kernels, block_outputs(): pl.pallas_call(functools.partial(value_kernel, inputs=len(parts)), in_spe...  0.95 us
    convert_element_type x1, other arithmetic, on_device(): index_rows[0].astype(jnp.bfloat16)  0.77 us
  transfers between devices with their start and end apart: 7, of which 5 were waited for; matrix products, arithmetic and copies ran while one was open for 9% of the time, Pallas kernels for 10%

profile of v3, /device:TPU:0, one launch (start us, length us, event | category | flops | bytes accessed | tf_op | source)
XLA Modules:
  0.0 27.2 jit_solution(12036108751806628442)
XLA Ops:
  0.0 0.8 %fusion.15 = bf16[8]{0:T(256)(128)(2,1)S(1)} fusion(s32[2,2,8]{2,1,0:T(2,128)} %param.11, s32[]{:T(128)S(6)} %select_n.108), kind=kLoop, calls=%fused_computation.53 | loop fusion | flops 8 | bytes 52 | tf_op jit(solution)/shard_map/convert_element_type | solution.py:221
  0.8 0.3 copy-done
  1.1 3.1 %collective-permute-start.3 = (bf16[1040,128]{1,0:T(8,128)(2,1)S(1)}, bf16[1040,128]{1,0:T(8,128)(2,1)S(1)}, u32[]{:S(2)}, u32[]{:S(2)}) collective-permute-start(bf16[1040,128]{1,0:T(8,128)(2,1)S(1)} %pad_maximum_fusion._.codes_ref), channel_id=1, source_target_pairs={{0,4},{1,13},{2,6},{3,15},{4,8},{5,1},{6,10},{7,3},{8,12},{9,5},{1... | collective-permute-start | bytes 798728 | tf_op jit(solution)/shard_map/ppermute | solution.py:28
  4.2 0.7 %reshape.51 = s32[2,2,32]{2,1,0:T(2,128)S(1)} reshape(s32[128]{0:T(128)} %param.8) | data formatting | bytes 1024 | tf_op jit(solution)/shard_map/reshape | solution.py:252
  5.0 0.1 convert_element_type.25
  5.1 1.0 %constant_dynamic-slice_fusion.7 = (bf16[1,1,32,8,128]{4,3,2,1,0:T(8,128)(2,1)S(1)}, bf16[1,1,32,8,128]{4,3,2,1,0:T(8,128)(2,1)S(1)}, bf16[1,1,32,8,128]{4,3,2,1,0:T(8,128)(2,1)S(1)}, bf16[1,1,32,8,128]{4,3,2,1,0:T(8,128)(2,1)S(1)}) fusion(bf16[2,2,32,8,128]{4,3,2,1,0:T(8,128)(2,1)} %bitcast.16, s32[]{:T(128)S(6)} %select_n.119, s32[]{:T(128)S(6)} %select_n.120, ...), kind=kLoop, calls=%fused_computation.38 | loop fusion | bytes 524304 | tf_op jit(solution)/shard_map/dynamic_slice | solution.py:254
  6.2 0.3 %fusion = (f32[128,128]{1,0:T(8,128)S(1)}, f32[128,128]{1,0:T(8,128)S(1)}) fusion(f32[128]{0:T(128)S(1)} %get-tuple-element.51, f32[128]{0:T(128)S(1)} %get-tuple-element.52, f32[128]{0:T(128)S(1)} %convert_element_type.25), kind=kLoop, calls=%fused_computation.6 | loop fusion | flops 32768 | bytes 132608 | tf_op jit(solution)/shard_map/mul | solution.py:270
  6.5 0.2 select_reduce_fusion.scales_ref
  6.7 0.5 %turn_queries.1 = (bf16[8,64,128]{2,1,0:T(8,128)(2,1)S(1)}, bf16[8,64,128]{2,1,0:T(8,128)(2,1)S(1)}, bf16[8,128,128]{2,1,0:T(8,128)(2,1)S(1)}) custom-call(bf16[8,128,128]{2,1,0:T(8,128)(2,1)S(1)} %bitcast.15, f32[128,128]{1,0:T(8,128)S(1)} %get-tuple-element.50.cosine_ref, f32[128,128]{1,0:T(8,128)S(1)} %get-tuple-element.49.sine_ref, ...), custom_call_target="tpu_custom_call" | custom-call | tf_op jit(solution)/shard_map/turn_queries/pallas_call | solution.py:78
  7.1 1.6 %collective-permute-start.2 = (bf16[8,64,128]{2,1,0:T(8,128)(2,1)S(1)}, bf16[8,64,128]{2,1,0:T(8,128)(2,1)S(1)}, u32[]{:S(2)}, u32[]{:S(2)}) collective-permute-start(bf16[8,64,128]{2,1,0:T(8,128)(2,1)S(1)} %get-tuple-element.33), channel_id=1, source_target_pairs={{0,1},{1,0},{2,3},{3,2},{4,5},{5,4},{6,7},{7,6},{8,9},{9,8},{10,11... | collective-permute-start | bytes 393224 | tf_op jit(solution)/shard_map/ppermute | solution.py:32
  8.8 0.1 collective-permute-start
  8.9 0.1 scale_values.1.rest_0_
  9.1 0.4 %collective-permute-start.1 = (bf16[8,128,128]{2,1,0:T(8,128)(2,1)S(1)}, bf16[8,128,128]{2,1,0:T(8,128)(2,1)S(1)}, u32[]{:S(2)}, u32[]{:S(2)}) collective-permute-start(bf16[8,128,128]{2,1,0:T(8,128)(2,1)S(1)} %scale_values.1.rest_0_), channel_id=1, source_target_pairs={{0,4},{1,13},{2,6},{3,15},{4,8},{5,1},{6,10},{7,3},{8,12},{9,5},{1... | collective-permute-start | bytes 786440 | tf_op jit(solution)/shard_map/ppermute | solution.py:28
  9.5 3.4 %collective-permute-done.3.rest_0_ = bf16[1040,128]{1,0:T(8,128)(2,1)S(1)} collective-permute-done((bf16[1040,128]{1,0:T(8,128)(2,1)S(1)}, bf16[1040,128]{1,0:T(8,128)(2,1)S(1)}, u32[]{:S(2)}, u32[]{:S(2)}) %collective-permute-start.3) | collective-permute-done | bytes 266272 | tf_op jit(solution)/shard_map/ppermute | solution.py:28
  12.9 0.0 collective-permute-start.4
  12.9 0.1 copy.19.table_ref
  13.1 1.4 %collective-permute-done.4.rest_1_ = bf16[1040,128]{1,0:T(8,128)(2,1)S(1)} collective-permute-done((bf16[1040,128]{1,0:T(8,128)(2,1)S(1)}, bf16[1040,128]{1,0:T(8,128)(2,1)S(1)}, u32[]{:S(2)}, u32[]{:S(2)}) %collective-permute-start.4) | collective-permute-done | bytes 266272 | tf_op jit(solution)/shard_map/ppermute | solution.py:32
  14.5 2.2 %block_weights.1 = (bf16[16,64,1024]{2,1,0:T(8,128)(2,1)S(1)}, f32[16,64,128]{2,1,0:T(8,128)S(1)}) custom-call(s32[16,8]{1,0:T(8,128)S(1)} %fusion.1.slots_ref, bf16[8,64,128]{2,1,0:T(8,128)(2,1)S(1)} %get-tuple-element.32.own_ref, bf16[8,64,128]{2,1,0:T(8,128)(2,1)S(1)} %collective-permute-done.2.sibling_ref, ...), custom_call_target="tpu_custom_call" | custom-call | tf_op jit(solution)/shard_map/block_weights/pallas_call | solution.py:130
  16.6 1.8 %collective-permute-done.1.rest_1_ = bf16[8,128,128]{2,1,0:T(8,128)(2,1)S(1)} collective-permute-done((bf16[8,128,128]{2,1,0:T(8,128)(2,1)S(1)}, bf16[8,128,128]{2,1,0:T(8,128)(2,1)S(1)}, u32[]{:S(2)}, u32[]{:S(2)}) %collective-permute-start.1) | collective-permute-done | bytes 262176 | tf_op jit(solution)/shard_map/ppermute | solution.py:28
  18.4 1.5 %collective-permute-done.5.rest_2_ = bf16[8,128,128]{2,1,0:T(8,128)(2,1)S(1)} collective-permute-done((bf16[8,128,128]{2,1,0:T(8,128)(2,1)S(1)}, bf16[8,128,128]{2,1,0:T(8,128)(2,1)S(1)}, u32[]{:S(2)}, u32[]{:S(2)}) %collective-permute-start.5) | collective-permute-done | bytes 262176 | tf_op jit(solution)/shard_map/ppermute | solution.py:32
  20.0 1.0 %block_outputs.1 = (bf16[32,2048]{1,0:T(8,128)(2,1)S(1)}, bf16[32,2048]{1,0:T(8,128)(2,1)S(1)}) custom-call(s32[16,8]{1,0:T(8,128)S(1)} %fusion.1.slots_ref, bf16[16,64,1024]{2,1,0:T(8,128)(2,1)S(1)} %get-tuple-element.36.weights_ref, f32[16,64,128]{2,1,0:T(8,128)S(1)} %get-tuple-element.37.total_ref, bf16[8,128,128]{2,1,0:T(8,128)(2,1)S(1)} %scale_values.1.rest_0_, ...), custom_call_target="tpu_custom_call" | custom-call | tf_op jit(solution)/shard_map/block_outputs/pallas_call | solution.py:170
  20.9 1.6 %collective-permute-start.6 = (bf16[32,2048]{1,0:T(8,128)(2,1)S(1)}, bf16[32,2048]{1,0:T(8,128)(2,1)S(1)}, u32[]{:S(2)}, u32[]{:S(2)}) collective-permute-start(bf16[32,2048]{1,0:T(8,128)(2,1)S(1)} %get-tuple-element.40), channel_id=1, source_target_pairs={{0,2},{1,3},{2,0},{3,1},{4,6},{5,7},{6,4},{7,5},{8,10},{9,11},{10,... | collective-permute-start | bytes 393224 | tf_op jit(solution)/shard_map/ppermute | solution.py:32
  22.5 4.0 %collective-permute-done.6.refs_1_ = bf16[32,2048]{1,0:T(8,128)(2,1)S(1)} collective-permute-done((bf16[32,2048]{1,0:T(8,128)(2,1)S(1)}, bf16[32,2048]{1,0:T(8,128)(2,1)S(1)}, u32[]{:S(2)}, u32[]{:S(2)}) %collective-permute-start.6) | collective-permute-done | bytes 131104 | tf_op jit(solution)/shard_map/ppermute | solution.py:32
  26.5 0.7 %join_pieces.1 = bf16[32,4096]{1,0:T(8,128)(2,1)} custom-call(bf16[32,2048]{1,0:T(8,128)(2,1)S(1)} %get-tuple-element.39.refs_0_, bf16[32,2048]{1,0:T(8,128)(2,1)S(1)} %collective-permute-done.6.refs_1_), custom_call_target="tpu_custom_call" | custom-call | tf_op jit(solution)/shard_map/join_pieces/pallas_call | solution.py:193
  (30 shorter events, 0.3 us)
Async XLA Ops:
  0.0 1.1 %copy-start = (bf16[2,1024,128]{2,1,0:T(8,128)(2,1)S(1)}, bf16[2,1024,128]{2,1,0:T(8,128)(2,1)}, u32[]{:S(2)}) copy-start(bf16[2,1024,128]{2,1,0:T(8,128)(2,1)} %param.9) | copy-start | bytes 1572868
  0.0 6.1 %copy-start.4 = (s32[2,2,8]{2,1,0:T(2,128)S(1)}, s32[2,2,8]{2,1,0:T(2,128)}, u32[]{:S(2)}) copy-start(s32[2,2,8]{2,1,0:T(2,128)} %param.11) | copy-start | bytes 388
  0.0 8.9 %copy-start.1 = (bf16[2,1024,128]{2,1,0:T(8,128)(2,1)S(1)}, bf16[2,1024,128]{2,1,0:T(8,128)(2,1)}, u32[]{:S(2)}) copy-start(bf16[2,1024,128]{2,1,0:T(8,128)(2,1)} %param.10) | copy-start | bytes 1572868
  0.0 6.5 %copy-start.3 = (f32[2,16]{1,0:T(2,128)S(1)}, f32[2,16]{1,0:T(2,128)}, u32[]{:S(2)}) copy-start(f32[2,16]{1,0:T(2,128)} %param.12) | copy-start | bytes 388
  0.0 8.8 %copy-start.2 = (s32[8,4,8]{2,1,0:T(4,128)S(1)}, s32[8,4,8]{2,1,0:T(4,128)}, u32[]{:S(2)}) copy-start(s32[8,4,8]{2,1,0:T(4,128)} %param.13) | copy-start | bytes 3076
  1.1 11.8 %collective-permute-start.3 = (bf16[1040,128]{1,0:T(8,128)(2,1)S(1)}, bf16[1040,128]{1,0:T(8,128)(2,1)S(1)}, u32[]{:S(2)}, u32[]{:S(2)}) collective-permute-start(bf16[1040,128]{1,0:T(8,128)(2,1)S(1)} %pad_maximum_fusion._.codes_ref), channel_id=1, source_target_pairs={{0,4},{1,13},{2,6},{3,15},{4,8},{5,1},{6,10},{7,3},{8,12},{9,5},{1... | collective-permute-start | bytes 798728 | tf_op jit(solution)/shard_map/ppermute | solution.py:28
  7.1 5.9 %collective-permute-start.2 = (bf16[8,64,128]{2,1,0:T(8,128)(2,1)S(1)}, bf16[8,64,128]{2,1,0:T(8,128)(2,1)S(1)}, u32[]{:S(2)}, u32[]{:S(2)}) collective-permute-start(bf16[8,64,128]{2,1,0:T(8,128)(2,1)S(1)} %get-tuple-element.33), channel_id=1, source_target_pairs={{0,1},{1,0},{2,3},{3,2},{4,5},{5,4},{6,7},{7,6},{8,9},{9,8},{10,11... | collective-permute-start | bytes 393224 | tf_op jit(solution)/shard_map/ppermute | solution.py:32
  8.8 4.2 %collective-permute-start = (s32[8,8]{1,0:T(8,128)S(1)}, s32[8,8]{1,0:T(8,128)S(1)}, u32[]{:S(2)}, u32[]{:S(2)}) collective-permute-start(s32[8,8]{1,0:T(8,128)S(1)} %dynamic-slice_bitcast_fusion.2), channel_id=1, source_target_pairs={{0,1},{1,0},{2,3},{3,2},{4,5},{5,4},{6,7},{7,6},{8,9},{9,8},{10,11... | collective-permute-start | bytes 776 | tf_op jit(solution)/shard_map/ppermute | solution.py:32
  9.1 9.3 %collective-permute-start.1 = (bf16[8,128,128]{2,1,0:T(8,128)(2,1)S(1)}, bf16[8,128,128]{2,1,0:T(8,128)(2,1)S(1)}, u32[]{:S(2)}, u32[]{:S(2)}) collective-permute-start(bf16[8,128,128]{2,1,0:T(8,128)(2,1)S(1)} %scale_values.1.rest_0_), channel_id=1, source_target_pairs={{0,4},{1,13},{2,6},{3,15},{4,8},{5,1},{6,10},{7,3},{8,12},{9,5},{1... | collective-permute-start | bytes 786440 | tf_op jit(solution)/shard_map/ppermute | solution.py:28
  12.9 1.5 %collective-permute-start.4 = (bf16[1040,128]{1,0:T(8,128)(2,1)S(1)}, bf16[1040,128]{1,0:T(8,128)(2,1)S(1)}, u32[]{:S(2)}, u32[]{:S(2)}) collective-permute-start(bf16[1040,128]{1,0:T(8,128)(2,1)S(1)} %collective-permute-done.3.rest_0_), channel_id=1, source_target_pairs={{0,1},{1,0},{2,3},{3,2},{4,5},{5,4},{6,7},{7,6},{8,9},{9,8},{10,11... | collective-permute-start | bytes 798728 | tf_op jit(solution)/shard_map/ppermute | solution.py:32
  18.4 1.5 %collective-permute-start.5 = (bf16[8,128,128]{2,1,0:T(8,128)(2,1)S(1)}, bf16[8,128,128]{2,1,0:T(8,128)(2,1)S(1)}, u32[]{:S(2)}, u32[]{:S(2)}) collective-permute-start(bf16[8,128,128]{2,1,0:T(8,128)(2,1)S(1)} %collective-permute-done.1.rest_1_), channel_id=1, source_target_pairs={{0,1},{1,0},{2,3},{3,2},{4,5},{5,4},{6,7},{7,6},{8,9},{9,8},{10,11... | collective-permute-start | bytes 786440 | tf_op jit(solution)/shard_map/ppermute | solution.py:32
  20.9 5.6 %collective-permute-start.6 = (bf16[32,2048]{1,0:T(8,128)(2,1)S(1)}, bf16[32,2048]{1,0:T(8,128)(2,1)S(1)}, u32[]{:S(2)}, u32[]{:S(2)}) collective-permute-start(bf16[32,2048]{1,0:T(8,128)(2,1)S(1)} %get-tuple-element.40), channel_id=1, source_target_pairs={{0,2},{1,3},{2,0},{3,1},{4,6},{5,7},{6,4},{7,5},{8,10},{9,11},{10,... | collective-permute-start | bytes 393224 | tf_op jit(solution)/shard_map/ppermute | solution.py:32

commit v4 on v3

--- a/solution.py
+++ b/solution.py
@@ -10,6 +10,7 @@
 
 GROUP = 16
 BLOCK = 128
+ROW_TILE = 16
 ROPE_BASE = 500000.0
 VMEM_GRANT = 16 * 2**20
 
@@ -17,15 +18,25 @@
 granted = pltpu.CompilerParams(vmem_limit_bytes=VMEM_GRANT)
 
 
-def sent(x, hop, share):
+def paired(cycle, hops):
+    return hops == 1 and cycle % 2 == 0
+
+
+def source(place, part, cycle, pairs):
+    if pairs:
+        return place + 1 if place % 2 == part else place - 1
+    return place - 1 if part == 0 else place + 1
+
+
+def sent(x, share, pairs):
     cycle = lax.axis_size("ctx")
     heads = lax.axis_size("head")
-    pairs = []
-    for place in range(cycle):
-        for head in range(heads):
-            by = hop if head % share == 0 else -hop
-            pairs.append((place * heads + head, (place + by) % cycle * heads + head))
-    return lax.ppermute(x, ("ctx", "head"), pairs)
+    moves = [
+        (source(place, head % share, cycle, pairs) % cycle * heads + head, place * heads + head)
+        for place in range(cycle)
+        for head in range(heads)
+    ]
+    return lax.ppermute(x, ("ctx", "head"), moves)
 
 
 def swapped(x, mask):
@@ -57,7 +68,7 @@
         store[at + block] = (codes * scales[0, block]).T.astype(jnp.bfloat16)
 
 
-def turn_kernel(queries_ref, cosine_ref, sine_ref, codes_ref, scales_ref, *outs):
+def turn_kernel(queries_ref, cosine_ref, sine_ref, codes_ref, scales_ref, lists_ref, *outs):
     own_ref, sibling_ref, keys_ref = outs
     heads_dev, rows, width = own_ref.shape
     cosine = cosine_ref[...]
@@ -68,25 +79,29 @@
         other = jnp.where(even, pltpu.roll(plain, width - 1, 1), pltpu.roll(plain, 1, 1))
         turned = (plain * cosine + other * sine).astype(jnp.bfloat16)
         own_ref[head] = turned[:rows]
-        sibling_ref[head] = turned[rows:]
+        sibling_ref[head, :rows] = turned[rows:]
+        sibling_ref[head, rows:] = jnp.broadcast_to(
+            lists_ref[head : head + 1], sibling_ref[head, rows:].shape
+        )
     scaled_keys(codes_ref, scales_ref[...], keys_ref.shape[0], keys_ref, 0)
 
 
-def turn_queries(queries, cosine, sine, codes, scales):
+def turn_queries(queries, cosine, sine, codes, scales, lists):
     heads_dev, rows, width = queries.shape
-    half = jax.ShapeDtypeStruct((heads_dev, rows // 2, width), jnp.bfloat16)
+    half = (heads_dev, rows // 2, width)
+    more = (heads_dev, rows // 2 + ROW_TILE, width)
     return pl.pallas_call(
         turn_kernel,
-        in_specs=[in_vmem] * 5,
+        in_specs=[in_vmem] * 6,
         out_specs=[in_vmem] * 3,
         out_shape=[
-            half,
-            half,
+            jax.ShapeDtypeStruct(half, jnp.bfloat16),
+            jax.ShapeDtypeStruct(more, jnp.bfloat16),
             jax.ShapeDtypeStruct((scales.shape[1], width, BLOCK), jnp.bfloat16),
         ],
         compiler_params=granted,
         name="turn_queries",
-    )(queries, cosine, sine, codes, scales)
+    )(queries, cosine, sine, codes, scales, lists)
 
 
 def score_kernel(slots_ref, own_ref, sibling_ref, near_ref, table_ref, *rest):
@@ -105,7 +120,7 @@
         scales = jnp.sum(jnp.where(index == entries, table, 0.0), axis=0, keepdims=True)
         scaled_keys(part, scales, blocks, store, (n + 1) * blocks)
     for head in range(heads):
-        turned = (own_ref if head < heads_dev else sibling_ref)[head % heads_dev]
+        turned = (own_ref if head < heads_dev else sibling_ref)[head % heads_dev, :rows]
         scores = [
             jnp.dot(turned, store[slots[head, i]], preferred_element_type=jnp.float32)
             for i in range(picks)
@@ -206,6 +221,7 @@
     head_count = lax.axis_size("head")
     head_place = lax.axis_index("head")
     reach_hops = min(3, (cycle_size - 1) // 2)
+    pairs = paired(cycle_size, reach_hops)
     rows_dev, heads_dev, head_width = queries.shape
     key_blocks = key_codes.shape[1] // BLOCK
     share = GROUP // heads_dev
@@ -233,21 +249,18 @@
     far_keys = near_keys
     key_parts = []
     for _ in range(reach_hops):
-        far_keys = sent(far_keys, 1, share)
-        key_parts += [far_keys, swapped(far_keys, 1)]
+        far_keys = sent(far_keys, share, pairs)
+        key_parts.append(far_keys)
 
     value_rows = lax.dynamic_index_in_dim(value_codes, kv_head, 0, keepdims=False)
     matches = index_rows[:, :, None] == jnp.arange(entries, dtype=jnp.int32)
     scales = jnp.sum(jnp.where(matches, scale_table[:, None, :], 0.0), axis=2)
 
+    values = scale_blocks(scales, value_rows, near_keys, 1)
+    values, queries, positions, block_lists = lax.optimization_barrier(
+        (values, queries, positions, block_lists)
+    )
     own_lists = lax.dynamic_index_in_dim(block_lists, cycle_place, 1, keepdims=False)
-    lists = jnp.concatenate([own_lists, swapped(own_lists, 1)], axis=0)
-    offset = jnp.mod(lists // key_blocks - cycle_place, cycle_size)
-    above = offset <= reach_hops
-    hops = jnp.where(above, offset, cycle_size - offset)
-    place = 2 * hops - jnp.where(above == (core == 1), 1, 0)
-    slots = lists % key_blocks + key_blocks * jnp.where(offset == 0, 0, place)
-
     def ordered(x):
         cut = x.reshape((groups, share, rows_dev // head_count) + x.shape[1:])
         taken = [
@@ -269,17 +282,30 @@
     cosine = jnp.cos(angles)
     sine = jnp.sin(angles) * signs[None, :]
 
+    picks = own_lists.shape[1]
+    carried = jnp.pad(own_lists.astype(jnp.bfloat16), ((0, 0), (0, head_width - picks)))
     own, sibling, near = turn_queries(
-        jnp.transpose(ordered(queries), (1, 0, 2)), cosine, sine, near_keys, scales
-    )
-    values = scale_blocks(scales, value_rows, near_keys, 1)
+        jnp.transpose(ordered(queries), (1, 0, 2)), cosine, sine, near_keys, scales, carried
+    )
+    sibling, key_parts[0] = lax.optimization_barrier((sibling, key_parts[0]))
+    key_parts = [part for far in key_parts for part in (far, swapped(far, 1))]
+    sibling = swapped(sibling, 1)
+    sibling_lists = sibling[:, rows_dev // share, :picks].astype(jnp.int32)
+    lists = jnp.concatenate([own_lists, sibling_lists], axis=0)
+    offset = jnp.mod(lists // key_blocks - cycle_place, cycle_size)
+    above = offset <= reach_hops
+    hops = jnp.where(above, offset, cycle_size - offset)
+    from_above = (cycle_place % 2 if pairs else 1) == core
+    place = 2 * hops - jnp.where(above == from_above, 1, 0)
+    slots = lists % key_blocks + key_blocks * jnp.where(offset == 0, 0, place)
+
     value_steps = []
     far_values = values
     for _ in range(reach_hops):
-        far_values = sent(far_values, 1, share)
+        far_values = sent(far_values, share, pairs)
         value_steps.append(far_values)
     weights, total = block_weights(
-        slots, own, swapped(sibling, 1), near, scale_table[0][:, None], key_parts
+        slots, own, sibling, near, scale_table[0][:, None], key_parts
     )
 
     *value_steps, weights = lax.optimization_barrier((*value_steps, weights))

time: 27.4 us -> 27.1 us (0.989)
  waiting for transfers between devices: 12.2 us -> 10.2 us
  starting transfers between devices: 6.86 us -> 7.59 us
  other arithmetic: 1.35 us -> 2.03 us
    ppermute x2, waiting for transfers between devices: 5.18 us -> 3.26 us  [sent(): return lax.ppermute(x, ('ctx', 'head'), moves)]
    ppermute x5 -> x4, starting transfers between devices: 3.34 us -> 4.42 us  [swapped(): lax.ppermute(x, 'head', [(i, i ^ mask) for i in range(lax.axis_size('head...]
    squeeze x1, local copies, waits for them, and re-layouts: 0.02 us -> 0.97 us  [on_device(): lax.dynamic_index_in_dim(value_codes, kv_head, 0, keepdims=False)]
    dynamic_slice x2, local copies, waits for them, and re-layouts: 0.96 us -> 0.04 us  [ordered(): lax.dynamic_slice(cut, (jnp.bitwise_xor(group, n), jnp.bitwise_xor(core,...]
    dynamic_slice x1, local copies, waits for them, and re-layouts: 0.01 us -> 0.69 us  [on_device(): lax.dynamic_index_in_dim(scale_index, kv_head, 1, keepdims=False)]
    reduce_sum x1, other arithmetic: 0.16 us -> 0.83 us  [on_device(): scales = jnp.sum(jnp.where(matches, scale_table[:, None, :], 0.0), axis=2)]
    reshape x1, local copies, waits for them, and re-layouts: 0.74 us -> 0.08 us  [ordered(): cut = x.reshape((groups, share, rows_dev // head_count) + x.shape[1:])]
    ppermute x2, starting transfers between devices: 3.52 us -> 3.17 us  [sent(): return lax.ppermute(x, ('ctx', 'head'), moves)]
  transfers between devices with their start and end apart: 7 -> 6, of which waited for: 5 -> 5; matrix products, arithmetic and copies ran while one was open for 9% -> 12% of each run, Pallas kernels for 10% -> 10%
where the time goes in v4:
time: 27.1 us; the launch traced here: 26.9 us
  waiting for transfers between devices  10.2 us (38%)
  starting transfers between devices  7.59 us (28%)
  Pallas kernels  4.45 us (16%)
  local copies, waits for them, and re-layouts  2.41 us (9%)
  other arithmetic  2.03 us (7%)
    ppermute x4, waiting for transfers between devices, swapped(): lax.ppermute(x, 'head', [(i, i ^ mask) for i in range(lax.axis_size('head...  6.93 us
    ppermute x4, starting transfers between devices, swapped(): lax.ppermute(x, 'head', [(i, i ^ mask) for i in range(lax.axis_size('head...  4.42 us
    ppermute x2, waiting for transfers between devices, sent(): return lax.ppermute(x, ('ctx', 'head'), moves)  3.26 us
    ppermute x2, starting transfers between devices, sent(): return lax.ppermute(x, ('ctx', 'head'), moves)  3.17 us
    pallas_call x1, Pallas kernels, block_weights(): pl.pallas_call(score_kernel, in_specs=[in_vmem] * (5 + len(parts)), out_s...  2.17 us
    squeeze x1, local copies, waits for them, and re-layouts, on_device(): lax.dynamic_index_in_dim(value_codes, kv_head, 0, keepdims=False)  0.97 us
    pallas_call x1, Pallas kernels, block_outputs(): pl.pallas_call(functools.partial(value_kernel, inputs=len(parts)), in_spe...  0.95 us
    reduce_sum x1, other arithmetic, on_device(): scales = jnp.sum(jnp.where(matches, scale_table[:, None, :], 0.0), axis=2)  0.83 us
  transfers between devices with their start and end apart: 6, of which 5 were waited for; matrix products, arithmetic and copies ran while one was open for 12% of the time, Pallas kernels for 10%

profile of v4, /device:TPU:0, one launch (start us, length us, event | category | flops | bytes accessed | tf_op | source)
XLA Modules:
  0.0 26.9 jit_solution(4263193927920064940)
XLA Ops:
  0.0 0.8 %fusion.15 = bf16[8]{0:T(256)(128)(2,1)S(1)} fusion(s32[2,2,8]{2,1,0:T(2,128)} %param.11, s32[]{:T(128)S(6)} %select_n.112), kind=kLoop, calls=%fused_computation.54 | loop fusion | flops 8 | bytes 52 | tf_op jit(solution)/shard_map/convert_element_type | solution.py:237
  0.8 0.3 %copy-done = bf16[2,1024,128]{2,1,0:T(8,128)(2,1)S(1)} copy-done((bf16[2,1024,128]{2,1,0:T(8,128)(2,1)S(1)}, bf16[2,1024,128]{2,1,0:T(8,128)(2,1)}, u32[]{:S(2)}) %copy-start) | copy-done | bytes 524312
  1.2 3.1 %collective-permute-start = (bf16[1040,128]{1,0:T(8,128)(2,1)S(1)}, bf16[1040,128]{1,0:T(8,128)(2,1)S(1)}, u32[]{:S(2)}, u32[]{:S(2)}) collective-permute-start(bf16[1040,128]{1,0:T(8,128)(2,1)S(1)} %pad_maximum_fusion._.codes_ref), channel_id=1, source_target_pairs={{4,0},{13,1},{6,2},{15,3},{0,4},{9,5},{2,6},{11,7},{12,8},{5,9},{1... | collective-permute-start | bytes 798728 | tf_op jit(solution)/shard_map/ppermute | solution.py:39
  4.3 1.0 %dynamic-slice_bitcast_fusion.codes_ref = bf16[1024,128]{1,0:T(8,128)(2,1)S(1)} fusion(bf16[2,1024,128]{2,1,0:T(8,128)(2,1)} %param.10, s32[]{:T(128)S(6)} %select_n.112), kind=kLoop, calls=%fused_computation.2 | loop fusion | bytes 524292 | tf_op jit(solution)/shard_map/jit(dynamic_index_in_dim)/squeeze | solution.py:255
  5.3 0.7 %constant_dynamic-slice_fusion.8 = s32[2,1,8]{2,1,0:T(1,128)S(1)} fusion(s32[2,2,8]{2,1,0:T(2,128)} %param.11, s32[]{:T(128)S(6)} %select_n.112), kind=kLoop, calls=%fused_computation.40 | loop fusion | bytes 132 | tf_op jit(solution)/shard_map/jit(dynamic_index_in_dim)/dynamic_slice | solution.py:248
  6.0 0.8 %select_reduce_fusion.scales_ref = f32[2,8]{1,0:T(2,128)S(1)} fusion(f32[2,16]{1,0:T(2,128)} %param.12, s32[2,8]{1,0:T(2,128)S(1)} %bitcast.20), kind=kLoop, calls=%fused_computation.26 | loop fusion | flops 752 | bytes 256 | tf_op jit(solution)/shard_map/reduce_sum | solution.py:257
  6.8 0.1 scale_values.1.rest_0_
  7.0 0.1 collective-permute-start.2
  7.1 0.1 reshape.53
  7.4 0.1 convert_element_type.36
  7.5 0.3 %fusion = (f32[128,128]{1,0:T(8,128)S(1)}, f32[128,128]{1,0:T(8,128)S(1)}) fusion(f32[128]{0:T(128)S(1)} %get-tuple-element.65, f32[128]{0:T(128)S(1)} %get-tuple-element.66, f32[128]{0:T(128)S(1)} %convert_element_type.36), kind=kLoop, calls=%fused_computation.6 | loop fusion | flops 32768 | bytes 132608 | tf_op jit(solution)/shard_map/mul | solution.py:283
  7.8 0.5 %turn_queries.1 = (bf16[8,64,128]{2,1,0:T(8,128)(2,1)S(1)}, bf16[8,80,128]{2,1,0:T(8,128)(2,1)S(1)}, bf16[8,128,128]{2,1,0:T(8,128)(2,1)S(1)}) custom-call(bf16[8,128,128]{2,1,0:T(8,128)(2,1)S(1)} %bitcast.17, f32[128,128]{1,0:T(8,128)S(1)} %get-tuple-element.64.cosine_ref, f32[128,128]{1,0:T(8,128)S(1)} %get-tuple-element.63.sine_ref, ...), custom_call_target="tpu_custom_call" | custom-call | tf_op jit(solution)/shard_map/turn_queries/pallas_call | solution.py:93
  8.3 3.3 %collective-permute-done.rest_0_ = bf16[1040,128]{1,0:T(8,128)(2,1)S(1)} collective-permute-done((bf16[1040,128]{1,0:T(8,128)(2,1)S(1)}, bf16[1040,128]{1,0:T(8,128)(2,1)S(1)}, u32[]{:S(2)}, u32[]{:S(2)}) %collective-permute-start) | collective-permute-done | bytes 266272 | tf_op jit(solution)/shard_map/ppermute | solution.py:39
  11.6 0.5 %collective-permute-start.1 = (bf16[8,80,128]{2,1,0:T(8,128)(2,1)S(1)}, bf16[8,80,128]{2,1,0:T(8,128)(2,1)S(1)}, u32[]{:S(2)}, u32[]{:S(2)}) collective-permute-start(bf16[8,80,128]{2,1,0:T(8,128)(2,1)S(1)} %get-tuple-element.42), channel_id=1, source_target_pairs={{0,1},{1,0},{2,3},{3,2},{4,5},{5,4},{6,7},{7,6},{8,9},{9,8},{10,11... | collective-permute-start | bytes 491528 | tf_op jit(solution)/shard_map/ppermute | solution.py:43
  12.1 0.1 copy.19.table_ref
  12.2 0.9 %collective-permute-done.1.sibling_ref = bf16[8,80,128]{2,1,0:T(8,128)(2,1)S(1)} collective-permute-done((bf16[8,80,128]{2,1,0:T(8,128)(2,1)S(1)}, bf16[8,80,128]{2,1,0:T(8,128)(2,1)S(1)}, u32[]{:S(2)}, u32[]{:S(2)}) %collective-permute-start.1) | collective-permute-done | bytes 163872 | tf_op jit(solution)/shard_map/ppermute | solution.py:43
  13.1 0.6 %collective-permute-done.3.rest_1_ = bf16[1040,128]{1,0:T(8,128)(2,1)S(1)} collective-permute-done((bf16[1040,128]{1,0:T(8,128)(2,1)S(1)}, bf16[1040,128]{1,0:T(8,128)(2,1)S(1)}, u32[]{:S(2)}, u32[]{:S(2)}) %collective-permute-start.3) | collective-permute-done | bytes 266272 | tf_op jit(solution)/shard_map/ppermute | solution.py:43
  13.7 2.2 %block_weights.1 = (bf16[16,64,1024]{2,1,0:T(8,128)(2,1)S(1)}, f32[16,64,128]{2,1,0:T(8,128)S(1)}) custom-call(s32[16,8]{1,0:T(8,128)S(1)} %fusion.1.slots_ref, bf16[8,64,128]{2,1,0:T(8,128)(2,1)S(1)} %get-tuple-element.44.own_ref, bf16[8,80,128]{2,1,0:T(8,128)(2,1)S(1)} %collective-permute-done.1.sibling_ref, ...), custom_call_target="tpu_custom_call" | custom-call | tf_op jit(solution)/shard_map/block_weights/pallas_call | solution.py:145
  15.9 2.3 %collective-permute-start.4 = (bf16[8,128,128]{2,1,0:T(8,128)(2,1)S(1)}, bf16[8,128,128]{2,1,0:T(8,128)(2,1)S(1)}, u32[]{:S(2)}, u32[]{:S(2)}) collective-permute-start(bf16[8,128,128]{2,1,0:T(8,128)(2,1)S(1)} %collective-permute-done.2.rest_1_), channel_id=1, source_target_pairs={{0,1},{1,0},{2,3},{3,2},{4,5},{5,4},{6,7},{7,6},{8,9},{9,8},{10,11... | collective-permute-start | bytes 786440 | tf_op jit(solution)/shard_map/ppermute | solution.py:43
  18.2 1.2 %collective-permute-done.4.rest_2_ = bf16[8,128,128]{2,1,0:T(8,128)(2,1)S(1)} collective-permute-done((bf16[8,128,128]{2,1,0:T(8,128)(2,1)S(1)}, bf16[8,128,128]{2,1,0:T(8,128)(2,1)S(1)}, u32[]{:S(2)}, u32[]{:S(2)}) %collective-permute-start.4) | collective-permute-done | bytes 262176 | tf_op jit(solution)/shard_map/ppermute | solution.py:43
  19.4 0.9 %block_outputs.1 = (bf16[32,2048]{1,0:T(8,128)(2,1)S(1)}, bf16[32,2048]{1,0:T(8,128)(2,1)S(1)}) custom-call(s32[16,8]{1,0:T(8,128)S(1)} %fusion.1.slots_ref, bf16[16,64,1024]{2,1,0:T(8,128)(2,1)S(1)} %get-tuple-element.48.weights_ref, f32[16,64,128]{2,1,0:T(8,128)S(1)} %get-tuple-element.49.total_ref, bf16[8,128,128]{2,1,0:T(8,128)(2,1)S(1)} %scale_values.1.rest_0_, ...), custom_call_target="tpu_custom_call" | custom-call | tf_op jit(solution)/shard_map/block_outputs/pallas_call | solution.py:185
  20.3 1.6 %collective-permute-start.5 = (bf16[32,2048]{1,0:T(8,128)(2,1)S(1)}, bf16[32,2048]{1,0:T(8,128)(2,1)S(1)}, u32[]{:S(2)}, u32[]{:S(2)}) collective-permute-start(bf16[32,2048]{1,0:T(8,128)(2,1)S(1)} %get-tuple-element.52), channel_id=1, source_target_pairs={{0,2},{1,3},{2,0},{3,1},{4,6},{5,7},{6,4},{7,5},{8,10},{9,11},{10,... | collective-permute-start | bytes 393224 | tf_op jit(solution)/shard_map/ppermute | solution.py:43
  21.9 4.3 %collective-permute-done.5.refs_1_ = bf16[32,2048]{1,0:T(8,128)(2,1)S(1)} collective-permute-done((bf16[32,2048]{1,0:T(8,128)(2,1)S(1)}, bf16[32,2048]{1,0:T(8,128)(2,1)S(1)}, u32[]{:S(2)}, u32[]{:S(2)}) %collective-permute-start.5) | collective-permute-done | bytes 131104 | tf_op jit(solution)/shard_map/ppermute | solution.py:43
  26.2 0.7 %join_pieces.1 = bf16[32,4096]{1,0:T(8,128)(2,1)} custom-call(bf16[32,2048]{1,0:T(8,128)(2,1)S(1)} %get-tuple-element.51.refs_0_, bf16[32,2048]{1,0:T(8,128)(2,1)S(1)} %collective-permute-done.5.refs_1_), custom_call_target="tpu_custom_call" | custom-call | tf_op jit(solution)/shard_map/join_pieces/pallas_call | solution.py:208
  (30 shorter events, 0.3 us)
Async XLA Ops:
  0.0 1.2 %copy-start = (bf16[2,1024,128]{2,1,0:T(8,128)(2,1)S(1)}, bf16[2,1024,128]{2,1,0:T(8,128)(2,1)}, u32[]{:S(2)}) copy-start(bf16[2,1024,128]{2,1,0:T(8,128)(2,1)} %param.9) | copy-start | bytes 1572868
  0.0 7.3 %copy-start.2 = (s32[8,4,8]{2,1,0:T(4,128)S(1)}, s32[8,4,8]{2,1,0:T(4,128)}, u32[]{:S(2)}) copy-start(s32[8,4,8]{2,1,0:T(4,128)} %param.13) | copy-start | bytes 3076
  0.0 7.2 %copy-start.1 = (bf16[128,8,128]{2,1,0:T(8,128)(2,1)S(1)}, bf16[128,8,128]{2,1,0:T(8,128)(2,1)}, u32[]{:S(2)}) copy-start(bf16[128,8,128]{2,1,0:T(8,128)(2,1)} %param.7) | copy-start | bytes 786436
  0.0 7.1 %copy-start.4 = (s32[128]{0:T(128)S(1)}, s32[128]{0:T(128)}, u32[]{:S(2)}) copy-start(s32[128]{0:T(128)} %param.8) | copy-start | bytes 1540
  1.2 10.9 %copy-start.3 = (f32[2,16]{1,0:T(2,128)S(1)}, f32[2,16]{1,0:T(2,128)}, u32[]{:S(2)}) copy-start(f32[2,16]{1,0:T(2,128)} %param.12) | copy-start | bytes 388
  1.2 10.3 %collective-permute-start = (bf16[1040,128]{1,0:T(8,128)(2,1)S(1)}, bf16[1040,128]{1,0:T(8,128)(2,1)S(1)}, u32[]{:S(2)}, u32[]{:S(2)}) collective-permute-start(bf16[1040,128]{1,0:T(8,128)(2,1)S(1)} %pad_maximum_fusion._.codes_ref), channel_id=1, source_target_pairs={{4,0},{13,1},{6,2},{15,3},{0,4},{9,5},{2,6},{11,7},{12,8},{5,9},{1... | collective-permute-start | bytes 798728 | tf_op jit(solution)/shard_map/ppermute | solution.py:39
  7.0 8.9 %collective-permute-start.2 = (bf16[8,128,128]{2,1,0:T(8,128)(2,1)S(1)}, bf16[8,128,128]{2,1,0:T(8,128)(2,1)S(1)}, u32[]{:S(2)}, u32[]{:S(2)}) collective-permute-start(bf16[8,128,128]{2,1,0:T(8,128)(2,1)S(1)} %scale_values.1.rest_0_), channel_id=1, source_target_pairs={{4,0},{13,1},{6,2},{15,3},{0,4},{9,5},{2,6},{11,7},{12,8},{5,9},{1... | collective-permute-start | bytes 786440 | tf_op jit(solution)/shard_map/ppermute | solution.py:39
  11.6 1.6 %collective-permute-start.1 = (bf16[8,80,128]{2,1,0:T(8,128)(2,1)S(1)}, bf16[8,80,128]{2,1,0:T(8,128)(2,1)S(1)}, u32[]{:S(2)}, u32[]{:S(2)}) collective-permute-start(bf16[8,80,128]{2,1,0:T(8,128)(2,1)S(1)} %get-tuple-element.42), channel_id=1, source_target_pairs={{0,1},{1,0},{2,3},{3,2},{4,5},{5,4},{6,7},{7,6},{8,9},{9,8},{10,11... | collective-permute-start | bytes 491528 | tf_op jit(solution)/shard_map/ppermute | solution.py:43
  12.2 1.5 %collective-permute-start.3 = (bf16[1040,128]{1,0:T(8,128)(2,1)S(1)}, bf16[1040,128]{1,0:T(8,128)(2,1)S(1)}, u32[]{:S(2)}, u32[]{:S(2)}) collective-permute-start(bf16[1040,128]{1,0:T(8,128)(2,1)S(1)} %collective-permute-done.rest_0_), channel_id=1, source_target_pairs={{0,1},{1,0},{2,3},{3,2},{4,5},{5,4},{6,7},{7,6},{8,9},{9,8},{10,11... | collective-permute-start | bytes 798728 | tf_op jit(solution)/shard_map/ppermute | solution.py:43
  15.9 3.5 %collective-permute-start.4 = (bf16[8,128,128]{2,1,0:T(8,128)(2,1)S(1)}, bf16[8,128,128]{2,1,0:T(8,128)(2,1)S(1)}, u32[]{:S(2)}, u32[]{:S(2)}) collective-permute-start(bf16[8,128,128]{2,1,0:T(8,128)(2,1)S(1)} %collective-permute-done.2.rest_1_), channel_id=1, source_target_pairs={{0,1},{1,0},{2,3},{3,2},{4,5},{5,4},{6,7},{7,6},{8,9},{9,8},{10,11... | collective-permute-start | bytes 786440 | tf_op jit(solution)/shard_map/ppermute | solution.py:43
  20.3 5.8 %collective-permute-start.5 = (bf16[32,2048]{1,0:T(8,128)(2,1)S(1)}, bf16[32,2048]{1,0:T(8,128)(2,1)S(1)}, u32[]{:S(2)}, u32[]{:S(2)}) collective-permute-start(bf16[32,2048]{1,0:T(8,128)(2,1)S(1)} %get-tuple-element.52), channel_id=1, source_target_pairs={{0,2},{1,3},{2,0},{3,1},{4,6},{5,7},{6,4},{7,5},{8,10},{9,11},{10,... | collective-permute-start | bytes 393224 | tf_op jit(solution)/shard_map/ppermute | solution.py:43

commit v5 on v4

--- a/solution.py
+++ b/solution.py
@@ -43,33 +43,65 @@
     return lax.ppermute(x, "head", [(i, i ^ mask) for i in range(lax.axis_size("head"))])
 
 
-def scale_kernel(scales_ref, codes_ref, _, out_ref, *, row):
-    scales = scales_ref[...]
-    for block in range(out_ref.shape[0]):
-        codes = codes_ref[block * BLOCK : (block + 1) * BLOCK, :].astype(jnp.float32)
-        out_ref[block] = (codes * scales[row, block]).astype(jnp.bfloat16)
-
-
-def scale_blocks(scales, codes, before, row):
-    keys_dev, width = codes.shape
-    return pl.pallas_call(
-        functools.partial(scale_kernel, row=row),
-        in_specs=[in_vmem, in_vmem, pl.BlockSpec(memory_space=pl.ANY)],
-        out_specs=in_vmem,
-        out_shape=jax.ShapeDtypeStruct((keys_dev // BLOCK, BLOCK, width), jnp.bfloat16),
-        compiler_params=granted,
-        name="scale_values",
-    )(scales, codes, before)
-
-
-def scaled_keys(codes_ref, scales, blocks, store, at):
+def begin_kernel(index_hbm, table_hbm, keys_hbm, values_hbm, keys_ref, values_ref, *scratch):
+    index_ref, table_ref, key_codes, value_codes, arrived = scratch
+    groups = index_hbm.shape[1]
+    kv_head = lax.axis_index("head") * groups // lax.axis_size("head")
+    copies = [
+        pltpu.make_async_copy(source, target, arrived.at[n])
+        for n, (source, target) in enumerate(
+            (
+                (index_hbm, index_ref),
+                (table_hbm, table_ref),
+                (keys_hbm.at[kv_head], key_codes),
+                (values_hbm.at[kv_head], value_codes),
+            )
+        )
+    ]
+    for copy in copies:
+        copy.start()
+    for copy in copies[:2]:
+        copy.wait()
+    blocks = keys_ref.shape[0]
+    scales = [
+        [table_ref[row, index_ref[row, kv_head, block]] for block in range(blocks)]
+        for row in range(2)
+    ]
+    copies[2].wait()
     for block in range(blocks):
-        codes = codes_ref[block * BLOCK : (block + 1) * BLOCK, :].astype(jnp.float32)
-        store[at + block] = (codes * scales[0, block]).T.astype(jnp.bfloat16)
-
-
-def turn_kernel(queries_ref, cosine_ref, sine_ref, codes_ref, scales_ref, lists_ref, *outs):
-    own_ref, sibling_ref, keys_ref = outs
+        codes = key_codes[block * BLOCK : (block + 1) * BLOCK, :].astype(jnp.float32)
+        keys_ref[block] = (codes * scales[0][block]).T.astype(jnp.bfloat16)
+    copies[3].wait()
+    for block in range(blocks):
+        codes = value_codes[block * BLOCK : (block + 1) * BLOCK, :].astype(jnp.float32)
+        values_ref[block] = (codes * scales[1][block]).astype(jnp.bfloat16)
+
+
+def begin(scale_index, scale_table, key_codes, value_codes):
+    _, keys_dev, width = key_codes.shape
+    blocks = keys_dev // BLOCK
+    stay = functools.partial(pltpu.with_memory_space_constraint, memory_space=pltpu.HBM)
+    return pl.pallas_call(
+        begin_kernel,
+        in_specs=[pl.BlockSpec(memory_space=pltpu.HBM)] * 4,
+        out_specs=[in_vmem] * 2,
+        out_shape=[
+            pltpu.VMEM((blocks, width, BLOCK), jnp.bfloat16),
+            pltpu.VMEM((blocks, BLOCK, width), jnp.bfloat16),
+        ],
+        scratch_shapes=[
+            pltpu.SMEM(scale_index.shape, scale_index.dtype),
+            pltpu.SMEM(scale_table.shape, scale_table.dtype),
+            pltpu.VMEM((keys_dev, width), key_codes.dtype),
+            pltpu.VMEM((keys_dev, width), value_codes.dtype),
+            pltpu.SemaphoreType.DMA((4,)),
+        ],
+        compiler_params=granted,
+        name="begin",
+    )(stay(scale_index), stay(scale_table), stay(key_codes), stay(value_codes))
+
+
+def turn_kernel(queries_ref, cosine_ref, sine_ref, lists_ref, own_ref, sibling_ref):
     heads_dev, rows, width = own_ref.shape
     cosine = cosine_ref[...]
     sine = sine_ref[...]
@@ -83,42 +115,40 @@
         sibling_ref[head, rows:] = jnp.broadcast_to(
             lists_ref[head : head + 1], sibling_ref[head, rows:].shape
         )
-    scaled_keys(codes_ref, scales_ref[...], keys_ref.shape[0], keys_ref, 0)
-
-
-def turn_queries(queries, cosine, sine, codes, scales, lists):
+
+
+def turn_queries(queries, cosine, sine, lists):
     heads_dev, rows, width = queries.shape
     half = (heads_dev, rows // 2, width)
     more = (heads_dev, rows // 2 + ROW_TILE, width)
     return pl.pallas_call(
         turn_kernel,
-        in_specs=[in_vmem] * 6,
-        out_specs=[in_vmem] * 3,
+        in_specs=[in_vmem] * 4,
+        out_specs=[in_vmem] * 2,
         out_shape=[
             jax.ShapeDtypeStruct(half, jnp.bfloat16),
             jax.ShapeDtypeStruct(more, jnp.bfloat16),
-            jax.ShapeDtypeStruct((scales.shape[1], width, BLOCK), jnp.bfloat16),
         ],
         compiler_params=granted,
         name="turn_queries",
-    )(queries, cosine, sine, codes, scales, lists)
-
-
-def score_kernel(slots_ref, own_ref, sibling_ref, near_ref, table_ref, *rest):
+    )(queries, cosine, sine, lists)
+
+
+def gather_parts(parts, store):
+    at = 0
+    for part in parts:
+        store[at : at + part.shape[0]] = part[...]
+        at += part.shape[0]
+
+
+def score_kernel(slots_ref, own_ref, sibling_ref, _, *rest):
     *parts, weights_ref, total_ref, store = rest
     heads_dev, rows, width = own_ref.shape
     heads = slots_ref.shape[0]
     picks = slots_ref.shape[1]
     slots = slots_ref[...]
     factor = math.log2(math.e) / math.sqrt(width)
-    blocks = near_ref.shape[0]
-    store[:blocks] = near_ref[...]
-    table = table_ref[...]
-    entries = lax.broadcasted_iota(jnp.int32, (table.shape[0], width), 0).astype(jnp.float32)
-    for n, part in enumerate(parts):
-        index = part[blocks * BLOCK :, :].astype(jnp.float32)
-        scales = jnp.sum(jnp.where(index == entries, table, 0.0), axis=0, keepdims=True)
-        scaled_keys(part, scales, blocks, store, (n + 1) * blocks)
+    gather_parts(parts, store)
     for head in range(heads):
         turned = (own_ref if head < heads_dev else sibling_ref)[head % heads_dev, :rows]
         scores = [
@@ -138,13 +168,13 @@
         total_ref[head] = jnp.broadcast_to(total, (rows, width))
 
 
-def block_weights(slots, own, sibling, near, table, parts):
+def block_weights(slots, own, sibling, extra, parts):
     _, rows, width = own.shape
     heads, picks = slots.shape
-    blocks = near.shape[0] * (1 + len(parts))
+    blocks = sum(part.shape[0] for part in parts)
     return pl.pallas_call(
         score_kernel,
-        in_specs=[in_vmem] * (5 + len(parts)),
+        in_specs=[in_vmem] * (4 + len(parts)),
         out_specs=[in_vmem, in_vmem],
         out_shape=[
             jax.ShapeDtypeStruct((heads, rows, picks * BLOCK), jnp.bfloat16),
@@ -153,7 +183,7 @@
         scratch_shapes=[pltpu.VMEM((blocks, width, BLOCK), jnp.bfloat16)],
         compiler_params=granted,
         name="block_weights",
-    )(slots, own, sibling, near, table, *parts)
+    )(slots, own, sibling, extra, *parts)
 
 
 def value_kernel(slots_ref, weights_ref, total_ref, *rest, inputs):
@@ -164,10 +194,7 @@
     picks = slots_ref.shape[1]
     rows = pieces[0].shape[0]
     slots = slots_ref[...]
-    at = 0
-    for part in parts:
-        store[at : at + part.shape[0]] = part[...]
-        at += part.shape[0]
+    gather_parts(parts, store)
     for head in range(heads):
         picked = jnp.concatenate([store[slots[head, i]] for i in range(picks)], axis=0)
         out = jnp.dot(weights_ref[head], picked, preferred_element_type=jnp.float32)
@@ -229,34 +256,13 @@
     core = head_place % share
     group = head_place // share
     groups = head_count // share
-    kv_head = head_place * heads_dev // GROUP
-
-    index_rows = lax.dynamic_index_in_dim(scale_index, kv_head, 1, keepdims=False)
-    entries = scale_table.shape[1]
-    labels = jnp.pad(
-        jnp.broadcast_to(index_rows[0].astype(jnp.bfloat16), (entries, key_blocks)),
-        ((0, 0), (0, head_width - key_blocks)),
-    )
-    labels, key_codes = lax.optimization_barrier((labels, key_codes))
-    key_rows = lax.dynamic_index_in_dim(key_codes, kv_head, 0, keepdims=False)
-    near_keys = jnp.concatenate([key_rows, labels], axis=0)
-    near_keys, queries, positions, value_codes, scale_index, scale_table, block_lists = (
-        lax.optimization_barrier(
-            (near_keys, queries, positions, value_codes, scale_index, scale_table, block_lists)
-        )
-    )
-    index_rows = lax.dynamic_index_in_dim(scale_index, kv_head, 1, keepdims=False)
-    far_keys = near_keys
+
+    keys, values = begin(scale_index, scale_table, key_codes, value_codes)
+    far_keys = keys
     key_parts = []
     for _ in range(reach_hops):
         far_keys = sent(far_keys, share, pairs)
         key_parts.append(far_keys)
-
-    value_rows = lax.dynamic_index_in_dim(value_codes, kv_head, 0, keepdims=False)
-    matches = index_rows[:, :, None] == jnp.arange(entries, dtype=jnp.int32)
-    scales = jnp.sum(jnp.where(matches, scale_table[:, None, :], 0.0), axis=2)
-
-    values = scale_blocks(scales, value_rows, near_keys, 1)
     values, queries, positions, block_lists = lax.optimization_barrier(
         (values, queries, positions, block_lists)
     )
@@ -284,11 +290,11 @@
 
     picks = own_lists.shape[1]
     carried = jnp.pad(own_lists.astype(jnp.bfloat16), ((0, 0), (0, head_width - picks)))
-    own, sibling, near = turn_queries(
-        jnp.transpose(ordered(queries), (1, 0, 2)), cosine, sine, near_keys, scales, carried
+    own, sibling = turn_queries(
+        jnp.transpose(ordered(queries), (1, 0, 2)), cosine, sine, carried
     )
     sibling, key_parts[0] = lax.optimization_barrier((sibling, key_parts[0]))
-    key_parts = [part for far in key_parts for part in (far, swapped(far, 1))]
+    key_parts = [keys] + [part for far in key_parts for part in (far, swapped(far, 1))]
     sibling = swapped(sibling, 1)
     sibling_lists = sibling[:, rows_dev // share, :picks].astype(jnp.int32)
     lists = jnp.concatenate([own_lists, sibling_lists], axis=0)
@@ -305,7 +311,7 @@
         far_values = sent(far_values, share, pairs)
         value_steps.append(far_values)
     weights, total = block_weights(
-        slots, own, sibling, near, scale_table[0][:, None], key_parts
+        slots, own, sibling, scale_table[0][:, None], key_parts
     )
 
     *value_steps, weights = lax.optimization_barrier((*value_steps, weights))

time: 27.1 us -> 26.3 us (0.970)
  waiting for transfers between devices: 10.2 us -> 13.3 us
  starting transfers between devices: 7.59 us -> 5.68 us
  other arithmetic: 2.03 us -> 0.42 us
  local copies, waits for them, and re-layouts: 2.41 us -> 1.94 us
    ppermute x2, waiting for transfers between devices: 3.26 us -> 6.49 us  [sent(): return lax.ppermute(x, ('ctx', 'head'), moves)]
    ppermute x4, starting transfers between devices: 4.42 us -> 2.51 us  [swapped(): lax.ppermute(x, 'head', [(i, i ^ mask) for i in range(lax.axis_size('head...]
    squeeze x2 -> x0, local copies, waits for them, and re-layouts: 0.98 us -> none  [the longest x1 0.97 us: on_device(): lax.dynamic_index_in_dim(value_codes, kv_head, 0, keepdims=False)]
    dynamic_slice x2, local copies, waits for them, and re-layouts: 0.04 us -> 0.97 us  [ordered(): lax.dynamic_slice(cut, (jnp.bitwise_xor(group, n), jnp.bitwise_xor(core,...]
    reduce_sum x1 -> x0, other arithmetic: 0.83 us -> none  [on_device(): scales = jnp.sum(jnp.where(matches, scale_table[:, None, :], 0.0), axis=2)]
    convert_element_type x1 -> x0, other arithmetic: 0.76 us -> none  [on_device(): index_rows[0].astype(jnp.bfloat16)]
    dynamic_slice x1 -> x0, local copies, waits for them, and re-layouts: 0.69 us -> none  [on_device(): lax.dynamic_index_in_dim(scale_index, kv_head, 1, keepdims=False)]
    reshape x1, local copies, waits for them, and re-layouts: 0.08 us -> 0.74 us  [ordered(): cut = x.reshape((groups, share, rows_dev // head_count) + x.shape[1:])]
  transfers between devices with their start and end apart: 6 -> 6, of which waited for: 5 -> 6; matrix products, arithmetic and copies ran while one was open for 12% -> 9% of each run, Pallas kernels for 10% -> 7%
where the time goes in v5:
time: 26.3 us; the launch traced here: 26.1 us
  waiting for transfers between devices  13.3 us (51%)
  starting transfers between devices  5.68 us (22%)
  Pallas kernels  4.64 us (18%)
  local copies, waits for them, and re-layouts  1.94 us (7%)
  other arithmetic  0.42 us (2%)
    ppermute x4, waiting for transfers between devices, swapped(): lax.ppermute(x, 'head', [(i, i ^ mask) for i in range(lax.axis_size('head...  6.77 us
    ppermute x2, waiting for transfers between devices, sent(): return lax.ppermute(x, ('ctx', 'head'), moves)  6.49 us
    ppermute x2, starting transfers between devices, sent(): return lax.ppermute(x, ('ctx', 'head'), moves)  3.17 us
    ppermute x4, starting transfers between devices, swapped(): lax.ppermute(x, 'head', [(i, i ^ mask) for i in range(lax.axis_size('head...  2.51 us
    pallas_call x1, Pallas kernels, block_weights(): pl.pallas_call(score_kernel, in_specs=[in_vmem] * (4 + len(parts)), out_s...  1.57 us
    pallas_call x1, Pallas kernels, begin(): pl.pallas_call(begin_kernel, in_specs=[pl.BlockSpec(memory_space=pltpu.HB...  1.2 us
    dynamic_slice x2, local copies, waits for them, and re-layouts, ordered(): lax.dynamic_slice(cut, (jnp.bitwise_xor(group, n), jnp.bitwise_xor(core,...  0.97 us
    pallas_call x1, Pallas kernels, block_outputs(): pl.pallas_call(functools.partial(value_kernel, inputs=len(parts)), in_spe...  0.93 us
  transfers between devices with their start and end apart: 6, of which 6 were waited for; matrix products, arithmetic and copies ran while one was open for 9% of the time, Pallas kernels for 7%

profile of v5, /device:TPU:0, one launch (start us, length us, event | category | flops | bytes accessed | tf_op | source)
XLA Modules:
  0.0 26.1 jit_solution(17590230052152988159)
XLA Ops:
  0.0 1.2 %begin.1 = (bf16[8,128,128]{2,1,0:T(8,128)(2,1)S(1)}, bf16[8,128,128]{2,1,0:T(8,128)(2,1)S(1)}) custom-call(s32[2,2,8]{2,1,0:T(2,128)} %index_hbm.1, f32[2,16]{1,0:T(2,128)} %table_hbm.1, bf16[2,1024,128]{2,1,0:T(8,128)(2,1)} %keys_hbm.1, bf16[2,1024,128]{2,1,0:T(8,128)(2,1)} %values_hbm.1), custom_call_target="tpu_custom_call" | custom-call | tf_op jit(solution)/shard_map/begin/pallas_call | solution.py:84
  1.2 3.1 %collective-permute-start = (bf16[8,128,128]{2,1,0:T(8,128)(2,1)S(1)}, bf16[8,128,128]{2,1,0:T(8,128)(2,1)S(1)}, u32[]{:S(2)}, u32[]{:S(2)}) collective-permute-start(bf16[8,128,128]{2,1,0:T(8,128)(2,1)S(1)} %get-tuple-element.26.rest_0_), channel_id=1, source_target_pairs={{4,0},{13,1},{6,2},{15,3},{0,4},{9,5},{2,6},{11,7},{12,8},{5,9},{1... | collective-permute-start | bytes 786440 | tf_op jit(solution)/shard_map/ppermute | solution.py:39
  4.3 0.1 collective-permute-start.2
  4.4 0.7 %reshape.47 = s32[2,2,32]{2,1,0:T(2,128)S(1)} reshape(s32[128]{0:T(128)} %param.8) | data formatting | bytes 1024 | tf_op jit(solution)/shard_map/reshape | solution.py:271
  5.1 1.0 %constant_dynamic-slice_fusion.7 = (bf16[1,1,32,8,128]{4,3,2,1,0:T(8,128)(2,1)S(1)}, bf16[1,1,32,8,128]{4,3,2,1,0:T(8,128)(2,1)S(1)}, bf16[1,1,32,8,128]{4,3,2,1,0:T(8,128)(2,1)S(1)}, bf16[1,1,32,8,128]{4,3,2,1,0:T(8,128)(2,1)S(1)}) fusion(bf16[2,2,32,8,128]{4,3,2,1,0:T(8,128)(2,1)} %bitcast.11, s32[]{:T(128)S(6)} %select_n.98, s32[]{:T(128)S(6)} %select_n.100, ...), kind=kLoop, calls=%fused_computation.34 | loop fusion | bytes 524304 | tf_op jit(solution)/shard_map/dynamic_slice | solution.py:273
  6.2 0.0 copy-done
  6.3 0.1 convert_element_type.29
  6.4 0.3 %fusion = (f32[128,128]{1,0:T(8,128)S(1)}, f32[128,128]{1,0:T(8,128)S(1)}) fusion(f32[128]{0:T(128)S(1)} %get-tuple-element.49, f32[128]{0:T(128)S(1)} %get-tuple-element.50, f32[128]{0:T(128)S(1)} %convert_element_type.29), kind=kLoop, calls=%fused_computation.3 | loop fusion | flops 32768 | bytes 132608 | tf_op jit(solution)/shard_map/mul | solution.py:289
  6.7 0.2 turn_queries.1
  6.9 4.6 %collective-permute-done.rest_1_ = bf16[8,128,128]{2,1,0:T(8,128)(2,1)S(1)} collective-permute-done((bf16[8,128,128]{2,1,0:T(8,128)(2,1)S(1)}, bf16[8,128,128]{2,1,0:T(8,128)(2,1)S(1)}, u32[]{:S(2)}, u32[]{:S(2)}) %collective-permute-start) | collective-permute-done | bytes 262176 | tf_op jit(solution)/shard_map/ppermute | solution.py:39
  11.5 0.5 %collective-permute-start.1 = (bf16[8,80,128]{2,1,0:T(8,128)(2,1)S(1)}, bf16[8,80,128]{2,1,0:T(8,128)(2,1)S(1)}, u32[]{:S(2)}, u32[]{:S(2)}) collective-permute-start(bf16[8,80,128]{2,1,0:T(8,128)(2,1)S(1)} %get-tuple-element.27), channel_id=1, source_target_pairs={{0,1},{1,0},{2,3},{3,2},{4,5},{5,4},{6,7},{7,6},{8,9},{9,8},{10,11... | collective-permute-start | bytes 491528 | tf_op jit(solution)/shard_map/ppermute | solution.py:43
  12.0 0.0 copy-done.1
  12.0 0.1 copy.13._
  12.1 0.1 collective-permute-start.3
  12.1 0.9 %collective-permute-done.1.sibling_ref = bf16[8,80,128]{2,1,0:T(8,128)(2,1)S(1)} collective-permute-done((bf16[8,80,128]{2,1,0:T(8,128)(2,1)S(1)}, bf16[8,80,128]{2,1,0:T(8,128)(2,1)S(1)}, u32[]{:S(2)}, u32[]{:S(2)}) %collective-permute-start.1) | collective-permute-done | bytes 163872 | tf_op jit(solution)/shard_map/ppermute | solution.py:43
  13.1 0.6 %collective-permute-done.3.rest_2_ = bf16[8,128,128]{2,1,0:T(8,128)(2,1)S(1)} collective-permute-done((bf16[8,128,128]{2,1,0:T(8,128)(2,1)S(1)}, bf16[8,128,128]{2,1,0:T(8,128)(2,1)S(1)}, u32[]{:S(2)}, u32[]{:S(2)}) %collective-permute-start.3) | collective-permute-done | bytes 262176 | tf_op jit(solution)/shard_map/ppermute | solution.py:43
  13.6 1.6 %block_weights.1 = (bf16[16,64,1024]{2,1,0:T(8,128)(2,1)S(1)}, f32[16,64,128]{2,1,0:T(8,128)S(1)}) custom-call(s32[16,8]{1,0:T(8,128)S(1)} %fusion.1.slots_ref, bf16[8,64,128]{2,1,0:T(8,128)(2,1)S(1)} %get-tuple-element.29.own_ref, bf16[8,80,128]{2,1,0:T(8,128)(2,1)S(1)} %collective-permute-done.1.sibling_ref, f32[16,1]{1,0:T(8,128)S(1)} %copy.13._, ...), custom_call_target="tpu_custom_call" | custom-call | tf_op jit(solution)/shard_map/block_weights/pallas_call | solution.py:175
  15.2 1.9 %collective-permute-done.2.rest_1_ = bf16[8,128,128]{2,1,0:T(8,128)(2,1)S(1)} collective-permute-done((bf16[8,128,128]{2,1,0:T(8,128)(2,1)S(1)}, bf16[8,128,128]{2,1,0:T(8,128)(2,1)S(1)}, u32[]{:S(2)}, u32[]{:S(2)}) %collective-permute-start.2) | collective-permute-done | bytes 262176 | tf_op jit(solution)/shard_map/ppermute | solution.py:39
  17.1 0.0 collective-permute-start.4
  17.1 1.5 %collective-permute-done.4.rest_2_ = bf16[8,128,128]{2,1,0:T(8,128)(2,1)S(1)} collective-permute-done((bf16[8,128,128]{2,1,0:T(8,128)(2,1)S(1)}, bf16[8,128,128]{2,1,0:T(8,128)(2,1)S(1)}, u32[]{:S(2)}, u32[]{:S(2)}) %collective-permute-start.4) | collective-permute-done | bytes 262176 | tf_op jit(solution)/shard_map/ppermute | solution.py:43
  18.6 0.9 %block_outputs.1 = (bf16[32,2048]{1,0:T(8,128)(2,1)S(1)}, bf16[32,2048]{1,0:T(8,128)(2,1)S(1)}) custom-call(s32[16,8]{1,0:T(8,128)S(1)} %fusion.1.slots_ref, bf16[16,64,1024]{2,1,0:T(8,128)(2,1)S(1)} %get-tuple-element.32.weights_ref, f32[16,64,128]{2,1,0:T(8,128)S(1)} %get-tuple-element.33.total_ref, bf16[8,128,128]{2,1,0:T(8,128)(2,1)S(1)} %get-tuple-element.28.rest_0_, ...), custom_call_target="tpu_custom_call" | custom-call | tf_op jit(solution)/shard_map/block_outputs/pallas_call | solution.py:212
  19.5 2.0 %collective-permute-start.5 = (bf16[32,2048]{1,0:T(8,128)(2,1)S(1)}, bf16[32,2048]{1,0:T(8,128)(2,1)S(1)}, u32[]{:S(2)}, u32[]{:S(2)}) collective-permute-start(bf16[32,2048]{1,0:T(8,128)(2,1)S(1)} %get-tuple-element.36), channel_id=1, source_target_pairs={{0,2},{1,3},{2,0},{3,1},{4,6},{5,7},{6,4},{7,5},{8,10},{9,11},{10,... | collective-permute-start | bytes 393224 | tf_op jit(solution)/shard_map/ppermute | solution.py:43
  21.5 3.8 %collective-permute-done.5.refs_1_ = bf16[32,2048]{1,0:T(8,128)(2,1)S(1)} collective-permute-done((bf16[32,2048]{1,0:T(8,128)(2,1)S(1)}, bf16[32,2048]{1,0:T(8,128)(2,1)S(1)}, u32[]{:S(2)}, u32[]{:S(2)}) %collective-permute-start.5) | collective-permute-done | bytes 131104 | tf_op jit(solution)/shard_map/ppermute | solution.py:43
  25.3 0.7 %join_pieces.1 = bf16[32,4096]{1,0:T(8,128)(2,1)} custom-call(bf16[32,2048]{1,0:T(8,128)(2,1)S(1)} %get-tuple-element.35.refs_0_, bf16[32,2048]{1,0:T(8,128)(2,1)S(1)} %collective-permute-done.5.refs_1_), custom_call_target="tpu_custom_call" | custom-call | tf_op jit(solution)/shard_map/join_pieces/pallas_call | solution.py:235
  (16 shorter events, 0.2 us)
Async XLA Ops:
  0.0 12.0 %copy-start.1 = (f32[2,16]{1,0:T(2,128)S(1)}, f32[2,16]{1,0:T(2,128)}, u32[]{:S(2)}) copy-start(f32[2,16]{1,0:T(2,128)} %table_hbm.1) | copy-start | bytes 388
  0.0 6.2 %copy-start = (s32[8,4,8]{2,1,0:T(4,128)S(1)}, s32[8,4,8]{2,1,0:T(4,128)}, u32[]{:S(2)}) copy-start(s32[8,4,8]{2,1,0:T(4,128)} %param.13) | copy-start | bytes 3076
  1.2 10.3 %collective-permute-start = (bf16[8,128,128]{2,1,0:T(8,128)(2,1)S(1)}, bf16[8,128,128]{2,1,0:T(8,128)(2,1)S(1)}, u32[]{:S(2)}, u32[]{:S(2)}) collective-permute-start(bf16[8,128,128]{2,1,0:T(8,128)(2,1)S(1)} %get-tuple-element.26.rest_0_), channel_id=1, source_target_pairs={{4,0},{13,1},{6,2},{15,3},{0,4},{9,5},{2,6},{11,7},{12,8},{5,9},{1... | collective-permute-start | bytes 786440 | tf_op jit(solution)/shard_map/ppermute | solution.py:39
  4.3 12.8 %collective-permute-start.2 = (bf16[8,128,128]{2,1,0:T(8,128)(2,1)S(1)}, bf16[8,128,128]{2,1,0:T(8,128)(2,1)S(1)}, u32[]{:S(2)}, u32[]{:S(2)}) collective-permute-start(bf16[8,128,128]{2,1,0:T(8,128)(2,1)S(1)} %get-tuple-element.28.rest_0_), channel_id=1, source_target_pairs={{4,0},{13,1},{6,2},{15,3},{0,4},{9,5},{2,6},{11,7},{12,8},{5,9},{1... | collective-permute-start | bytes 786440 | tf_op jit(solution)/shard_map/ppermute | solution.py:39
  11.5 1.5 %collective-permute-start.1 = (bf16[8,80,128]{2,1,0:T(8,128)(2,1)S(1)}, bf16[8,80,128]{2,1,0:T(8,128)(2,1)S(1)}, u32[]{:S(2)}, u32[]{:S(2)}) collective-permute-start(bf16[8,80,128]{2,1,0:T(8,128)(2,1)S(1)} %get-tuple-element.27), channel_id=1, source_target_pairs={{0,1},{1,0},{2,3},{3,2},{4,5},{5,4},{6,7},{7,6},{8,9},{9,8},{10,11... | collective-permute-start | bytes 491528 | tf_op jit(solution)/shard_map/ppermute | solution.py:43
  12.1 1.5 %collective-permute-start.3 = (bf16[8,128,128]{2,1,0:T(8,128)(2,1)S(1)}, bf16[8,128,128]{2,1,0:T(8,128)(2,1)S(1)}, u32[]{:S(2)}, u32[]{:S(2)}) collective-permute-start(bf16[8,128,128]{2,1,0:T(8,128)(2,1)S(1)} %collective-permute-done.rest_1_), channel_id=1, source_target_pairs={{0,1},{1,0},{2,3},{3,2},{4,5},{5,4},{6,7},{7,6},{8,9},{9,8},{10,11... | collective-permute-start | bytes 786440 | tf_op jit(solution)/shard_map/ppermute | solution.py:43
  17.1 1.5 %collective-permute-start.4 = (bf16[8,128,128]{2,1,0:T(8,128)(2,1)S(1)}, bf16[8,128,128]{2,1,0:T(8,128)(2,1)S(1)}, u32[]{:S(2)}, u32[]{:S(2)}) collective-permute-start(bf16[8,128,128]{2,1,0:T(8,128)(2,1)S(1)} %collective-permute-done.2.rest_1_), channel_id=1, source_target_pairs={{0,1},{1,0},{2,3},{3,2},{4,5},{5,4},{6,7},{7,6},{8,9},{9,8},{10,11... | collective-permute-start | bytes 786440 | tf_op jit(solution)/shard_map/ppermute | solution.py:43
  19.5 5.8 %collective-permute-start.5 = (bf16[32,2048]{1,0:T(8,128)(2,1)S(1)}, bf16[32,2048]{1,0:T(8,128)(2,1)S(1)}, u32[]{:S(2)}, u32[]{:S(2)}) collective-permute-start(bf16[32,2048]{1,0:T(8,128)(2,1)S(1)} %get-tuple-element.36), channel_id=1, source_target_pairs={{0,2},{1,3},{2,0},{3,1},{4,6},{5,7},{6,4},{7,5},{8,10},{9,11},{10,... | collective-permute-start | bytes 393224 | tf_op jit(solution)/shard_map/ppermute | solution.py:43

commit v6 on v5

--- a/solution.py
+++ b/solution.py
@@ -43,8 +43,12 @@
     return lax.ppermute(x, "head", [(i, i ^ mask) for i in range(lax.axis_size("head"))])
 
 
-def begin_kernel(index_hbm, table_hbm, keys_hbm, values_hbm, keys_ref, values_ref, *scratch):
-    index_ref, table_ref, key_codes, value_codes, arrived = scratch
+def lower_half(shape):
+    return lax.broadcasted_iota(jnp.int32, shape, 1) < shape[1] // 2
+
+
+def begin_kernel(index_hbm, table_hbm, keys_hbm, values_hbm, keys_ref, *rest):
+    first_ref, second_ref, index_ref, table_ref, key_codes, value_codes, arrived = rest
     groups = index_hbm.shape[1]
     kv_head = lax.axis_index("head") * groups // lax.axis_size("head")
     copies = [
@@ -72,9 +76,19 @@
         codes = key_codes[block * BLOCK : (block + 1) * BLOCK, :].astype(jnp.float32)
         keys_ref[block] = (codes * scales[0][block]).T.astype(jnp.bfloat16)
     copies[3].wait()
-    for block in range(blocks):
-        codes = value_codes[block * BLOCK : (block + 1) * BLOCK, :].astype(jnp.float32)
-        values_ref[block] = (codes * scales[1][block]).astype(jnp.bfloat16)
+    pairs = first_ref.shape[0]
+    width = value_codes.shape[1]
+    low = lower_half((BLOCK, width))
+    for pair in range(pairs):
+        left, right = (
+            value_codes[block * BLOCK : (block + 1) * BLOCK, :].astype(jnp.float32)
+            * scales[1][block]
+            for block in (pair, pair + pairs)
+        )
+        first = jnp.where(low, left, pltpu.roll(right, width // 2, 1))
+        second = jnp.where(low, pltpu.roll(left, width // 2, 1), right)
+        first_ref[pair] = first.astype(jnp.bfloat16)
+        second_ref[pair] = second.astype(jnp.bfloat16)
 
 
 def begin(scale_index, scale_table, key_codes, value_codes):
@@ -84,10 +98,11 @@
     return pl.pallas_call(
         begin_kernel,
         in_specs=[pl.BlockSpec(memory_space=pltpu.HBM)] * 4,
-        out_specs=[in_vmem] * 2,
+        out_specs=[in_vmem] * 3,
         out_shape=[
             pltpu.VMEM((blocks, width, BLOCK), jnp.bfloat16),
-            pltpu.VMEM((blocks, BLOCK, width), jnp.bfloat16),
+            pltpu.VMEM((blocks // 2, BLOCK, width), jnp.bfloat16),
+            pltpu.VMEM((blocks // 2, BLOCK, width), jnp.bfloat16),
         ],
         scratch_shapes=[
             pltpu.SMEM(scale_index.shape, scale_index.dtype),
@@ -141,16 +156,16 @@
         at += part.shape[0]
 
 
-def score_kernel(slots_ref, own_ref, sibling_ref, _, *rest):
-    *parts, weights_ref, total_ref, store = rest
-    heads_dev, rows, width = own_ref.shape
-    heads = slots_ref.shape[0]
+def score_kernel(slots_ref, queries_ref, *rest, inputs):
+    parts = rest[:inputs]
+    weights_ref, total_ref, store = rest[-3:]
+    heads, rows, width = total_ref.shape
     picks = slots_ref.shape[1]
     slots = slots_ref[...]
     factor = math.log2(math.e) / math.sqrt(width)
     gather_parts(parts, store)
     for head in range(heads):
-        turned = (own_ref if head < heads_dev else sibling_ref)[head % heads_dev, :rows]
+        turned = queries_ref[head, :rows]
         scores = [
             jnp.dot(turned, store[slots[head, i]], preferred_element_type=jnp.float32)
             for i in range(picks)
@@ -165,16 +180,16 @@
             total = total + weight
             weights_ref[head, :, i * BLOCK : (i + 1) * BLOCK] = weight.astype(jnp.bfloat16)
         total = jnp.sum(total, axis=1, keepdims=True)
-        total_ref[head] = jnp.broadcast_to(total, (rows, width))
-
-
-def block_weights(slots, own, sibling, extra, parts):
-    _, rows, width = own.shape
+        total_ref[head] = jnp.broadcast_to(1.0 / total, (rows, width))
+
+
+def block_weights(slots, queries, parts, rows, *extra):
+    width = queries.shape[2]
     heads, picks = slots.shape
     blocks = sum(part.shape[0] for part in parts)
     return pl.pallas_call(
-        score_kernel,
-        in_specs=[in_vmem] * (4 + len(parts)),
+        functools.partial(score_kernel, inputs=len(parts)),
+        in_specs=[in_vmem] * (2 + len(parts) + len(extra)),
         out_specs=[in_vmem, in_vmem],
         out_shape=[
             jax.ShapeDtypeStruct((heads, rows, picks * BLOCK), jnp.bfloat16),
@@ -183,60 +198,98 @@
         scratch_shapes=[pltpu.VMEM((blocks, width, BLOCK), jnp.bfloat16)],
         compiler_params=granted,
         name="block_weights",
-    )(slots, own, sibling, extra, *parts)
-
-
-def value_kernel(slots_ref, weights_ref, total_ref, *rest, inputs):
-    parts = rest[:inputs]
-    pieces = rest[inputs:-1]
+    )(slots, queries, *parts, *extra)
+
+
+def value_kernel(slots_ref, *rest, inputs, flip, first, last):
+    weights = rest[:2]
+    totals = rest[2:4]
+    parts = rest[4 : 4 + inputs]
+    pieces = rest[4 + inputs : -1]
     store = rest[-1]
-    heads, _, width = total_ref.shape
-    picks = slots_ref.shape[1]
+    heads_dev, _, width = totals[0].shape
+    heads, picks = slots_ref.shape
     rows = pieces[0].shape[0]
     slots = slots_ref[...]
-    gather_parts(parts, store)
-    for head in range(heads):
-        picked = jnp.concatenate([store[slots[head, i]] for i in range(picks)], axis=0)
-        out = jnp.dot(weights_ref[head], picked, preferred_element_type=jnp.float32)
-        out = out / total_ref[head]
+    half = store.shape[0] // 2
+    at = 0
+    for part in parts:
+        for pair in range(part.shape[0]):
+            block = part[pair]
+            store[at] = block
+            turned = pltpu.roll(block.astype(jnp.float32), width // 2, 1)
+            store[half + at] = turned.astype(jnp.bfloat16)
+            at += 1
+    low = lower_half((last - first, width))
+    for pair in range(heads // 2):
+        both = []
+        for head in (2 * pair, 2 * pair + 1):
+            picked = jnp.concatenate([store[slots[head, i]] for i in range(picks)], axis=0)
+            owner, place = divmod(head, heads_dev)
+            weight = weights[owner][place, first:last]
+            out = jnp.dot(weight, picked, preferred_element_type=jnp.float32)
+            both.append(out * totals[owner][place, first:last])
+        out = jnp.where(low, both[flip], both[1 - flip])
         for n, piece in enumerate(pieces):
-            piece[:, head * width : (head + 1) * width] = out[n * rows : (n + 1) * rows].astype(
+            piece[:, pair * width : (pair + 1) * width] = out[n * rows : (n + 1) * rows].astype(
                 jnp.bfloat16
             )
 
 
-def block_outputs(slots, weights, total, parts, pieces):
-    heads, rows, width = total.shape
-    blocks = sum(part.shape[0] for part in parts)
-    piece = jax.ShapeDtypeStruct((rows // pieces, heads * width), jnp.bfloat16)
+def block_outputs(slots, weights, totals, parts, pieces, flip, first, last):
+    heads = slots.shape[0]
+    _, rows, width = totals[0].shape
+    pairs = sum(part.shape[0] for part in parts)
+    rows //= pieces
+    pieces = last - first
+    piece = jax.ShapeDtypeStruct((rows, heads // 2 * width), jnp.bfloat16)
     return pl.pallas_call(
-        functools.partial(value_kernel, inputs=len(parts)),
-        in_specs=[in_vmem] * (3 + len(parts)),
+        functools.partial(
+            value_kernel,
+            inputs=len(parts),
+            flip=flip,
+            first=first * rows,
+            last=last * rows,
+        ),
+        in_specs=[in_vmem] * (5 + len(parts)),
         out_specs=[in_vmem] * pieces,
         out_shape=[piece] * pieces,
-        scratch_shapes=[pltpu.VMEM((blocks, BLOCK, width), jnp.bfloat16)],
+        scratch_shapes=[pltpu.VMEM((2 * pairs, BLOCK, width), jnp.bfloat16)],
         compiler_params=granted,
         name="block_outputs",
-    )(slots, weights, total, *parts)
-
-
-def join_kernel(*refs, share):
+    )(slots, *weights, *totals, *parts)
+
+
+def join_kernel(*refs, share, width):
     *pieces, out_ref = refs
     place = lax.axis_index("head")
-    width = pieces[0].shape[1] // share
-    for n, piece in enumerate(pieces):
+    chips = len(pieces) // 2
+    rows = out_ref.shape[0]
+    pairs = pieces[0].shape[1] // width // share
+    low = lower_half((rows, width))
+    for n in range(chips):
         for part in range(share):
-            column = pl.multiple_of(jnp.bitwise_xor(place, n * share + part) * width, width)
-            out_ref[:, pl.ds(column, width)] = piece[:, part * width : (part + 1) * width]
-
-
-def join_pieces(pieces, share):
-    rows, width = pieces[0].shape
+            column = jnp.bitwise_xor(place, n * share + part) * (2 * pairs * width)
+            for pair in range(pairs):
+                at = (part * pairs + pair) * width
+                first, second = (
+                    piece[:, at : at + width].astype(jnp.float32)
+                    for piece in (pieces[n], pieces[chips + n])
+                )
+                even = jnp.where(low, first, second)
+                odd = pltpu.roll(jnp.where(low, second, first), width // 2, 1)
+                for m, out in enumerate((even, odd)):
+                    to = pl.multiple_of(column + (2 * pair + m) * width, width)
+                    out_ref[:, pl.ds(to, width)] = out.astype(jnp.bfloat16)
+
+
+def join_pieces(pieces, share, width):
+    rows, across = pieces[0].shape
     return pl.pallas_call(
-        functools.partial(join_kernel, share=share),
+        functools.partial(join_kernel, share=share, width=width),
         in_specs=[in_vmem] * len(pieces),
         out_specs=in_vmem,
-        out_shape=jax.ShapeDtypeStruct((rows, width * len(pieces)), jnp.bfloat16),
+        out_shape=jax.ShapeDtypeStruct((rows, across * len(pieces)), jnp.bfloat16),
         compiler_params=granted,
         name="join_pieces",
     )(*pieces)
@@ -257,14 +310,14 @@
     group = head_place // share
     groups = head_count // share
 
-    keys, values = begin(scale_index, scale_table, key_codes, value_codes)
+    keys, *values = begin(scale_index, scale_table, key_codes, value_codes)
     far_keys = keys
     key_parts = []
     for _ in range(reach_hops):
         far_keys = sent(far_keys, share, pairs)
         key_parts.append(far_keys)
-    values, queries, positions, block_lists = lax.optimization_barrier(
-        (values, queries, positions, block_lists)
+    *values, queries, positions, block_lists = lax.optimization_barrier(
+        (*values, queries, positions, block_lists)
     )
     own_lists = lax.dynamic_index_in_dim(block_lists, cycle_place, 1, keepdims=False)
     def ordered(x):
@@ -305,22 +358,48 @@
     place = 2 * hops - jnp.where(above == from_above, 1, 0)
     slots = lists % key_blocks + key_blocks * jnp.where(offset == 0, 0, place)
 
-    value_steps = []
+    steps = []
     far_values = values
     for _ in range(reach_hops):
-        far_values = sent(far_values, share, pairs)
-        value_steps.append(far_values)
-    weights, total = block_weights(
-        slots, own, sibling, scale_table[0][:, None], key_parts
-    )
-
-    *value_steps, weights = lax.optimization_barrier((*value_steps, weights))
-    value_parts = [values]
-    for step in value_steps:
-        value_parts += [step, swapped(step, 1)]
-    pieces = block_outputs(slots, weights, total, value_parts, groups)
-    moved = [pieces[0]] + [swapped(pieces[n], n * share) for n in range(1, groups)]
-    return join_pieces(moved, share)
+        far_values = [sent(half, share, pairs) for half in far_values]
+        steps.append(far_values)
+    rows = rows_dev // share
+    own_weights, own_total = block_weights(slots[:heads_dev], own, key_parts, rows)
+    sibling_weights, sibling_total = block_weights(slots[heads_dev:], sibling, key_parts, rows)
+    weights = (own_weights, sibling_weights)
+    totals = (own_total, sibling_total)
+
+    inner = slots % key_blocks
+    places = slots // key_blocks * (key_blocks // 2) + inner % (key_blocks // 2)
+    parity = jnp.arange(slots.shape[0])[:, None] % 2
+    turned_places = (2 * reach_hops + 1) * (key_blocks // 2)
+    ready = own_weights
+    moved = []
+    for half in range(2):
+        *far_values, ready = lax.optimization_barrier((*[step[half] for step in steps], ready))
+        value_parts = [values[half]]
+        for far in far_values:
+            value_parts += [far, swapped(far, 1)]
+        side = jnp.bitwise_xor(inner // (key_blocks // 2), jnp.bitwise_xor(parity, half))
+        outputs = functools.partial(
+            block_outputs,
+            places + turned_places * side,
+            weights,
+            totals,
+            value_parts,
+            groups,
+            half,
+        )
+        if half == 0 or groups == 1:
+            pieces = outputs(0, groups)
+        else:
+            pieces = [None, *outputs(1, groups)]
+        sent_pieces = [swapped(pieces[n], n * share) for n in range(1, groups)]
+        if pieces[0] is None:
+            pieces[0] = outputs(0, 1)[0]
+        moved += [pieces[0], *sent_pieces]
+        ready = pieces[0]
+    return join_pieces(moved, share, head_width)
 
 
 def solution(mesh):

time: 26.3 us -> 26.1 us (level)
  waiting for transfers between devices: 13.3 us -> 6.52 us
  starting transfers between devices: 5.68 us -> 9.59 us
  Pallas kernels: 4.64 us -> 7.38 us
  local copies, waits for them, and re-layouts: 1.94 us -> 1.61 us
    ppermute x2 -> x3, waiting for transfers between devices: 6.49 us -> 2.92 us  [sent(): return lax.ppermute(x, ('ctx', 'head'), moves)]
    ppermute x4 -> x6, waiting for transfers between devices: 6.77 us -> 3.6 us  [swapped(): lax.ppermute(x, 'head', [(i, i ^ mask) for i in range(lax.axis_size('head...]
    pallas_call x3 -> x6, Pallas kernels: 3.23 us -> 5.85 us  [the longest x3 3.02 us: block_outputs(): pl.pallas_call(functools.partial(value_kernel, inputs=len(parts), flip=fl...]
    ppermute x4 -> x6, starting transfers between devices: 2.51 us -> 4.48 us  [swapped(): lax.ppermute(x, 'head', [(i, i ^ mask) for i in range(lax.axis_size('head...]
    ppermute x2 -> x3, starting transfers between devices: 3.17 us -> 5.11 us  [sent(): return lax.ppermute(x, ('ctx', 'head'), moves)]
    unnamed x8 -> x10, local copies, waits for them, and re-layouts: 0.05 us -> 1.39 us
    dynamic_slice x2, local copies, waits for them, and re-layouts: 0.97 us -> 0.04 us  [ordered(): lax.dynamic_slice(cut, (jnp.bitwise_xor(group, n), jnp.bitwise_xor(core,...]
    reshape x1, local copies, waits for them, and re-layouts: 0.74 us -> 0.08 us  [ordered(): cut = x.reshape((groups, share, rows_dev // head_count) + x.shape[1:])]
  transfers between devices with their start and end apart: 6 -> 9, of which waited for: 6 -> 4; matrix products, arithmetic and copies ran while one was open for 9% -> 3% of each run, Pallas kernels for 7% -> 20%
where the time goes in v6:
time: 26.1 us; the launch traced here: 25.8 us
  starting transfers between devices  9.59 us (37%)
  Pallas kernels  7.38 us (28%)
  waiting for transfers between devices  6.52 us (25%)
  local copies, waits for them, and re-layouts  1.61 us (6%)
  other arithmetic  0.55 us (2%)
    ppermute x3, starting transfers between devices, sent(): return lax.ppermute(x, ('ctx', 'head'), moves)  5.11 us
    ppermute x6, starting transfers between devices, swapped(): lax.ppermute(x, 'head', [(i, i ^ mask) for i in range(lax.axis_size('head...  4.48 us
    ppermute x6, waiting for transfers between devices, swapped(): lax.ppermute(x, 'head', [(i, i ^ mask) for i in range(lax.axis_size('head...  3.6 us
    pallas_call x3, Pallas kernels, block_outputs(): pl.pallas_call(functools.partial(value_kernel, inputs=len(parts), flip=fl...  3.02 us
    ppermute x3, waiting for transfers between devices, sent(): return lax.ppermute(x, ('ctx', 'head'), moves)  2.92 us
    pallas_call x2, Pallas kernels, block_weights(): pl.pallas_call(functools.partial(score_kernel, inputs=len(parts)), in_spe...  2.02 us
    unnamed x10, local copies, waits for them, and re-layouts  1.39 us
    pallas_call x1, Pallas kernels, begin(): pl.pallas_call(begin_kernel, in_specs=[pl.BlockSpec(memory_space=pltpu.HB...  1.31 us
  transfers between devices with their start and end apart: 9, of which 4 were waited for; matrix products, arithmetic and copies ran while one was open for 3% of the time, Pallas kernels for 20%

profile of v6, /device:TPU:0, one launch (start us, length us, event | category | flops | bytes accessed | tf_op | source)
XLA Modules:
  0.0 25.8 jit_solution(3279937934785602147)
XLA Ops:
  0.0 1.3 %begin.1 = (bf16[8,128,128]{2,1,0:T(8,128)(2,1)S(1)}, bf16[4,128,128]{2,1,0:T(8,128)(2,1)S(1)}, bf16[4,128,128]{2,1,0:T(8,128)(2,1)S(1)}) custom-call(s32[2,2,8]{2,1,0:T(2,128)} %index_hbm.1, f32[2,16]{1,0:T(2,128)} %table_hbm.1, bf16[2,1024,128]{2,1,0:T(8,128)(2,1)} %keys_hbm.1, bf16[2,1024,128]{2,1,0:T(8,128)(2,1)} %values_hbm.1), custom_call_target="tpu_custom_call" | custom-call | tf_op jit(solution)/shard_map/begin/pallas_call | solution.py:98
  1.3 3.1 %collective-permute-start = (bf16[8,128,128]{2,1,0:T(8,128)(2,1)S(1)}, bf16[8,128,128]{2,1,0:T(8,128)(2,1)S(1)}, u32[]{:S(2)}, u32[]{:S(2)}) collective-permute-start(bf16[8,128,128]{2,1,0:T(8,128)(2,1)S(1)} %get-tuple-element.31.rest_0_), channel_id=1, source_target_pairs={{4,0},{13,1},{6,2},{15,3},{0,4},{9,5},{2,6},{11,7},{12,8},{5,9},{1... | collective-permute-start | bytes 786440 | tf_op jit(solution)/shard_map/ppermute | solution.py:39
  4.5 1.9 %collective-permute-start.6 = (bf16[4,128,128]{2,1,0:T(8,128)(2,1)S(1)}, bf16[4,128,128]{2,1,0:T(8,128)(2,1)S(1)}, u32[]{:S(2)}, u32[]{:S(2)}) collective-permute-start(bf16[4,128,128]{2,1,0:T(8,128)(2,1)S(1)} %get-tuple-element.43.rest_4_), channel_id=1, source_target_pairs={{4,0},{13,1},{6,2},{15,3},{0,4},{9,5},{2,6},{11,7},{12,8},{5,9},{1... | collective-permute-start | bytes 393224 | tf_op jit(solution)/shard_map/ppermute | solution.py:39
  6.4 0.7 %copy-done.2 = s32[128]{0:T(128)S(1)} copy-done((s32[128]{0:T(128)S(1)}, s32[128]{0:T(128)}, u32[]{:S(2)}) %copy-start.2) | copy-done | bytes 536
  7.1 0.1 reshape.65
  7.3 0.7 %copy-done.1 = s32[8,4,8]{2,1,0:T(4,128)S(1)} copy-done((s32[8,4,8]{2,1,0:T(4,128)S(1)}, s32[8,4,8]{2,1,0:T(4,128)}, u32[]{:S(2)}) %copy-start.1) | copy-done | bytes 1048
  8.1 0.1 convert_element_type.29
  8.2 0.3 %fusion = (f32[128,128]{1,0:T(8,128)S(1)}, f32[128,128]{1,0:T(8,128)S(1)}) fusion(f32[128]{0:T(128)S(1)} %get-tuple-element.62, f32[128]{0:T(128)S(1)} %get-tuple-element.63, f32[128]{0:T(128)S(1)} %convert_element_type.29), kind=kLoop, calls=%fused_computation.3 | loop fusion | flops 32768 | bytes 132608 | tf_op jit(solution)/shard_map/mul | solution.py:342
  8.5 0.2 turn_queries.1
  8.7 2.9 %collective-permute-done.rest_1_ = bf16[8,128,128]{2,1,0:T(8,128)(2,1)S(1)} collective-permute-done((bf16[8,128,128]{2,1,0:T(8,128)(2,1)S(1)}, bf16[8,128,128]{2,1,0:T(8,128)(2,1)S(1)}, u32[]{:S(2)}, u32[]{:S(2)}) %collective-permute-start) | collective-permute-done | bytes 262176 | tf_op jit(solution)/shard_map/ppermute | solution.py:39
  11.6 0.5 %collective-permute-start.1 = (bf16[8,80,128]{2,1,0:T(8,128)(2,1)S(1)}, bf16[8,80,128]{2,1,0:T(8,128)(2,1)S(1)}, u32[]{:S(2)}, u32[]{:S(2)}) collective-permute-start(bf16[8,80,128]{2,1,0:T(8,128)(2,1)S(1)} %get-tuple-element.32), channel_id=1, source_target_pairs={{0,1},{1,0},{2,3},{3,2},{4,5},{5,4},{6,7},{7,6},{8,9},{9,8},{10,11... | collective-permute-start | bytes 491528 | tf_op jit(solution)/shard_map/ppermute | solution.py:43
  12.2 1.0 %collective-permute-done.1.queries_ref = bf16[8,80,128]{2,1,0:T(8,128)(2,1)S(1)} collective-permute-done((bf16[8,80,128]{2,1,0:T(8,128)(2,1)S(1)}, bf16[8,80,128]{2,1,0:T(8,128)(2,1)S(1)}, u32[]{:S(2)}, u32[]{:S(2)}) %collective-permute-start.1) | collective-permute-done | bytes 163872 | tf_op jit(solution)/shard_map/ppermute | solution.py:43
  13.2 0.4 %collective-permute-done.2.rest_2_ = bf16[8,128,128]{2,1,0:T(8,128)(2,1)S(1)} collective-permute-done((bf16[8,128,128]{2,1,0:T(8,128)(2,1)S(1)}, bf16[8,128,128]{2,1,0:T(8,128)(2,1)S(1)}, u32[]{:S(2)}, u32[]{:S(2)}) %collective-permute-start.2) | collective-permute-done | bytes 262176 | tf_op jit(solution)/shard_map/ppermute | solution.py:43
  13.6 1.0 %block_weights.2 = (bf16[8,64,1024]{2,1,0:T(8,128)(2,1)S(1)}, f32[8,64,128]{2,1,0:T(8,128)S(1)}) custom-call(s32[8,8]{1,0:T(8,128)S(1)} %get-tuple-element.55.slots_ref, bf16[8,64,128]{2,1,0:T(8,128)(2,1)S(1)} %get-tuple-element.33.queries_ref, bf16[8,128,128]{2,1,0:T(8,128)(2,1)S(1)} %get-tuple-element.31.rest_0_, ...), custom_call_target="tpu_custom_call" | custom-call | tf_op jit(solution)/shard_map/block_weights/pallas_call | solution.py:190
  14.7 0.3 %collective-permute-start.4 = (bf16[4,128,128]{2,1,0:T(8,128)(2,1)S(1)}, bf16[4,128,128]{2,1,0:T(8,128)(2,1)S(1)}, u32[]{:S(2)}, u32[]{:S(2)}) collective-permute-start(bf16[4,128,128]{2,1,0:T(8,128)(2,1)S(1)} %collective-permute-done.3.rest_5_), channel_id=1, source_target_pairs={{0,1},{1,0},{2,3},{3,2},{4,5},{5,4},{6,7},{7,6},{8,9},{9,8},{10,11... | collective-permute-start | bytes 393224 | tf_op jit(solution)/shard_map/ppermute | solution.py:43
  15.0 1.0 %block_weights.3 = (bf16[8,64,1024]{2,1,0:T(8,128)(2,1)S(1)}, f32[8,64,128]{2,1,0:T(8,128)S(1)}) custom-call(s32[8,8]{1,0:T(8,128)S(1)} %get-tuple-element.54.slots_ref, bf16[8,80,128]{2,1,0:T(8,128)(2,1)S(1)} %collective-permute-done.1.queries_ref, bf16[8,128,128]{2,1,0:T(8,128)(2,1)S(1)} %get-tuple-element.31.rest_0_, ...), custom_call_target="tpu_custom_call" | custom-call | tf_op jit(solution)/shard_map/block_weights/pallas_call | solution.py:190
  16.1 1.1 %block_outputs.3 = (bf16[32,1024]{1,0:T(8,128)(2,1)S(1)}, bf16[32,1024]{1,0:T(8,128)(2,1)S(1)}) custom-call(s32[16,8]{1,0:T(8,128)S(1)} %multiply_add_fusion.1.slots_ref, bf16[8,64,1024]{2,1,0:T(8,128)(2,1)S(1)} %get-tuple-element.35.rest_0_, bf16[8,64,1024]{2,1,0:T(8,128)(2,1)S(1)} %get-tuple-element.36.rest_1_, ...), custom_call_target="tpu_custom_call" | custom-call | tf_op jit(solution)/shard_map/block_outputs/pallas_call | solution.py:246
  17.2 0.3 %collective-permute-start.7 = (bf16[4,128,128]{2,1,0:T(8,128)(2,1)S(1)}, bf16[4,128,128]{2,1,0:T(8,128)(2,1)S(1)}, u32[]{:S(2)}, u32[]{:S(2)}) collective-permute-start(bf16[4,128,128]{2,1,0:T(8,128)(2,1)S(1)} %collective-permute-done.6.rest_5_), channel_id=1, source_target_pairs={{0,1},{1,0},{2,3},{3,2},{4,5},{5,4},{6,7},{7,6},{8,9},{9,8},{10,11... | collective-permute-start | bytes 393224 | tf_op jit(solution)/shard_map/ppermute | solution.py:43
  17.5 2.2 %collective-permute-start.5 = (bf16[32,1024]{1,0:T(8,128)(2,1)S(1)}, bf16[32,1024]{1,0:T(8,128)(2,1)S(1)}, u32[]{:S(2)}, u32[]{:S(2)}) collective-permute-start(bf16[32,1024]{1,0:T(8,128)(2,1)S(1)} %get-tuple-element.42), channel_id=1, source_target_pairs={{0,2},{1,3},{2,0},{3,1},{4,6},{5,7},{6,4},{7,5},{8,10},{9,11},{10,... | collective-permute-start | bytes 196616 | tf_op jit(solution)/shard_map/ppermute | solution.py:43
  19.7 1.0 %block_outputs.5 = bf16[32,1024]{1,0:T(8,128)(2,1)S(1)} custom-call(s32[16,8]{1,0:T(8,128)S(1)} %get-tuple-element.45.slots_ref, bf16[8,64,1024]{2,1,0:T(8,128)(2,1)S(1)} %get-tuple-element.35.rest_0_, bf16[8,64,1024]{2,1,0:T(8,128)(2,1)S(1)} %get-tuple-element.36.rest_1_, f32[8,64,128]{2,1,0:T(8,128)S(1)} %get-tuple-element.37.rest_2_, ...), custom_call_target="tpu_custom_call" | custom-call | tf_op jit(solution)/shard_map/block_outputs/pallas_call | solution.py:246
  20.7 1.2 %collective-permute-start.8 = (bf16[32,1024]{1,0:T(8,128)(2,1)S(1)}, bf16[32,1024]{1,0:T(8,128)(2,1)S(1)}, u32[]{:S(2)}, u32[]{:S(2)}) collective-permute-start(bf16[32,1024]{1,0:T(8,128)(2,1)S(1)} %block_outputs.5), channel_id=1, source_target_pairs={{0,2},{1,3},{2,0},{3,1},{4,6},{5,7},{6,4},{7,5},{8,10},{9,11},{10,... | collective-permute-start | bytes 196616 | tf_op jit(solution)/shard_map/ppermute | solution.py:43
  21.8 1.0 %block_outputs.4.refs_2_ = bf16[32,1024]{1,0:T(8,128)(2,1)S(1)} custom-call(s32[16,8]{1,0:T(8,128)S(1)} %get-tuple-element.45.slots_ref, bf16[8,64,1024]{2,1,0:T(8,128)(2,1)S(1)} %get-tuple-element.35.rest_0_, bf16[8,64,1024]{2,1,0:T(8,128)(2,1)S(1)} %get-tuple-element.36.rest_1_, f32[8,64,128]{2,1,0:T(8,128)S(1)} %get-tuple-element.37.rest_2_, ...), custom_call_target="tpu_custom_call" | custom-call | tf_op jit(solution)/shard_map/block_outputs/pallas_call | solution.py:246
  22.8 2.2 %collective-permute-done.8.refs_3_ = bf16[32,1024]{1,0:T(8,128)(2,1)S(1)} collective-permute-done((bf16[32,1024]{1,0:T(8,128)(2,1)S(1)}, bf16[32,1024]{1,0:T(8,128)(2,1)S(1)}, u32[]{:S(2)}, u32[]{:S(2)}) %collective-permute-start.8) | collective-permute-done | bytes 65568 | tf_op jit(solution)/shard_map/ppermute | solution.py:43
  25.0 0.8 %join_pieces.1 = bf16[32,4096]{1,0:T(8,128)(2,1)} custom-call(bf16[32,1024]{1,0:T(8,128)(2,1)S(1)} %get-tuple-element.41.refs_0_, bf16[32,1024]{1,0:T(8,128)(2,1)S(1)} %collective-permute-done.5.refs_1_, bf16[32,1024]{1,0:T(8,128)(2,1)S(1)} %block_outputs.4.refs_2_, bf16[32,1024]{1,0:T(8,128)(2,1)S(1)} %collective-permute-done.8.refs_3_), custom_call_target="tpu_custom_call" | custom-call | tf_op jit(solution)/shard_map/join_pieces/pallas_call | solution.py:288
  (29 shorter events, 0.5 us)
Async XLA Ops:
  0.0 7.2 %copy-start = (bf16[128,8,128]{2,1,0:T(8,128)(2,1)S(1)}, bf16[128,8,128]{2,1,0:T(8,128)(2,1)}, u32[]{:S(2)}) copy-start(bf16[128,8,128]{2,1,0:T(8,128)(2,1)} %param.7) | copy-start | bytes 786436
  1.3 10.3 %collective-permute-start = (bf16[8,128,128]{2,1,0:T(8,128)(2,1)S(1)}, bf16[8,128,128]{2,1,0:T(8,128)(2,1)S(1)}, u32[]{:S(2)}, u32[]{:S(2)}) collective-permute-start(bf16[8,128,128]{2,1,0:T(8,128)(2,1)S(1)} %get-tuple-element.31.rest_0_), channel_id=1, source_target_pairs={{4,0},{13,1},{6,2},{15,3},{0,4},{9,5},{2,6},{11,7},{12,8},{5,9},{1... | collective-permute-start | bytes 786440 | tf_op jit(solution)/shard_map/ppermute | solution.py:39
  4.4 10.3 %collective-permute-start.3 = (bf16[4,128,128]{2,1,0:T(8,128)(2,1)S(1)}, bf16[4,128,128]{2,1,0:T(8,128)(2,1)S(1)}, u32[]{:S(2)}, u32[]{:S(2)}) collective-permute-start(bf16[4,128,128]{2,1,0:T(8,128)(2,1)S(1)} %get-tuple-element.39.rest_4_), channel_id=1, source_target_pairs={{4,0},{13,1},{6,2},{15,3},{0,4},{9,5},{2,6},{11,7},{12,8},{5,9},{1... | collective-permute-start | bytes 393224 | tf_op jit(solution)/shard_map/ppermute | solution.py:39
  4.5 12.7 %collective-permute-start.6 = (bf16[4,128,128]{2,1,0:T(8,128)(2,1)S(1)}, bf16[4,128,128]{2,1,0:T(8,128)(2,1)S(1)}, u32[]{:S(2)}, u32[]{:S(2)}) collective-permute-start(bf16[4,128,128]{2,1,0:T(8,128)(2,1)S(1)} %get-tuple-element.43.rest_4_), channel_id=1, source_target_pairs={{4,0},{13,1},{6,2},{15,3},{0,4},{9,5},{2,6},{11,7},{12,8},{5,9},{1... | collective-permute-start | bytes 393224 | tf_op jit(solution)/shard_map/ppermute | solution.py:39
  6.4 0.7 %copy-start.2 = (s32[128]{0:T(128)S(1)}, s32[128]{0:T(128)}, u32[]{:S(2)}) copy-start(s32[128]{0:T(128)} %param.8) | copy-start | bytes 1540
  7.3 0.7 %copy-start.1 = (s32[8,4,8]{2,1,0:T(4,128)S(1)}, s32[8,4,8]{2,1,0:T(4,128)}, u32[]{:S(2)}) copy-start(s32[8,4,8]{2,1,0:T(4,128)} %param.13) | copy-start | bytes 3076
  11.6 1.5 %collective-permute-start.1 = (bf16[8,80,128]{2,1,0:T(8,128)(2,1)S(1)}, bf16[8,80,128]{2,1,0:T(8,128)(2,1)S(1)}, u32[]{:S(2)}, u32[]{:S(2)}) collective-permute-start(bf16[8,80,128]{2,1,0:T(8,128)(2,1)S(1)} %get-tuple-element.32), channel_id=1, source_target_pairs={{0,1},{1,0},{2,3},{3,2},{4,5},{5,4},{6,7},{7,6},{8,9},{9,8},{10,11... | collective-permute-start | bytes 491528 | tf_op jit(solution)/shard_map/ppermute | solution.py:43
  12.1 1.5 %collective-permute-start.2 = (bf16[8,128,128]{2,1,0:T(8,128)(2,1)S(1)}, bf16[8,128,128]{2,1,0:T(8,128)(2,1)S(1)}, u32[]{:S(2)}, u32[]{:S(2)}) collective-permute-start(bf16[8,128,128]{2,1,0:T(8,128)(2,1)S(1)} %collective-permute-done.rest_1_), channel_id=1, source_target_pairs={{0,1},{1,0},{2,3},{3,2},{4,5},{5,4},{6,7},{7,6},{8,9},{9,8},{10,11... | collective-permute-start | bytes 786440 | tf_op jit(solution)/shard_map/ppermute | solution.py:43
  14.7 1.4 %collective-permute-start.4 = (bf16[4,128,128]{2,1,0:T(8,128)(2,1)S(1)}, bf16[4,128,128]{2,1,0:T(8,128)(2,1)S(1)}, u32[]{:S(2)}, u32[]{:S(2)}) collective-permute-start(bf16[4,128,128]{2,1,0:T(8,128)(2,1)S(1)} %collective-permute-done.3.rest_5_), channel_id=1, source_target_pairs={{0,1},{1,0},{2,3},{3,2},{4,5},{5,4},{6,7},{7,6},{8,9},{9,8},{10,11... | collective-permute-start | bytes 393224 | tf_op jit(solution)/shard_map/ppermute | solution.py:43
  17.2 2.5 %collective-permute-start.7 = (bf16[4,128,128]{2,1,0:T(8,128)(2,1)S(1)}, bf16[4,128,128]{2,1,0:T(8,128)(2,1)S(1)}, u32[]{:S(2)}, u32[]{:S(2)}) collective-permute-start(bf16[4,128,128]{2,1,0:T(8,128)(2,1)S(1)} %collective-permute-done.6.rest_5_), channel_id=1, source_target_pairs={{0,1},{1,0},{2,3},{3,2},{4,5},{5,4},{6,7},{7,6},{8,9},{9,8},{10,11... | collective-permute-start | bytes 393224 | tf_op jit(solution)/shard_map/ppermute | solution.py:43
  17.5 5.3 %collective-permute-start.5 = (bf16[32,1024]{1,0:T(8,128)(2,1)S(1)}, bf16[32,1024]{1,0:T(8,128)(2,1)S(1)}, u32[]{:S(2)}, u32[]{:S(2)}) collective-permute-start(bf16[32,1024]{1,0:T(8,128)(2,1)S(1)} %get-tuple-element.42), channel_id=1, source_target_pairs={{0,2},{1,3},{2,0},{3,1},{4,6},{5,7},{6,4},{7,5},{8,10},{9,11},{10,... | collective-permute-start | bytes 196616 | tf_op jit(solution)/shard_map/ppermute | solution.py:43
  20.7 4.3 %collective-permute-start.8 = (bf16[32,1024]{1,0:T(8,128)(2,1)S(1)}, bf16[32,1024]{1,0:T(8,128)(2,1)S(1)}, u32[]{:S(2)}, u32[]{:S(2)}) collective-permute-start(bf16[32,1024]{1,0:T(8,128)(2,1)S(1)} %block_outputs.5), channel_id=1, source_target_pairs={{0,2},{1,3},{2,0},{3,1},{4,6},{5,7},{6,4},{7,5},{8,10},{9,11},{10,... | collective-permute-start | bytes 196616 | tf_op jit(solution)/shard_map/ppermute | solution.py:43

commit v7 on v6

--- a/solution.py
+++ b/solution.py
@@ -39,16 +39,15 @@
     return lax.ppermute(x, ("ctx", "head"), moves)
 
 
+def across(n, share):
+    return n * share ^ n % share
+
+
 def swapped(x, mask):
     return lax.ppermute(x, "head", [(i, i ^ mask) for i in range(lax.axis_size("head"))])
 
 
-def lower_half(shape):
-    return lax.broadcasted_iota(jnp.int32, shape, 1) < shape[1] // 2
-
-
-def begin_kernel(index_hbm, table_hbm, keys_hbm, values_hbm, keys_ref, *rest):
-    first_ref, second_ref, index_ref, table_ref, key_codes, value_codes, arrived = rest
+def fetch(index_hbm, table_hbm, codes_hbm, index_ref, table_ref, codes_ref, arrived, row):
     groups = index_hbm.shape[1]
     kv_head = lax.axis_index("head") * groups // lax.axis_size("head")
     copies = [
@@ -57,8 +56,7 @@
             (
                 (index_hbm, index_ref),
                 (table_hbm, table_ref),
-                (keys_hbm.at[kv_head], key_codes),
-                (values_hbm.at[kv_head], value_codes),
+                (codes_hbm.at[kv_head], codes_ref),
             )
         )
     ]
@@ -66,54 +64,79 @@
         copy.start()
     for copy in copies[:2]:
         copy.wait()
-    blocks = keys_ref.shape[0]
     scales = [
-        [table_ref[row, index_ref[row, kv_head, block]] for block in range(blocks)]
-        for row in range(2)
+        table_ref[row, index_ref[row, kv_head, block]] for block in range(index_hbm.shape[2])
     ]
     copies[2].wait()
-    for block in range(blocks):
-        codes = key_codes[block * BLOCK : (block + 1) * BLOCK, :].astype(jnp.float32)
-        keys_ref[block] = (codes * scales[0][block]).T.astype(jnp.bfloat16)
-    copies[3].wait()
+    return scales
+
+
+def key_kernel(index_hbm, table_hbm, codes_hbm, out_ref, *scratch):
+    codes_ref = scratch[2]
+    for block, scale in enumerate(fetch(index_hbm, table_hbm, codes_hbm, *scratch, 0)):
+        codes = codes_ref[block * BLOCK : (block + 1) * BLOCK, :].astype(jnp.float32)
+        out_ref[block] = (codes * scale).T.astype(jnp.bfloat16)
+
+
+def half_kernel(index_hbm, table_hbm, codes_hbm, _, *rest):
+    *others, index_ref, table_ref, codes_ref, arrived = rest
+    scratch = (index_ref, table_ref, codes_ref, arrived)
+    count = len(others) // 2 - 1
+    first_ref, second_ref = others[count : count + 2]
+    copies = [
+        pltpu.make_async_copy(others[n], others[count + 2 + n], arrived.at[3 + n])
+        for n in range(count)
+    ]
+    for copy in copies:
+        copy.start()
+    scales = fetch(index_hbm, table_hbm, codes_hbm, *scratch, 1)
     pairs = first_ref.shape[0]
-    width = value_codes.shape[1]
+    width = codes_ref.shape[1]
     low = lower_half((BLOCK, width))
     for pair in range(pairs):
         left, right = (
-            value_codes[block * BLOCK : (block + 1) * BLOCK, :].astype(jnp.float32)
-            * scales[1][block]
+            codes_ref[block * BLOCK : (block + 1) * BLOCK, :].astype(jnp.float32) * scales[block]
             for block in (pair, pair + pairs)
         )
         first = jnp.where(low, left, pltpu.roll(right, width // 2, 1))
         second = jnp.where(low, pltpu.roll(left, width // 2, 1), right)
         first_ref[pair] = first.astype(jnp.bfloat16)
         second_ref[pair] = second.astype(jnp.bfloat16)
-
-
-def begin(scale_index, scale_table, key_codes, value_codes):
-    _, keys_dev, width = key_codes.shape
-    blocks = keys_dev // BLOCK
+    for copy in copies:
+        copy.wait()
+
+
+def lower_half(shape):
+    return lax.broadcasted_iota(jnp.int32, shape, 1) < shape[1] // 2
+
+
+def begin(kernel, scale_index, scale_table, codes, outputs, *after, others=()):
+    _, keys_dev, width = codes.shape
+    blocks = keys_dev // BLOCK // outputs
     stay = functools.partial(pltpu.with_memory_space_constraint, memory_space=pltpu.HBM)
     return pl.pallas_call(
-        begin_kernel,
-        in_specs=[pl.BlockSpec(memory_space=pltpu.HBM)] * 4,
-        out_specs=[in_vmem] * 3,
-        out_shape=[
-            pltpu.VMEM((blocks, width, BLOCK), jnp.bfloat16),
-            pltpu.VMEM((blocks // 2, BLOCK, width), jnp.bfloat16),
-            pltpu.VMEM((blocks // 2, BLOCK, width), jnp.bfloat16),
-        ],
+        kernel,
+        in_specs=[pl.BlockSpec(memory_space=pltpu.HBM)] * 3
+        + [pl.BlockSpec(memory_space=pl.ANY)] * len(after)
+        + [pl.BlockSpec(memory_space=pltpu.HBM)] * len(others),
+        out_specs=[in_vmem] * (outputs + len(others)),
+        out_shape=[pltpu.VMEM((blocks, BLOCK, width), jnp.bfloat16)] * outputs
+        + [pltpu.VMEM(other.shape, other.dtype) for other in others],
         scratch_shapes=[
             pltpu.SMEM(scale_index.shape, scale_index.dtype),
             pltpu.SMEM(scale_table.shape, scale_table.dtype),
-            pltpu.VMEM((keys_dev, width), key_codes.dtype),
-            pltpu.VMEM((keys_dev, width), value_codes.dtype),
-            pltpu.SemaphoreType.DMA((4,)),
+            pltpu.VMEM((keys_dev, width), codes.dtype),
+            pltpu.SemaphoreType.DMA((3 + len(others),)),
         ],
         compiler_params=granted,
-        name="begin",
-    )(stay(scale_index), stay(scale_table), stay(key_codes), stay(value_codes))
+        name=kernel.__name__,
+    )(
+        stay(scale_index),
+        stay(scale_table),
+        stay(codes),
+        *after,
+        *[stay(other) for other in others],
+    )
 
 
 def turn_kernel(queries_ref, cosine_ref, sine_ref, lists_ref, own_ref, sibling_ref):
@@ -269,7 +292,7 @@
     low = lower_half((rows, width))
     for n in range(chips):
         for part in range(share):
-            column = jnp.bitwise_xor(place, n * share + part) * (2 * pairs * width)
+            column = jnp.bitwise_xor(place, across(n, share) ^ part) * (2 * pairs * width)
             for pair in range(pairs):
                 at = (part * pairs + pair) * width
                 first, second = (
@@ -310,22 +333,29 @@
     group = head_place // share
     groups = head_count // share
 
-    keys, *values = begin(scale_index, scale_table, key_codes, value_codes)
+    (keys,) = begin(key_kernel, scale_index, scale_table, key_codes, 1)
+    *values, queries, positions, block_lists = begin(
+        half_kernel,
+        scale_index,
+        scale_table,
+        value_codes,
+        2,
+        keys,
+        others=(queries, positions, block_lists),
+    )
     far_keys = keys
     key_parts = []
     for _ in range(reach_hops):
         far_keys = sent(far_keys, share, pairs)
         key_parts.append(far_keys)
-    *values, queries, positions, block_lists = lax.optimization_barrier(
-        (*values, queries, positions, block_lists)
-    )
     own_lists = lax.dynamic_index_in_dim(block_lists, cycle_place, 1, keepdims=False)
     def ordered(x):
         cut = x.reshape((groups, share, rows_dev // head_count) + x.shape[1:])
         taken = [
             lax.dynamic_slice(
                 cut,
-                (jnp.bitwise_xor(group, n), jnp.bitwise_xor(core, part)) + (0,) * x.ndim,
+                (jnp.bitwise_xor(group, n), jnp.bitwise_xor(core, part ^ n % share))
+                + (0,) * x.ndim,
                 (1, 1) + cut.shape[2:],
             )
             for part in range(share)
@@ -394,7 +424,7 @@
             pieces = outputs(0, groups)
         else:
             pieces = [None, *outputs(1, groups)]
-        sent_pieces = [swapped(pieces[n], n * share) for n in range(1, groups)]
+        sent_pieces = [swapped(pieces[n], across(n, share)) for n in range(1, groups)]
         if pieces[0] is None:
             pieces[0] = outputs(0, 1)[0]
         moved += [pieces[0], *sent_pieces]

time: 26.1 us -> 25.2 us (0.966)
  local copies, waits for them, and re-layouts: 1.61 us -> 0.27 us
  Pallas kernels: 7.38 us -> 8.44 us
  starting transfers between devices: 9.59 us -> 9.3 us
    unnamed x10 -> x4, local copies, waits for them, and re-layouts: 1.39 us -> 0.05 us
    pallas_call x1 -> x2, Pallas kernels: 1.31 us -> 2.37 us  [begin(): pl.pallas_call(kernel, in_specs=[pl.BlockSpec(memory_space=pltpu.HBM)] *...]
    ppermute x6, starting transfers between devices: 4.48 us -> 4.12 us  [swapped(): lax.ppermute(x, 'head', [(i, i ^ mask) for i in range(lax.axis_size('head...]
  transfers between devices with their start and end apart: 9 -> 9, of which waited for: 4 -> 4; matrix products, arithmetic and copies ran while one was open for 3% -> 3% of each run, Pallas kernels for 20% -> 26%
where the time goes in v7:
time: 25.2 us; the launch traced here: 25 us
  starting transfers between devices  9.3 us (37%)
  Pallas kernels  8.44 us (33%)
  waiting for transfers between devices  6.27 us (25%)
  other arithmetic  0.54 us (2%)
  local copies, waits for them, and re-layouts  0.27 us (1%)
    ppermute x3, starting transfers between devices, sent(): return lax.ppermute(x, ('ctx', 'head'), moves)  5.18 us
    ppermute x6, starting transfers between devices, swapped(): lax.ppermute(x, 'head', [(i, i ^ mask) for i in range(lax.axis_size('head...  4.12 us
    ppermute x6, waiting for transfers between devices, swapped(): lax.ppermute(x, 'head', [(i, i ^ mask) for i in range(lax.axis_size('head...  3.41 us
    pallas_call x3, Pallas kernels, block_outputs(): pl.pallas_call(functools.partial(value_kernel, inputs=len(parts), flip=fl...  3.01 us
    ppermute x3, waiting for transfers between devices, sent(): return lax.ppermute(x, ('ctx', 'head'), moves)  2.86 us
    pallas_call x2, Pallas kernels, begin(): pl.pallas_call(kernel, in_specs=[pl.BlockSpec(memory_space=pltpu.HBM)] *...  2.37 us
    pallas_call x2, Pallas kernels, block_weights(): pl.pallas_call(functools.partial(score_kernel, inputs=len(parts)), in_spe...  2.02 us
    pallas_call x1, Pallas kernels, join_pieces(): pl.pallas_call(functools.partial(join_kernel, share=share, width=width),...  0.82 us
  transfers between devices with their start and end apart: 9, of which 4 were waited for; matrix products, arithmetic and copies ran while one was open for 3% of the time, Pallas kernels for 26%

profile of v7, /device:TPU:0, one launch (start us, length us, event | category | flops | bytes accessed | tf_op | source)
XLA Modules:
  0.0 25.0 jit_solution(6133868983365613563)
XLA Ops:
  0.0 1.1 %key_kernel.1._.rest_0_ = bf16[8,128,128]{2,1,0:T(8,128)(2,1)S(1)} custom-call(s32[2,2,8]{2,1,0:T(2,128)} %index_hbm.3, f32[2,16]{1,0:T(2,128)} %table_hbm.3, bf16[2,1024,128]{2,1,0:T(8,128)(2,1)} %codes_hbm.2), custom_call_target="tpu_custom_call" | custom-call | tf_op jit(solution)/shard_map/key_kernel/pallas_call | solution.py:117
  1.1 3.1 %collective-permute-start = (bf16[8,128,128]{2,1,0:T(8,128)(2,1)S(1)}, bf16[8,128,128]{2,1,0:T(8,128)(2,1)S(1)}, u32[]{:S(2)}, u32[]{:S(2)}) collective-permute-start(bf16[8,128,128]{2,1,0:T(8,128)(2,1)S(1)} %key_kernel.1._.rest_0_), channel_id=1, source_target_pairs={{4,0},{13,1},{6,2},{15,3},{0,4},{9,5},{2,6},{11,7},{12,8},{5,9},{1... | collective-permute-start | bytes 786440 | tf_op jit(solution)/shard_map/ppermute | solution.py:39
  4.2 1.3 %half_kernel.1 = (bf16[4,128,128]{2,1,0:T(8,128)(2,1)S(1)}, bf16[4,128,128]{2,1,0:T(8,128)(2,1)S(1)}, bf16[128,8,128]{2,1,0:T(8,128)(2,1)S(1)}, s32[128]{0:T(128)S(1)}, s32[8,4,8]{2,1,0:T(4,128)S(1)}) custom-call(s32[2,2,8]{2,1,0:T(2,128)} %index_hbm.3, f32[2,16]{1,0:T(2,128)} %table_hbm.3, bf16[2,1024,128]{2,1,0:T(8,128)(2,1)} %codes_hbm.3, ...), custom_call_target="tpu_custom_call" | custom-call | tf_op jit(solution)/shard_map/half_kernel/pallas_call | solution.py:117
  5.5 0.1 collective-permute-start.3
  5.6 2.0 %collective-permute-start.6 = (bf16[4,128,128]{2,1,0:T(8,128)(2,1)S(1)}, bf16[4,128,128]{2,1,0:T(8,128)(2,1)S(1)}, u32[]{:S(2)}, u32[]{:S(2)}) collective-permute-start(bf16[4,128,128]{2,1,0:T(8,128)(2,1)S(1)} %get-tuple-element.37.rest_4_), channel_id=1, source_target_pairs={{4,0},{13,1},{6,2},{15,3},{0,4},{9,5},{2,6},{11,7},{12,8},{5,9},{1... | collective-permute-start | bytes 393224 | tf_op jit(solution)/shard_map/ppermute | solution.py:39
  7.6 0.1 reshape.65
  7.9 0.1 convert_element_type.29
  8.0 0.3 %fusion = (f32[128,128]{1,0:T(8,128)S(1)}, f32[128,128]{1,0:T(8,128)S(1)}) fusion(f32[128]{0:T(128)S(1)} %get-tuple-element.54, f32[128]{0:T(128)S(1)} %get-tuple-element.55, f32[128]{0:T(128)S(1)} %convert_element_type.29), kind=kLoop, calls=%fused_computation.3 | loop fusion | flops 32768 | bytes 132608 | tf_op jit(solution)/shard_map/mul | solution.py:372
  8.3 0.2 turn_queries.1
  8.5 2.9 %collective-permute-done.rest_1_ = bf16[8,128,128]{2,1,0:T(8,128)(2,1)S(1)} collective-permute-done((bf16[8,128,128]{2,1,0:T(8,128)(2,1)S(1)}, bf16[8,128,128]{2,1,0:T(8,128)(2,1)S(1)}, u32[]{:S(2)}, u32[]{:S(2)}) %collective-permute-start) | collective-permute-done | bytes 262176 | tf_op jit(solution)/shard_map/ppermute | solution.py:39
  11.4 0.5 %collective-permute-start.1 = (bf16[8,80,128]{2,1,0:T(8,128)(2,1)S(1)}, bf16[8,80,128]{2,1,0:T(8,128)(2,1)S(1)}, u32[]{:S(2)}, u32[]{:S(2)}) collective-permute-start(bf16[8,80,128]{2,1,0:T(8,128)(2,1)S(1)} %get-tuple-element.26), channel_id=1, source_target_pairs={{0,1},{1,0},{2,3},{3,2},{4,5},{5,4},{6,7},{7,6},{8,9},{9,8},{10,11... | collective-permute-start | bytes 491528 | tf_op jit(solution)/shard_map/ppermute | solution.py:47
  12.0 1.0 %collective-permute-done.1.queries_ref = bf16[8,80,128]{2,1,0:T(8,128)(2,1)S(1)} collective-permute-done((bf16[8,80,128]{2,1,0:T(8,128)(2,1)S(1)}, bf16[8,80,128]{2,1,0:T(8,128)(2,1)S(1)}, u32[]{:S(2)}, u32[]{:S(2)}) %collective-permute-start.1) | collective-permute-done | bytes 163872 | tf_op jit(solution)/shard_map/ppermute | solution.py:47
  13.0 0.4 %collective-permute-done.2.rest_2_ = bf16[8,128,128]{2,1,0:T(8,128)(2,1)S(1)} collective-permute-done((bf16[8,128,128]{2,1,0:T(8,128)(2,1)S(1)}, bf16[8,128,128]{2,1,0:T(8,128)(2,1)S(1)}, u32[]{:S(2)}, u32[]{:S(2)}) %collective-permute-start.2) | collective-permute-done | bytes 262176 | tf_op jit(solution)/shard_map/ppermute | solution.py:47
  13.4 1.0 %block_weights.2 = (bf16[8,64,1024]{2,1,0:T(8,128)(2,1)S(1)}, f32[8,64,128]{2,1,0:T(8,128)S(1)}) custom-call(s32[8,8]{1,0:T(8,128)S(1)} %get-tuple-element.47.slots_ref, bf16[8,64,128]{2,1,0:T(8,128)(2,1)S(1)} %get-tuple-element.27.queries_ref, bf16[8,128,128]{2,1,0:T(8,128)(2,1)S(1)} %key_kernel.1._.rest_0_, ...), custom_call_target="tpu_custom_call" | custom-call | tf_op jit(solution)/shard_map/block_weights/pallas_call | solution.py:213
  14.5 0.3 %collective-permute-start.4 = (bf16[4,128,128]{2,1,0:T(8,128)(2,1)S(1)}, bf16[4,128,128]{2,1,0:T(8,128)(2,1)S(1)}, u32[]{:S(2)}, u32[]{:S(2)}) collective-permute-start(bf16[4,128,128]{2,1,0:T(8,128)(2,1)S(1)} %collective-permute-done.3.rest_5_), channel_id=1, source_target_pairs={{0,1},{1,0},{2,3},{3,2},{4,5},{5,4},{6,7},{7,6},{8,9},{9,8},{10,11... | collective-permute-start | bytes 393224 | tf_op jit(solution)/shard_map/ppermute | solution.py:47
  14.8 1.0 %block_weights.3 = (bf16[8,64,1024]{2,1,0:T(8,128)(2,1)S(1)}, f32[8,64,128]{2,1,0:T(8,128)S(1)}) custom-call(s32[8,8]{1,0:T(8,128)S(1)} %get-tuple-element.46.slots_ref, bf16[8,80,128]{2,1,0:T(8,128)(2,1)S(1)} %collective-permute-done.1.queries_ref, bf16[8,128,128]{2,1,0:T(8,128)(2,1)S(1)} %key_kernel.1._.rest_0_, ...), custom_call_target="tpu_custom_call" | custom-call | tf_op jit(solution)/shard_map/block_weights/pallas_call | solution.py:213
  15.9 1.1 %block_outputs.3 = (bf16[32,1024]{1,0:T(8,128)(2,1)S(1)}, bf16[32,1024]{1,0:T(8,128)(2,1)S(1)}) custom-call(s32[16,8]{1,0:T(8,128)S(1)} %multiply_add_fusion.1.slots_ref, bf16[8,64,1024]{2,1,0:T(8,128)(2,1)S(1)} %get-tuple-element.29.rest_0_, bf16[8,64,1024]{2,1,0:T(8,128)(2,1)S(1)} %get-tuple-element.30.rest_1_, ...), custom_call_target="tpu_custom_call" | custom-call | tf_op jit(solution)/shard_map/block_outputs/pallas_call | solution.py:269
  17.0 0.3 %collective-permute-start.7 = (bf16[4,128,128]{2,1,0:T(8,128)(2,1)S(1)}, bf16[4,128,128]{2,1,0:T(8,128)(2,1)S(1)}, u32[]{:S(2)}, u32[]{:S(2)}) collective-permute-start(bf16[4,128,128]{2,1,0:T(8,128)(2,1)S(1)} %collective-permute-done.6.rest_5_), channel_id=1, source_target_pairs={{0,1},{1,0},{2,3},{3,2},{4,5},{5,4},{6,7},{7,6},{8,9},{9,8},{10,11... | collective-permute-start | bytes 393224 | tf_op jit(solution)/shard_map/ppermute | solution.py:47
  17.3 1.8 %collective-permute-start.5 = (bf16[32,1024]{1,0:T(8,128)(2,1)S(1)}, bf16[32,1024]{1,0:T(8,128)(2,1)S(1)}, u32[]{:S(2)}, u32[]{:S(2)}) collective-permute-start(bf16[32,1024]{1,0:T(8,128)(2,1)S(1)} %get-tuple-element.36), channel_id=1, source_target_pairs={{0,3},{1,2},{2,1},{3,0},{4,7},{5,6},{6,5},{7,4},{8,11},{9,10},{10,... | collective-permute-start | bytes 196616 | tf_op jit(solution)/shard_map/ppermute | solution.py:47
  19.1 1.0 %block_outputs.5 = bf16[32,1024]{1,0:T(8,128)(2,1)S(1)} custom-call(s32[16,8]{1,0:T(8,128)S(1)} %get-tuple-element.39.slots_ref, bf16[8,64,1024]{2,1,0:T(8,128)(2,1)S(1)} %get-tuple-element.29.rest_0_, bf16[8,64,1024]{2,1,0:T(8,128)(2,1)S(1)} %get-tuple-element.30.rest_1_, f32[8,64,128]{2,1,0:T(8,128)S(1)} %get-tuple-element.31.rest_2_, ...), custom_call_target="tpu_custom_call" | custom-call | tf_op jit(solution)/shard_map/block_outputs/pallas_call | solution.py:269
  20.1 1.1 %collective-permute-start.8 = (bf16[32,1024]{1,0:T(8,128)(2,1)S(1)}, bf16[32,1024]{1,0:T(8,128)(2,1)S(1)}, u32[]{:S(2)}, u32[]{:S(2)}) collective-permute-start(bf16[32,1024]{1,0:T(8,128)(2,1)S(1)} %block_outputs.5), channel_id=1, source_target_pairs={{0,3},{1,2},{2,1},{3,0},{4,7},{5,6},{6,5},{7,4},{8,11},{9,10},{10,... | collective-permute-start | bytes 196616 | tf_op jit(solution)/shard_map/ppermute | solution.py:47
  21.2 1.0 %block_outputs.4.refs_2_ = bf16[32,1024]{1,0:T(8,128)(2,1)S(1)} custom-call(s32[16,8]{1,0:T(8,128)S(1)} %get-tuple-element.39.slots_ref, bf16[8,64,1024]{2,1,0:T(8,128)(2,1)S(1)} %get-tuple-element.29.rest_0_, bf16[8,64,1024]{2,1,0:T(8,128)(2,1)S(1)} %get-tuple-element.30.rest_1_, f32[8,64,128]{2,1,0:T(8,128)S(1)} %get-tuple-element.31.rest_2_, ...), custom_call_target="tpu_custom_call" | custom-call | tf_op jit(solution)/shard_map/block_outputs/pallas_call | solution.py:269
  22.2 2.0 %collective-permute-done.8.refs_3_ = bf16[32,1024]{1,0:T(8,128)(2,1)S(1)} collective-permute-done((bf16[32,1024]{1,0:T(8,128)(2,1)S(1)}, bf16[32,1024]{1,0:T(8,128)(2,1)S(1)}, u32[]{:S(2)}, u32[]{:S(2)}) %collective-permute-start.8) | collective-permute-done | bytes 65568 | tf_op jit(solution)/shard_map/ppermute | solution.py:47
  24.2 0.8 %join_pieces.1 = bf16[32,4096]{1,0:T(8,128)(2,1)} custom-call(bf16[32,1024]{1,0:T(8,128)(2,1)S(1)} %get-tuple-element.35.refs_0_, bf16[32,1024]{1,0:T(8,128)(2,1)S(1)} %collective-permute-done.5.refs_1_, bf16[32,1024]{1,0:T(8,128)(2,1)S(1)} %block_outputs.4.refs_2_, bf16[32,1024]{1,0:T(8,128)(2,1)S(1)} %collective-permute-done.8.refs_3_), custom_call_target="tpu_custom_call" | custom-call | tf_op jit(solution)/shard_map/join_pieces/pallas_call | solution.py:311
  (24 shorter events, 0.4 us)
Async XLA Ops:
  1.1 10.2 %collective-permute-start = (bf16[8,128,128]{2,1,0:T(8,128)(2,1)S(1)}, bf16[8,128,128]{2,1,0:T(8,128)(2,1)S(1)}, u32[]{:S(2)}, u32[]{:S(2)}) collective-permute-start(bf16[8,128,128]{2,1,0:T(8,128)(2,1)S(1)} %key_kernel.1._.rest_0_), channel_id=1, source_target_pairs={{4,0},{13,1},{6,2},{15,3},{0,4},{9,5},{2,6},{11,7},{12,8},{5,9},{1... | collective-permute-start | bytes 786440 | tf_op jit(solution)/shard_map/ppermute | solution.py:39
  5.5 9.0 %collective-permute-start.3 = (bf16[4,128,128]{2,1,0:T(8,128)(2,1)S(1)}, bf16[4,128,128]{2,1,0:T(8,128)(2,1)S(1)}, u32[]{:S(2)}, u32[]{:S(2)}) collective-permute-start(bf16[4,128,128]{2,1,0:T(8,128)(2,1)S(1)} %get-tuple-element.33.rest_4_), channel_id=1, source_target_pairs={{4,0},{13,1},{6,2},{15,3},{0,4},{9,5},{2,6},{11,7},{12,8},{5,9},{1... | collective-permute-start | bytes 393224 | tf_op jit(solution)/shard_map/ppermute | solution.py:39
  5.6 11.4 %collective-permute-start.6 = (bf16[4,128,128]{2,1,0:T(8,128)(2,1)S(1)}, bf16[4,128,128]{2,1,0:T(8,128)(2,1)S(1)}, u32[]{:S(2)}, u32[]{:S(2)}) collective-permute-start(bf16[4,128,128]{2,1,0:T(8,128)(2,1)S(1)} %get-tuple-element.37.rest_4_), channel_id=1, source_target_pairs={{4,0},{13,1},{6,2},{15,3},{0,4},{9,5},{2,6},{11,7},{12,8},{5,9},{1... | collective-permute-start | bytes 393224 | tf_op jit(solution)/shard_map/ppermute | solution.py:39
  11.4 1.6 %collective-permute-start.1 = (bf16[8,80,128]{2,1,0:T(8,128)(2,1)S(1)}, bf16[8,80,128]{2,1,0:T(8,128)(2,1)S(1)}, u32[]{:S(2)}, u32[]{:S(2)}) collective-permute-start(bf16[8,80,128]{2,1,0:T(8,128)(2,1)S(1)} %get-tuple-element.26), channel_id=1, source_target_pairs={{0,1},{1,0},{2,3},{3,2},{4,5},{5,4},{6,7},{7,6},{8,9},{9,8},{10,11... | collective-permute-start | bytes 491528 | tf_op jit(solution)/shard_map/ppermute | solution.py:47
  11.9 1.5 %collective-permute-start.2 = (bf16[8,128,128]{2,1,0:T(8,128)(2,1)S(1)}, bf16[8,128,128]{2,1,0:T(8,128)(2,1)S(1)}, u32[]{:S(2)}, u32[]{:S(2)}) collective-permute-start(bf16[8,128,128]{2,1,0:T(8,128)(2,1)S(1)} %collective-permute-done.rest_1_), channel_id=1, source_target_pairs={{0,1},{1,0},{2,3},{3,2},{4,5},{5,4},{6,7},{7,6},{8,9},{9,8},{10,11... | collective-permute-start | bytes 786440 | tf_op jit(solution)/shard_map/ppermute | solution.py:47
  14.5 1.4 %collective-permute-start.4 = (bf16[4,128,128]{2,1,0:T(8,128)(2,1)S(1)}, bf16[4,128,128]{2,1,0:T(8,128)(2,1)S(1)}, u32[]{:S(2)}, u32[]{:S(2)}) collective-permute-start(bf16[4,128,128]{2,1,0:T(8,128)(2,1)S(1)} %collective-permute-done.3.rest_5_), channel_id=1, source_target_pairs={{0,1},{1,0},{2,3},{3,2},{4,5},{5,4},{6,7},{7,6},{8,9},{9,8},{10,11... | collective-permute-start | bytes 393224 | tf_op jit(solution)/shard_map/ppermute | solution.py:47
  17.0 2.1 %collective-permute-start.7 = (bf16[4,128,128]{2,1,0:T(8,128)(2,1)S(1)}, bf16[4,128,128]{2,1,0:T(8,128)(2,1)S(1)}, u32[]{:S(2)}, u32[]{:S(2)}) collective-permute-start(bf16[4,128,128]{2,1,0:T(8,128)(2,1)S(1)} %collective-permute-done.6.rest_5_), channel_id=1, source_target_pairs={{0,1},{1,0},{2,3},{3,2},{4,5},{5,4},{6,7},{7,6},{8,9},{9,8},{10,11... | collective-permute-start | bytes 393224 | tf_op jit(solution)/shard_map/ppermute | solution.py:47
  17.3 4.9 %collective-permute-start.5 = (bf16[32,1024]{1,0:T(8,128)(2,1)S(1)}, bf16[32,1024]{1,0:T(8,128)(2,1)S(1)}, u32[]{:S(2)}, u32[]{:S(2)}) collective-permute-start(bf16[32,1024]{1,0:T(8,128)(2,1)S(1)} %get-tuple-element.36), channel_id=1, source_target_pairs={{0,3},{1,2},{2,1},{3,0},{4,7},{5,6},{6,5},{7,4},{8,11},{9,10},{10,... | collective-permute-start | bytes 196616 | tf_op jit(solution)/shard_map/ppermute | solution.py:47
  20.1 4.1 %collective-permute-start.8 = (bf16[32,1024]{1,0:T(8,128)(2,1)S(1)}, bf16[32,1024]{1,0:T(8,128)(2,1)S(1)}, u32[]{:S(2)}, u32[]{:S(2)}) collective-permute-start(bf16[32,1024]{1,0:T(8,128)(2,1)S(1)} %block_outputs.5), channel_id=1, source_target_pairs={{0,3},{1,2},{2,1},{3,0},{4,7},{5,6},{6,5},{7,4},{8,11},{9,10},{10,... | collective-permute-start | bytes 196616 | tf_op jit(solution)/shard_map/ppermute | solution.py:47

commit v8 on v7

--- a/solution.py
+++ b/solution.py
@@ -11,6 +11,7 @@
 GROUP = 16
 BLOCK = 128
 ROW_TILE = 16
+ABREAST = 2
 ROPE_BASE = 500000.0
 VMEM_GRANT = 16 * 2**20
 
@@ -189,10 +190,11 @@
     gather_parts(parts, store)
     for head in range(heads):
         turned = queries_ref[head, :rows]
-        scores = [
-            jnp.dot(turned, store[slots[head, i]], preferred_element_type=jnp.float32)
-            for i in range(picks)
-        ]
+        scores = []
+        for i in range(0, picks, ABREAST):
+            wide = jnp.concatenate([store[slots[head, i + j]] for j in range(ABREAST)], axis=1)
+            wide = jnp.dot(turned, wide, preferred_element_type=jnp.float32)
+            scores += [wide[:, j * BLOCK : (j + 1) * BLOCK] for j in range(ABREAST)]
         top = scores[0]
         for i in range(1, picks):
             top = jnp.maximum(top, scores[i])

time: 25.2 us -> 25.1 us (level)
  Pallas kernels: 8.44 us -> 8.11 us
    pallas_call x2, Pallas kernels: 2.02 us -> 1.69 us  [block_weights(): pl.pallas_call(functools.partial(score_kernel, inputs=len(parts)), in_spe...]
  transfers between devices with their start and end apart: 9 -> 9, of which waited for: 4 -> 5; matrix products, arithmetic and copies ran while one was open for 3% -> 3% of each run, Pallas kernels for 26% -> 25%
where the time goes in v8:
time: 25.1 us; the launch traced here: 25 us
  starting transfers between devices  9.44 us (38%)
  Pallas kernels  8.11 us (32%)
  waiting for transfers between devices  6.43 us (26%)
  other arithmetic  0.54 us (2%)
  local copies, waits for them, and re-layouts  0.27 us (1%)
    ppermute x3, starting transfers between devices, sent(): return lax.ppermute(x, ('ctx', 'head'), moves)  5.18 us
    ppermute x6, starting transfers between devices, swapped(): lax.ppermute(x, 'head', [(i, i ^ mask) for i in range(lax.axis_size('head...  4.26 us
    ppermute x6, waiting for transfers between devices, swapped(): lax.ppermute(x, 'head', [(i, i ^ mask) for i in range(lax.axis_size('head...  3.57 us
    pallas_call x3, Pallas kernels, block_outputs(): pl.pallas_call(functools.partial(value_kernel, inputs=len(parts), flip=fl...  3.01 us
    ppermute x3, waiting for transfers between devices, sent(): return lax.ppermute(x, ('ctx', 'head'), moves)  2.86 us
    pallas_call x2, Pallas kernels, begin(): pl.pallas_call(kernel, in_specs=[pl.BlockSpec(memory_space=pltpu.HBM)] *...  2.37 us
    pallas_call x2, Pallas kernels, block_weights(): pl.pallas_call(functools.partial(score_kernel, inputs=len(parts)), in_spe...  1.69 us
    pallas_call x1, Pallas kernels, join_pieces(): pl.pallas_call(functools.partial(join_kernel, share=share, width=width),...  0.82 us
  transfers between devices with their start and end apart: 9, of which 5 were waited for; matrix products, arithmetic and copies ran while one was open for 3% of the time, Pallas kernels for 25%

profile of v8, /device:TPU:0, one launch (start us, length us, event | category | flops | bytes accessed | tf_op | source)
XLA Modules:
  0.0 25.0 jit_solution(4244935974958394607)
XLA Ops:
  0.0 1.1 %key_kernel.1._.rest_0_ = bf16[8,128,128]{2,1,0:T(8,128)(2,1)S(1)} custom-call(s32[2,2,8]{2,1,0:T(2,128)} %index_hbm.3, f32[2,16]{1,0:T(2,128)} %table_hbm.3, bf16[2,1024,128]{2,1,0:T(8,128)(2,1)} %codes_hbm.2), custom_call_target="tpu_custom_call" | custom-call | tf_op jit(solution)/shard_map/key_kernel/pallas_call | solution.py:118
  1.1 3.1 %collective-permute-start = (bf16[8,128,128]{2,1,0:T(8,128)(2,1)S(1)}, bf16[8,128,128]{2,1,0:T(8,128)(2,1)S(1)}, u32[]{:S(2)}, u32[]{:S(2)}) collective-permute-start(bf16[8,128,128]{2,1,0:T(8,128)(2,1)S(1)} %key_kernel.1._.rest_0_), channel_id=1, source_target_pairs={{4,0},{13,1},{6,2},{15,3},{0,4},{9,5},{2,6},{11,7},{12,8},{5,9},{1... | collective-permute-start | bytes 786440 | tf_op jit(solution)/shard_map/ppermute | solution.py:40
  4.2 1.3 %half_kernel.1 = (bf16[4,128,128]{2,1,0:T(8,128)(2,1)S(1)}, bf16[4,128,128]{2,1,0:T(8,128)(2,1)S(1)}, bf16[128,8,128]{2,1,0:T(8,128)(2,1)S(1)}, s32[128]{0:T(128)S(1)}, s32[8,4,8]{2,1,0:T(4,128)S(1)}) custom-call(s32[2,2,8]{2,1,0:T(2,128)} %index_hbm.3, f32[2,16]{1,0:T(2,128)} %table_hbm.3, bf16[2,1024,128]{2,1,0:T(8,128)(2,1)} %codes_hbm.3, ...), custom_call_target="tpu_custom_call" | custom-call | tf_op jit(solution)/shard_map/half_kernel/pallas_call | solution.py:118
  5.5 0.1 collective-permute-start.3
  5.6 2.0 %collective-permute-start.6 = (bf16[4,128,128]{2,1,0:T(8,128)(2,1)S(1)}, bf16[4,128,128]{2,1,0:T(8,128)(2,1)S(1)}, u32[]{:S(2)}, u32[]{:S(2)}) collective-permute-start(bf16[4,128,128]{2,1,0:T(8,128)(2,1)S(1)} %get-tuple-element.37.rest_4_), channel_id=1, source_target_pairs={{4,0},{13,1},{6,2},{15,3},{0,4},{9,5},{2,6},{11,7},{12,8},{5,9},{1... | collective-permute-start | bytes 393224 | tf_op jit(solution)/shard_map/ppermute | solution.py:40
  7.9 0.1 convert_element_type.29
  8.0 0.3 %fusion = (f32[128,128]{1,0:T(8,128)S(1)}, f32[128,128]{1,0:T(8,128)S(1)}) fusion(f32[128]{0:T(128)S(1)} %get-tuple-element.54, f32[128]{0:T(128)S(1)} %get-tuple-element.55, f32[128]{0:T(128)S(1)} %convert_element_type.29), kind=kLoop, calls=%fused_computation.3 | loop fusion | flops 32768 | bytes 132608 | tf_op jit(solution)/shard_map/mul | solution.py:374
  8.3 0.2 turn_queries.1
  8.5 2.9 %collective-permute-done.rest_1_ = bf16[8,128,128]{2,1,0:T(8,128)(2,1)S(1)} collective-permute-done((bf16[8,128,128]{2,1,0:T(8,128)(2,1)S(1)}, bf16[8,128,128]{2,1,0:T(8,128)(2,1)S(1)}, u32[]{:S(2)}, u32[]{:S(2)}) %collective-permute-start) | collective-permute-done | bytes 262176 | tf_op jit(solution)/shard_map/ppermute | solution.py:40
  11.4 0.5 %collective-permute-start.1 = (bf16[8,80,128]{2,1,0:T(8,128)(2,1)S(1)}, bf16[8,80,128]{2,1,0:T(8,128)(2,1)S(1)}, u32[]{:S(2)}, u32[]{:S(2)}) collective-permute-start(bf16[8,80,128]{2,1,0:T(8,128)(2,1)S(1)} %get-tuple-element.26), channel_id=1, source_target_pairs={{0,1},{1,0},{2,3},{3,2},{4,5},{5,4},{6,7},{7,6},{8,9},{9,8},{10,11... | collective-permute-start | bytes 491528 | tf_op jit(solution)/shard_map/ppermute | solution.py:48
  12.0 1.0 %collective-permute-done.1.queries_ref = bf16[8,80,128]{2,1,0:T(8,128)(2,1)S(1)} collective-permute-done((bf16[8,80,128]{2,1,0:T(8,128)(2,1)S(1)}, bf16[8,80,128]{2,1,0:T(8,128)(2,1)S(1)}, u32[]{:S(2)}, u32[]{:S(2)}) %collective-permute-start.1) | collective-permute-done | bytes 163872 | tf_op jit(solution)/shard_map/ppermute | solution.py:48
  13.0 0.4 %collective-permute-done.2.rest_2_ = bf16[8,128,128]{2,1,0:T(8,128)(2,1)S(1)} collective-permute-done((bf16[8,128,128]{2,1,0:T(8,128)(2,1)S(1)}, bf16[8,128,128]{2,1,0:T(8,128)(2,1)S(1)}, u32[]{:S(2)}, u32[]{:S(2)}) %collective-permute-start.2) | collective-permute-done | bytes 262176 | tf_op jit(solution)/shard_map/ppermute | solution.py:48
  13.4 0.8 %block_weights.2 = (bf16[8,64,1024]{2,1,0:T(8,128)(2,1)S(1)}, f32[8,64,128]{2,1,0:T(8,128)S(1)}) custom-call(s32[8,8]{1,0:T(8,128)S(1)} %get-tuple-element.47.slots_ref, bf16[8,64,128]{2,1,0:T(8,128)(2,1)S(1)} %get-tuple-element.27.queries_ref, bf16[8,128,128]{2,1,0:T(8,128)(2,1)S(1)} %key_kernel.1._.rest_0_, ...), custom_call_target="tpu_custom_call" | custom-call | tf_op jit(solution)/shard_map/block_weights/pallas_call | solution.py:215
  14.3 0.4 %collective-permute-start.4 = (bf16[4,128,128]{2,1,0:T(8,128)(2,1)S(1)}, bf16[4,128,128]{2,1,0:T(8,128)(2,1)S(1)}, u32[]{:S(2)}, u32[]{:S(2)}) collective-permute-start(bf16[4,128,128]{2,1,0:T(8,128)(2,1)S(1)} %collective-permute-done.3.rest_5_), channel_id=1, source_target_pairs={{0,1},{1,0},{2,3},{3,2},{4,5},{5,4},{6,7},{7,6},{8,9},{9,8},{10,11... | collective-permute-start | bytes 393224 | tf_op jit(solution)/shard_map/ppermute | solution.py:48
  14.8 0.8 %block_weights.3 = (bf16[8,64,1024]{2,1,0:T(8,128)(2,1)S(1)}, f32[8,64,128]{2,1,0:T(8,128)S(1)}) custom-call(s32[8,8]{1,0:T(8,128)S(1)} %get-tuple-element.46.slots_ref, bf16[8,80,128]{2,1,0:T(8,128)(2,1)S(1)} %collective-permute-done.1.queries_ref, bf16[8,128,128]{2,1,0:T(8,128)(2,1)S(1)} %key_kernel.1._.rest_0_, ...), custom_call_target="tpu_custom_call" | custom-call | tf_op jit(solution)/shard_map/block_weights/pallas_call | solution.py:215
  15.6 0.1 collective-permute-done.4.rest_6_
  15.7 1.1 %block_outputs.3 = (bf16[32,1024]{1,0:T(8,128)(2,1)S(1)}, bf16[32,1024]{1,0:T(8,128)(2,1)S(1)}) custom-call(s32[16,8]{1,0:T(8,128)S(1)} %multiply_add_fusion.1.slots_ref, bf16[8,64,1024]{2,1,0:T(8,128)(2,1)S(1)} %get-tuple-element.29.rest_0_, bf16[8,64,1024]{2,1,0:T(8,128)(2,1)S(1)} %get-tuple-element.30.rest_1_, ...), custom_call_target="tpu_custom_call" | custom-call | tf_op jit(solution)/shard_map/block_outputs/pallas_call | solution.py:271
  16.8 0.4 %collective-permute-start.7 = (bf16[4,128,128]{2,1,0:T(8,128)(2,1)S(1)}, bf16[4,128,128]{2,1,0:T(8,128)(2,1)S(1)}, u32[]{:S(2)}, u32[]{:S(2)}) collective-permute-start(bf16[4,128,128]{2,1,0:T(8,128)(2,1)S(1)} %collective-permute-done.6.rest_5_), channel_id=1, source_target_pairs={{0,1},{1,0},{2,3},{3,2},{4,5},{5,4},{6,7},{7,6},{8,9},{9,8},{10,11... | collective-permute-start | bytes 393224 | tf_op jit(solution)/shard_map/ppermute | solution.py:48
  17.2 1.8 %collective-permute-start.5 = (bf16[32,1024]{1,0:T(8,128)(2,1)S(1)}, bf16[32,1024]{1,0:T(8,128)(2,1)S(1)}, u32[]{:S(2)}, u32[]{:S(2)}) collective-permute-start(bf16[32,1024]{1,0:T(8,128)(2,1)S(1)} %get-tuple-element.36), channel_id=1, source_target_pairs={{0,3},{1,2},{2,1},{3,0},{4,7},{5,6},{6,5},{7,4},{8,11},{9,10},{10,... | collective-permute-start | bytes 196616 | tf_op jit(solution)/shard_map/ppermute | solution.py:48
  19.0 1.0 %block_outputs.5 = bf16[32,1024]{1,0:T(8,128)(2,1)S(1)} custom-call(s32[16,8]{1,0:T(8,128)S(1)} %get-tuple-element.39.slots_ref, bf16[8,64,1024]{2,1,0:T(8,128)(2,1)S(1)} %get-tuple-element.29.rest_0_, bf16[8,64,1024]{2,1,0:T(8,128)(2,1)S(1)} %get-tuple-element.30.rest_1_, f32[8,64,128]{2,1,0:T(8,128)S(1)} %get-tuple-element.31.rest_2_, ...), custom_call_target="tpu_custom_call" | custom-call | tf_op jit(solution)/shard_map/block_outputs/pallas_call | solution.py:271
  20.0 1.0 %collective-permute-start.8 = (bf16[32,1024]{1,0:T(8,128)(2,1)S(1)}, bf16[32,1024]{1,0:T(8,128)(2,1)S(1)}, u32[]{:S(2)}, u32[]{:S(2)}) collective-permute-start(bf16[32,1024]{1,0:T(8,128)(2,1)S(1)} %block_outputs.5), channel_id=1, source_target_pairs={{0,3},{1,2},{2,1},{3,0},{4,7},{5,6},{6,5},{7,4},{8,11},{9,10},{10,... | collective-permute-start | bytes 196616 | tf_op jit(solution)/shard_map/ppermute | solution.py:48
  21.1 1.0 %block_outputs.4.refs_2_ = bf16[32,1024]{1,0:T(8,128)(2,1)S(1)} custom-call(s32[16,8]{1,0:T(8,128)S(1)} %get-tuple-element.39.slots_ref, bf16[8,64,1024]{2,1,0:T(8,128)(2,1)S(1)} %get-tuple-element.29.rest_0_, bf16[8,64,1024]{2,1,0:T(8,128)(2,1)S(1)} %get-tuple-element.30.rest_1_, f32[8,64,128]{2,1,0:T(8,128)S(1)} %get-tuple-element.31.rest_2_, ...), custom_call_target="tpu_custom_call" | custom-call | tf_op jit(solution)/shard_map/block_outputs/pallas_call | solution.py:271
  22.1 2.1 %collective-permute-done.8.refs_3_ = bf16[32,1024]{1,0:T(8,128)(2,1)S(1)} collective-permute-done((bf16[32,1024]{1,0:T(8,128)(2,1)S(1)}, bf16[32,1024]{1,0:T(8,128)(2,1)S(1)}, u32[]{:S(2)}, u32[]{:S(2)}) %collective-permute-start.8) | collective-permute-done | bytes 65568 | tf_op jit(solution)/shard_map/ppermute | solution.py:48
  24.1 0.8 %join_pieces.1 = bf16[32,4096]{1,0:T(8,128)(2,1)} custom-call(bf16[32,1024]{1,0:T(8,128)(2,1)S(1)} %get-tuple-element.35.refs_0_, bf16[32,1024]{1,0:T(8,128)(2,1)S(1)} %collective-permute-done.5.refs_1_, bf16[32,1024]{1,0:T(8,128)(2,1)S(1)} %block_outputs.4.refs_2_, bf16[32,1024]{1,0:T(8,128)(2,1)S(1)} %collective-permute-done.8.refs_3_), custom_call_target="tpu_custom_call" | custom-call | tf_op jit(solution)/shard_map/join_pieces/pallas_call | solution.py:313
  (24 shorter events, 0.5 us)
Async XLA Ops:
  1.1 10.2 %collective-permute-start = (bf16[8,128,128]{2,1,0:T(8,128)(2,1)S(1)}, bf16[8,128,128]{2,1,0:T(8,128)(2,1)S(1)}, u32[]{:S(2)}, u32[]{:S(2)}) collective-permute-start(bf16[8,128,128]{2,1,0:T(8,128)(2,1)S(1)} %key_kernel.1._.rest_0_), channel_id=1, source_target_pairs={{4,0},{13,1},{6,2},{15,3},{0,4},{9,5},{2,6},{11,7},{12,8},{5,9},{1... | collective-permute-start | bytes 786440 | tf_op jit(solution)/shard_map/ppermute | solution.py:40
  5.5 8.8 %collective-permute-start.3 = (bf16[4,128,128]{2,1,0:T(8,128)(2,1)S(1)}, bf16[4,128,128]{2,1,0:T(8,128)(2,1)S(1)}, u32[]{:S(2)}, u32[]{:S(2)}) collective-permute-start(bf16[4,128,128]{2,1,0:T(8,128)(2,1)S(1)} %get-tuple-element.33.rest_4_), channel_id=1, source_target_pairs={{4,0},{13,1},{6,2},{15,3},{0,4},{9,5},{2,6},{11,7},{12,8},{5,9},{1... | collective-permute-start | bytes 393224 | tf_op jit(solution)/shard_map/ppermute | solution.py:40
  5.6 11.3 %collective-permute-start.6 = (bf16[4,128,128]{2,1,0:T(8,128)(2,1)S(1)}, bf16[4,128,128]{2,1,0:T(8,128)(2,1)S(1)}, u32[]{:S(2)}, u32[]{:S(2)}) collective-permute-start(bf16[4,128,128]{2,1,0:T(8,128)(2,1)S(1)} %get-tuple-element.37.rest_4_), channel_id=1, source_target_pairs={{4,0},{13,1},{6,2},{15,3},{0,4},{9,5},{2,6},{11,7},{12,8},{5,9},{1... | collective-permute-start | bytes 393224 | tf_op jit(solution)/shard_map/ppermute | solution.py:40
  11.4 1.6 %collective-permute-start.1 = (bf16[8,80,128]{2,1,0:T(8,128)(2,1)S(1)}, bf16[8,80,128]{2,1,0:T(8,128)(2,1)S(1)}, u32[]{:S(2)}, u32[]{:S(2)}) collective-permute-start(bf16[8,80,128]{2,1,0:T(8,128)(2,1)S(1)} %get-tuple-element.26), channel_id=1, source_target_pairs={{0,1},{1,0},{2,3},{3,2},{4,5},{5,4},{6,7},{7,6},{8,9},{9,8},{10,11... | collective-permute-start | bytes 491528 | tf_op jit(solution)/shard_map/ppermute | solution.py:48
  11.9 1.5 %collective-permute-start.2 = (bf16[8,128,128]{2,1,0:T(8,128)(2,1)S(1)}, bf16[8,128,128]{2,1,0:T(8,128)(2,1)S(1)}, u32[]{:S(2)}, u32[]{:S(2)}) collective-permute-start(bf16[8,128,128]{2,1,0:T(8,128)(2,1)S(1)} %collective-permute-done.rest_1_), channel_id=1, source_target_pairs={{0,1},{1,0},{2,3},{3,2},{4,5},{5,4},{6,7},{7,6},{8,9},{9,8},{10,11... | collective-permute-start | bytes 786440 | tf_op jit(solution)/shard_map/ppermute | solution.py:48
  14.3 1.4 %collective-permute-start.4 = (bf16[4,128,128]{2,1,0:T(8,128)(2,1)S(1)}, bf16[4,128,128]{2,1,0:T(8,128)(2,1)S(1)}, u32[]{:S(2)}, u32[]{:S(2)}) collective-permute-start(bf16[4,128,128]{2,1,0:T(8,128)(2,1)S(1)} %collective-permute-done.3.rest_5_), channel_id=1, source_target_pairs={{0,1},{1,0},{2,3},{3,2},{4,5},{5,4},{6,7},{7,6},{8,9},{9,8},{10,11... | collective-permute-start | bytes 393224 | tf_op jit(solution)/shard_map/ppermute | solution.py:48
  16.8 2.2 %collective-permute-start.7 = (bf16[4,128,128]{2,1,0:T(8,128)(2,1)S(1)}, bf16[4,128,128]{2,1,0:T(8,128)(2,1)S(1)}, u32[]{:S(2)}, u32[]{:S(2)}) collective-permute-start(bf16[4,128,128]{2,1,0:T(8,128)(2,1)S(1)} %collective-permute-done.6.rest_5_), channel_id=1, source_target_pairs={{0,1},{1,0},{2,3},{3,2},{4,5},{5,4},{6,7},{7,6},{8,9},{9,8},{10,11... | collective-permute-start | bytes 393224 | tf_op jit(solution)/shard_map/ppermute | solution.py:48
  17.2 4.8 %collective-permute-start.5 = (bf16[32,1024]{1,0:T(8,128)(2,1)S(1)}, bf16[32,1024]{1,0:T(8,128)(2,1)S(1)}, u32[]{:S(2)}, u32[]{:S(2)}) collective-permute-start(bf16[32,1024]{1,0:T(8,128)(2,1)S(1)} %get-tuple-element.36), channel_id=1, source_target_pairs={{0,3},{1,2},{2,1},{3,0},{4,7},{5,6},{6,5},{7,4},{8,11},{9,10},{10,... | collective-permute-start | bytes 196616 | tf_op jit(solution)/shard_map/ppermute | solution.py:48
  20.0 4.1 %collective-permute-start.8 = (bf16[32,1024]{1,0:T(8,128)(2,1)S(1)}, bf16[32,1024]{1,0:T(8,128)(2,1)S(1)}, u32[]{:S(2)}, u32[]{:S(2)}) collective-permute-start(bf16[32,1024]{1,0:T(8,128)(2,1)S(1)} %block_outputs.5), channel_id=1, source_target_pairs={{0,3},{1,2},{2,1},{3,0},{4,7},{5,6},{6,5},{7,4},{8,11},{9,10},{10,... | collective-permute-start | bytes 196616 | tf_op jit(solution)/shard_map/ppermute | solution.py:48

commit v9 on v8

--- a/solution.py
+++ b/solution.py
@@ -76,7 +76,7 @@
     codes_ref = scratch[2]
     for block, scale in enumerate(fetch(index_hbm, table_hbm, codes_hbm, *scratch, 0)):
         codes = codes_ref[block * BLOCK : (block + 1) * BLOCK, :].astype(jnp.float32)
-        out_ref[block] = (codes * scale).T.astype(jnp.bfloat16)
+        out_ref[block] = (codes * scale).astype(jnp.bfloat16)
 
 
 def half_kernel(index_hbm, table_hbm, codes_hbm, _, *rest):
@@ -173,21 +173,18 @@
     )(queries, cosine, sine, lists)
 
 
-def gather_parts(parts, store):
-    at = 0
-    for part in parts:
-        store[at : at + part.shape[0]] = part[...]
-        at += part.shape[0]
-
-
 def score_kernel(slots_ref, queries_ref, *rest, inputs):
     parts = rest[:inputs]
-    weights_ref, total_ref, store = rest[-3:]
+    weights_ref, total_ref, store = rest[inputs : inputs + 3]
     heads, rows, width = total_ref.shape
     picks = slots_ref.shape[1]
     slots = slots_ref[...]
     factor = math.log2(math.e) / math.sqrt(width)
-    gather_parts(parts, store)
+    at = 0
+    for part in parts:
+        for block in range(part.shape[0]):
+            store[at] = part[block].astype(jnp.float32).T.astype(jnp.bfloat16)
+            at += 1
     for head in range(heads):
         turned = queries_ref[head, :rows]
         scores = []
@@ -208,22 +205,28 @@
         total_ref[head] = jnp.broadcast_to(1.0 / total, (rows, width))
 
 
-def block_weights(slots, queries, parts, rows, *extra):
+def held_kernel(slots_ref, queries_ref, store, weights_ref, total_ref):
+    score_kernel(slots_ref, queries_ref, weights_ref, total_ref, store, inputs=0)
+
+
+def block_weights(slots, queries, parts, rows):
     width = queries.shape[2]
     heads, picks = slots.shape
     blocks = sum(part.shape[0] for part in parts)
+    outputs = [
+        jax.ShapeDtypeStruct((heads, rows, picks * BLOCK), jnp.bfloat16),
+        jax.ShapeDtypeStruct((heads, rows, width), jnp.float32),
+    ]
+    if len(parts) > 1:
+        outputs.append(jax.ShapeDtypeStruct((blocks, width, BLOCK), jnp.bfloat16))
     return pl.pallas_call(
-        functools.partial(score_kernel, inputs=len(parts)),
-        in_specs=[in_vmem] * (2 + len(parts) + len(extra)),
-        out_specs=[in_vmem, in_vmem],
-        out_shape=[
-            jax.ShapeDtypeStruct((heads, rows, picks * BLOCK), jnp.bfloat16),
-            jax.ShapeDtypeStruct((heads, rows, width), jnp.float32),
-        ],
-        scratch_shapes=[pltpu.VMEM((blocks, width, BLOCK), jnp.bfloat16)],
+        functools.partial(score_kernel, inputs=len(parts)) if len(parts) > 1 else held_kernel,
+        in_specs=[in_vmem] * (2 + len(parts)),
+        out_specs=[in_vmem] * len(outputs),
+        out_shape=outputs,
         compiler_params=granted,
         name="block_weights",
-    )(slots, queries, *parts, *extra)
+    )(slots, queries, *parts)
 
 
 def value_kernel(slots_ref, *rest, inputs, flip, first, last):
@@ -396,8 +399,8 @@
         far_values = [sent(half, share, pairs) for half in far_values]
         steps.append(far_values)
     rows = rows_dev // share
-    own_weights, own_total = block_weights(slots[:heads_dev], own, key_parts, rows)
-    sibling_weights, sibling_total = block_weights(slots[heads_dev:], sibling, key_parts, rows)
+    own_weights, own_total, held = block_weights(slots[:heads_dev], own, key_parts, rows)
+    sibling_weights, sibling_total = block_weights(slots[heads_dev:], sibling, [held], rows)
     weights = (own_weights, sibling_weights)
     totals = (own_total, sibling_total)
 

time: 25.1 us -> 25 us (level)
  transfers between devices with their start and end apart: 9 -> 9, of which waited for: 5 -> 5; matrix products, arithmetic and copies ran while one was open for 3% -> 3% of each run, Pallas kernels for 25% -> 26%
where the time goes in v9:
time: 25 us; the launch traced here: 24.9 us
  starting transfers between devices  9.29 us (37%)
  Pallas kernels  8.23 us (33%)
  waiting for transfers between devices  6.37 us (25%)
  other arithmetic  0.54 us (2%)
  local copies, waits for them, and re-layouts  0.26 us (1%)
    ppermute x3, starting transfers between devices, sent(): return lax.ppermute(x, ('ctx', 'head'), moves)  5.18 us
    ppermute x6, starting transfers between devices, swapped(): lax.ppermute(x, 'head', [(i, i ^ mask) for i in range(lax.axis_size('head...  4.11 us
    ppermute x6, waiting for transfers between devices, swapped(): lax.ppermute(x, 'head', [(i, i ^ mask) for i in range(lax.axis_size('head...  3.49 us
    pallas_call x3, Pallas kernels, block_outputs(): pl.pallas_call(functools.partial(value_kernel, inputs=len(parts), flip=fl...  3.02 us
    ppermute x3, waiting for transfers between devices, sent(): return lax.ppermute(x, ('ctx', 'head'), moves)  2.88 us
    pallas_call x2, Pallas kernels, begin(): pl.pallas_call(kernel, in_specs=[pl.BlockSpec(memory_space=pltpu.HBM)] *...  2.28 us
    pallas_call x2, Pallas kernels, block_weights(): pl.pallas_call(functools.partial(score_kernel, inputs=len(parts)) if len(...  1.91 us
    pallas_call x1, Pallas kernels, join_pieces(): pl.pallas_call(functools.partial(join_kernel, share=share, width=width),...  0.82 us
  transfers between devices with their start and end apart: 9, of which 5 were waited for; matrix products, arithmetic and copies ran while one was open for 3% of the time, Pallas kernels for 26%

profile of v9, /device:TPU:0, one launch (start us, length us, event | category | flops | bytes accessed | tf_op | source)
XLA Modules:
  0.0 24.9 jit_solution(9215576147560453592)
XLA Ops:
  0.0 1.0 %key_kernel.1._.rest_0_ = bf16[8,128,128]{2,1,0:T(8,128)(2,1)S(1)} custom-call(s32[2,2,8]{2,1,0:T(2,128)} %index_hbm.3, f32[2,16]{1,0:T(2,128)} %table_hbm.3, bf16[2,1024,128]{2,1,0:T(8,128)(2,1)} %codes_hbm.2), custom_call_target="tpu_custom_call" | custom-call | tf_op jit(solution)/shard_map/key_kernel/pallas_call | solution.py:118
  1.0 3.1 %collective-permute-start = (bf16[8,128,128]{2,1,0:T(8,128)(2,1)S(1)}, bf16[8,128,128]{2,1,0:T(8,128)(2,1)S(1)}, u32[]{:S(2)}, u32[]{:S(2)}) collective-permute-start(bf16[8,128,128]{2,1,0:T(8,128)(2,1)S(1)} %key_kernel.1._.rest_0_), channel_id=1, source_target_pairs={{4,0},{13,1},{6,2},{15,3},{0,4},{9,5},{2,6},{11,7},{12,8},{5,9},{1... | collective-permute-start | bytes 786440 | tf_op jit(solution)/shard_map/ppermute | solution.py:40
  4.1 1.3 %half_kernel.1 = (bf16[4,128,128]{2,1,0:T(8,128)(2,1)S(1)}, bf16[4,128,128]{2,1,0:T(8,128)(2,1)S(1)}, bf16[128,8,128]{2,1,0:T(8,128)(2,1)S(1)}, s32[128]{0:T(128)S(1)}, s32[8,4,8]{2,1,0:T(4,128)S(1)}) custom-call(s32[2,2,8]{2,1,0:T(2,128)} %index_hbm.3, f32[2,16]{1,0:T(2,128)} %table_hbm.3, bf16[2,1024,128]{2,1,0:T(8,128)(2,1)} %codes_hbm.3, ...), custom_call_target="tpu_custom_call" | custom-call | tf_op jit(solution)/shard_map/half_kernel/pallas_call | solution.py:118
  5.4 0.1 collective-permute-start.3
  5.5 2.0 %collective-permute-start.6 = (bf16[4,128,128]{2,1,0:T(8,128)(2,1)S(1)}, bf16[4,128,128]{2,1,0:T(8,128)(2,1)S(1)}, u32[]{:S(2)}, u32[]{:S(2)}) collective-permute-start(bf16[4,128,128]{2,1,0:T(8,128)(2,1)S(1)} %get-tuple-element.39.rest_4_), channel_id=1, source_target_pairs={{4,0},{13,1},{6,2},{15,3},{0,4},{9,5},{2,6},{11,7},{12,8},{5,9},{1... | collective-permute-start | bytes 393224 | tf_op jit(solution)/shard_map/ppermute | solution.py:40
  7.8 0.1 convert_element_type.29
  7.9 0.3 %fusion = (f32[128,128]{1,0:T(8,128)S(1)}, f32[128,128]{1,0:T(8,128)S(1)}) fusion(f32[128]{0:T(128)S(1)} %get-tuple-element.56, f32[128]{0:T(128)S(1)} %get-tuple-element.57, f32[128]{0:T(128)S(1)} %convert_element_type.29), kind=kLoop, calls=%fused_computation.3 | loop fusion | flops 32768 | bytes 132608 | tf_op jit(solution)/shard_map/mul | solution.py:377
  8.2 0.2 turn_queries.1
  8.4 2.9 %collective-permute-done.rest_1_ = bf16[8,128,128]{2,1,0:T(8,128)(2,1)S(1)} collective-permute-done((bf16[8,128,128]{2,1,0:T(8,128)(2,1)S(1)}, bf16[8,128,128]{2,1,0:T(8,128)(2,1)S(1)}, u32[]{:S(2)}, u32[]{:S(2)}) %collective-permute-start) | collective-permute-done | bytes 262176 | tf_op jit(solution)/shard_map/ppermute | solution.py:40
  11.3 0.5 %collective-permute-start.1 = (bf16[8,80,128]{2,1,0:T(8,128)(2,1)S(1)}, bf16[8,80,128]{2,1,0:T(8,128)(2,1)S(1)}, u32[]{:S(2)}, u32[]{:S(2)}) collective-permute-start(bf16[8,80,128]{2,1,0:T(8,128)(2,1)S(1)} %get-tuple-element.27), channel_id=1, source_target_pairs={{0,1},{1,0},{2,3},{3,2},{4,5},{5,4},{6,7},{7,6},{8,9},{9,8},{10,11... | collective-permute-start | bytes 491528 | tf_op jit(solution)/shard_map/ppermute | solution.py:48
  11.9 1.0 %collective-permute-done.1.queries_ref = bf16[8,80,128]{2,1,0:T(8,128)(2,1)S(1)} collective-permute-done((bf16[8,80,128]{2,1,0:T(8,128)(2,1)S(1)}, bf16[8,80,128]{2,1,0:T(8,128)(2,1)S(1)}, u32[]{:S(2)}, u32[]{:S(2)}) %collective-permute-start.1) | collective-permute-done | bytes 163872 | tf_op jit(solution)/shard_map/ppermute | solution.py:48
  12.9 0.4 %collective-permute-done.2.rest_2_ = bf16[8,128,128]{2,1,0:T(8,128)(2,1)S(1)} collective-permute-done((bf16[8,128,128]{2,1,0:T(8,128)(2,1)S(1)}, bf16[8,128,128]{2,1,0:T(8,128)(2,1)S(1)}, u32[]{:S(2)}, u32[]{:S(2)}) %collective-permute-start.2) | collective-permute-done | bytes 262176 | tf_op jit(solution)/shard_map/ppermute | solution.py:48
  13.4 1.1 %block_weights.2 = (bf16[8,64,1024]{2,1,0:T(8,128)(2,1)S(1)}, f32[8,64,128]{2,1,0:T(8,128)S(1)}, bf16[24,128,128]{2,1,0:T(8,128)(2,1)S(1)}) custom-call(s32[8,8]{1,0:T(8,128)S(1)} %get-tuple-element.49.slots_ref, bf16[8,64,128]{2,1,0:T(8,128)(2,1)S(1)} %get-tuple-element.28.queries_ref, bf16[8,128,128]{2,1,0:T(8,128)(2,1)S(1)} %key_kernel.1._.rest_0_, ...), custom_call_target="tpu_custom_call" | custom-call | tf_op jit(solution)/shard_map/block_weights/pallas_call | solution.py:222
  14.4 0.3 %collective-permute-start.4 = (bf16[4,128,128]{2,1,0:T(8,128)(2,1)S(1)}, bf16[4,128,128]{2,1,0:T(8,128)(2,1)S(1)}, u32[]{:S(2)}, u32[]{:S(2)}) collective-permute-start(bf16[4,128,128]{2,1,0:T(8,128)(2,1)S(1)} %collective-permute-done.3.rest_5_), channel_id=1, source_target_pairs={{0,1},{1,0},{2,3},{3,2},{4,5},{5,4},{6,7},{7,6},{8,9},{9,8},{10,11... | collective-permute-start | bytes 393224 | tf_op jit(solution)/shard_map/ppermute | solution.py:48
  14.8 0.8 %block_weights.3 = (bf16[8,64,1024]{2,1,0:T(8,128)(2,1)S(1)}, f32[8,64,128]{2,1,0:T(8,128)S(1)}) custom-call(s32[8,8]{1,0:T(8,128)S(1)} %get-tuple-element.48.slots_ref, bf16[8,80,128]{2,1,0:T(8,128)(2,1)S(1)} %collective-permute-done.1.queries_ref, bf16[24,128,128]{2,1,0:T(8,128)(2,1)S(1)} %get-tuple-element.31.store), custom_call_target="tpu_custom_call" | custom-call | tf_op jit(solution)/shard_map/block_weights/pallas_call | solution.py:222
  15.7 0.2 collective-permute-done.4.rest_6_
  15.8 1.1 %block_outputs.3 = (bf16[32,1024]{1,0:T(8,128)(2,1)S(1)}, bf16[32,1024]{1,0:T(8,128)(2,1)S(1)}) custom-call(s32[16,8]{1,0:T(8,128)S(1)} %multiply_add_fusion.1.slots_ref, bf16[8,64,1024]{2,1,0:T(8,128)(2,1)S(1)} %get-tuple-element.30.rest_0_, bf16[8,64,1024]{2,1,0:T(8,128)(2,1)S(1)} %get-tuple-element.32.rest_1_, ...), custom_call_target="tpu_custom_call" | custom-call | tf_op jit(solution)/shard_map/block_outputs/pallas_call | solution.py:274
  16.9 0.3 %collective-permute-start.7 = (bf16[4,128,128]{2,1,0:T(8,128)(2,1)S(1)}, bf16[4,128,128]{2,1,0:T(8,128)(2,1)S(1)}, u32[]{:S(2)}, u32[]{:S(2)}) collective-permute-start(bf16[4,128,128]{2,1,0:T(8,128)(2,1)S(1)} %collective-permute-done.6.rest_5_), channel_id=1, source_target_pairs={{0,1},{1,0},{2,3},{3,2},{4,5},{5,4},{6,7},{7,6},{8,9},{9,8},{10,11... | collective-permute-start | bytes 393224 | tf_op jit(solution)/shard_map/ppermute | solution.py:48
  17.2 1.8 %collective-permute-start.5 = (bf16[32,1024]{1,0:T(8,128)(2,1)S(1)}, bf16[32,1024]{1,0:T(8,128)(2,1)S(1)}, u32[]{:S(2)}, u32[]{:S(2)}) collective-permute-start(bf16[32,1024]{1,0:T(8,128)(2,1)S(1)} %get-tuple-element.38), channel_id=1, source_target_pairs={{0,3},{1,2},{2,1},{3,0},{4,7},{5,6},{6,5},{7,4},{8,11},{9,10},{10,... | collective-permute-start | bytes 196616 | tf_op jit(solution)/shard_map/ppermute | solution.py:48
  19.0 1.0 %block_outputs.5 = bf16[32,1024]{1,0:T(8,128)(2,1)S(1)} custom-call(s32[16,8]{1,0:T(8,128)S(1)} %get-tuple-element.41.slots_ref, bf16[8,64,1024]{2,1,0:T(8,128)(2,1)S(1)} %get-tuple-element.30.rest_0_, bf16[8,64,1024]{2,1,0:T(8,128)(2,1)S(1)} %get-tuple-element.32.rest_1_, f32[8,64,128]{2,1,0:T(8,128)S(1)} %get-tuple-element.33.rest_2_, ...), custom_call_target="tpu_custom_call" | custom-call | tf_op jit(solution)/shard_map/block_outputs/pallas_call | solution.py:274
  20.0 1.2 %collective-permute-start.8 = (bf16[32,1024]{1,0:T(8,128)(2,1)S(1)}, bf16[32,1024]{1,0:T(8,128)(2,1)S(1)}, u32[]{:S(2)}, u32[]{:S(2)}) collective-permute-start(bf16[32,1024]{1,0:T(8,128)(2,1)S(1)} %block_outputs.5), channel_id=1, source_target_pairs={{0,3},{1,2},{2,1},{3,0},{4,7},{5,6},{6,5},{7,4},{8,11},{9,10},{10,... | collective-permute-start | bytes 196616 | tf_op jit(solution)/shard_map/ppermute | solution.py:48
  21.2 1.0 %block_outputs.4.refs_2_ = bf16[32,1024]{1,0:T(8,128)(2,1)S(1)} custom-call(s32[16,8]{1,0:T(8,128)S(1)} %get-tuple-element.41.slots_ref, bf16[8,64,1024]{2,1,0:T(8,128)(2,1)S(1)} %get-tuple-element.30.rest_0_, bf16[8,64,1024]{2,1,0:T(8,128)(2,1)S(1)} %get-tuple-element.32.rest_1_, f32[8,64,128]{2,1,0:T(8,128)S(1)} %get-tuple-element.33.rest_2_, ...), custom_call_target="tpu_custom_call" | custom-call | tf_op jit(solution)/shard_map/block_outputs/pallas_call | solution.py:274
  22.1 1.9 %collective-permute-done.8.refs_3_ = bf16[32,1024]{1,0:T(8,128)(2,1)S(1)} collective-permute-done((bf16[32,1024]{1,0:T(8,128)(2,1)S(1)}, bf16[32,1024]{1,0:T(8,128)(2,1)S(1)}, u32[]{:S(2)}, u32[]{:S(2)}) %collective-permute-start.8) | collective-permute-done | bytes 65568 | tf_op jit(solution)/shard_map/ppermute | solution.py:48
  24.0 0.8 %join_pieces.1 = bf16[32,4096]{1,0:T(8,128)(2,1)} custom-call(bf16[32,1024]{1,0:T(8,128)(2,1)S(1)} %get-tuple-element.37.refs_0_, bf16[32,1024]{1,0:T(8,128)(2,1)S(1)} %collective-permute-done.5.refs_1_, bf16[32,1024]{1,0:T(8,128)(2,1)S(1)} %block_outputs.4.refs_2_, bf16[32,1024]{1,0:T(8,128)(2,1)S(1)} %collective-permute-done.8.refs_3_), custom_call_target="tpu_custom_call" | custom-call | tf_op jit(solution)/shard_map/join_pieces/pallas_call | solution.py:316
  (24 shorter events, 0.5 us)
Async XLA Ops:
  1.0 10.2 %collective-permute-start = (bf16[8,128,128]{2,1,0:T(8,128)(2,1)S(1)}, bf16[8,128,128]{2,1,0:T(8,128)(2,1)S(1)}, u32[]{:S(2)}, u32[]{:S(2)}) collective-permute-start(bf16[8,128,128]{2,1,0:T(8,128)(2,1)S(1)} %key_kernel.1._.rest_0_), channel_id=1, source_target_pairs={{4,0},{13,1},{6,2},{15,3},{0,4},{9,5},{2,6},{11,7},{12,8},{5,9},{1... | collective-permute-start | bytes 786440 | tf_op jit(solution)/shard_map/ppermute | solution.py:40
  5.4 9.0 %collective-permute-start.3 = (bf16[4,128,128]{2,1,0:T(8,128)(2,1)S(1)}, bf16[4,128,128]{2,1,0:T(8,128)(2,1)S(1)}, u32[]{:S(2)}, u32[]{:S(2)}) collective-permute-start(bf16[4,128,128]{2,1,0:T(8,128)(2,1)S(1)} %get-tuple-element.35.rest_4_), channel_id=1, source_target_pairs={{4,0},{13,1},{6,2},{15,3},{0,4},{9,5},{2,6},{11,7},{12,8},{5,9},{1... | collective-permute-start | bytes 393224 | tf_op jit(solution)/shard_map/ppermute | solution.py:40
  5.5 11.5 %collective-permute-start.6 = (bf16[4,128,128]{2,1,0:T(8,128)(2,1)S(1)}, bf16[4,128,128]{2,1,0:T(8,128)(2,1)S(1)}, u32[]{:S(2)}, u32[]{:S(2)}) collective-permute-start(bf16[4,128,128]{2,1,0:T(8,128)(2,1)S(1)} %get-tuple-element.39.rest_4_), channel_id=1, source_target_pairs={{4,0},{13,1},{6,2},{15,3},{0,4},{9,5},{2,6},{11,7},{12,8},{5,9},{1... | collective-permute-start | bytes 393224 | tf_op jit(solution)/shard_map/ppermute | solution.py:40
  11.3 1.6 %collective-permute-start.1 = (bf16[8,80,128]{2,1,0:T(8,128)(2,1)S(1)}, bf16[8,80,128]{2,1,0:T(8,128)(2,1)S(1)}, u32[]{:S(2)}, u32[]{:S(2)}) collective-permute-start(bf16[8,80,128]{2,1,0:T(8,128)(2,1)S(1)} %get-tuple-element.27), channel_id=1, source_target_pairs={{0,1},{1,0},{2,3},{3,2},{4,5},{5,4},{6,7},{7,6},{8,9},{9,8},{10,11... | collective-permute-start | bytes 491528 | tf_op jit(solution)/shard_map/ppermute | solution.py:48
  11.8 1.5 %collective-permute-start.2 = (bf16[8,128,128]{2,1,0:T(8,128)(2,1)S(1)}, bf16[8,128,128]{2,1,0:T(8,128)(2,1)S(1)}, u32[]{:S(2)}, u32[]{:S(2)}) collective-permute-start(bf16[8,128,128]{2,1,0:T(8,128)(2,1)S(1)} %collective-permute-done.rest_1_), channel_id=1, source_target_pairs={{0,1},{1,0},{2,3},{3,2},{4,5},{5,4},{6,7},{7,6},{8,9},{9,8},{10,11... | collective-permute-start | bytes 786440 | tf_op jit(solution)/shard_map/ppermute | solution.py:48
  14.4 1.4 %collective-permute-start.4 = (bf16[4,128,128]{2,1,0:T(8,128)(2,1)S(1)}, bf16[4,128,128]{2,1,0:T(8,128)(2,1)S(1)}, u32[]{:S(2)}, u32[]{:S(2)}) collective-permute-start(bf16[4,128,128]{2,1,0:T(8,128)(2,1)S(1)} %collective-permute-done.3.rest_5_), channel_id=1, source_target_pairs={{0,1},{1,0},{2,3},{3,2},{4,5},{5,4},{6,7},{7,6},{8,9},{9,8},{10,11... | collective-permute-start | bytes 393224 | tf_op jit(solution)/shard_map/ppermute | solution.py:48
  16.9 2.0 %collective-permute-start.7 = (bf16[4,128,128]{2,1,0:T(8,128)(2,1)S(1)}, bf16[4,128,128]{2,1,0:T(8,128)(2,1)S(1)}, u32[]{:S(2)}, u32[]{:S(2)}) collective-permute-start(bf16[4,128,128]{2,1,0:T(8,128)(2,1)S(1)} %collective-permute-done.6.rest_5_), channel_id=1, source_target_pairs={{0,1},{1,0},{2,3},{3,2},{4,5},{5,4},{6,7},{7,6},{8,9},{9,8},{10,11... | collective-permute-start | bytes 393224 | tf_op jit(solution)/shard_map/ppermute | solution.py:48
  17.2 4.9 %collective-permute-start.5 = (bf16[32,1024]{1,0:T(8,128)(2,1)S(1)}, bf16[32,1024]{1,0:T(8,128)(2,1)S(1)}, u32[]{:S(2)}, u32[]{:S(2)}) collective-permute-start(bf16[32,1024]{1,0:T(8,128)(2,1)S(1)} %get-tuple-element.38), channel_id=1, source_target_pairs={{0,3},{1,2},{2,1},{3,0},{4,7},{5,6},{6,5},{7,4},{8,11},{9,10},{10,... | collective-permute-start | bytes 196616 | tf_op jit(solution)/shard_map/ppermute | solution.py:48
  20.0 4.1 %collective-permute-start.8 = (bf16[32,1024]{1,0:T(8,128)(2,1)S(1)}, bf16[32,1024]{1,0:T(8,128)(2,1)S(1)}, u32[]{:S(2)}, u32[]{:S(2)}) collective-permute-start(bf16[32,1024]{1,0:T(8,128)(2,1)S(1)} %block_outputs.5), channel_id=1, source_target_pairs={{0,3},{1,2},{2,1},{3,0},{4,7},{5,6},{6,5},{7,4},{8,11},{9,10},{10,... | collective-permute-start | bytes 196616 | tf_op jit(solution)/shard_map/ppermute | solution.py:48

commit v10 on v9

--- a/solution.py
+++ b/solution.py
@@ -24,19 +24,23 @@
 
 
 def source(place, part, cycle, pairs):
-    if pairs:
-        return place + 1 if place % 2 == part else place - 1
-    return place - 1 if part == 0 else place + 1
+    if not pairs:
+        return (place + (1 if part else -1)) % cycle, part
+    outer = place % 4 in (0, 3)
+    odd = part == outer
+    other = (place + (1 if place % 2 == odd else -1)) % cycle
+    return other, int((other % 4 in (0, 3)) == odd)
 
 
 def sent(x, share, pairs):
     cycle = lax.axis_size("ctx")
     heads = lax.axis_size("head")
-    moves = [
-        (source(place, head % share, cycle, pairs) % cycle * heads + head, place * heads + head)
-        for place in range(cycle)
-        for head in range(heads)
-    ]
+    moves = []
+    for place in range(cycle):
+        for head in range(heads):
+            part = head % share
+            other, core = source(place, part, cycle, pairs)
+            moves.append((other * heads + head - part + core, place * heads + head))
     return lax.ppermute(x, ("ctx", "head"), moves)
 
 
@@ -389,7 +393,8 @@
     offset = jnp.mod(lists // key_blocks - cycle_place, cycle_size)
     above = offset <= reach_hops
     hops = jnp.where(above, offset, cycle_size - offset)
-    from_above = (cycle_place % 2 if pairs else 1) == core
+    outer = jnp.logical_or(cycle_place % 4 == 0, cycle_place % 4 == 3)
+    from_above = (cycle_place % 2 == (core == outer)) if pairs else core == 1
     place = 2 * hops - jnp.where(above == from_above, 1, 0)
     slots = lists % key_blocks + key_blocks * jnp.where(offset == 0, 0, place)
 

time: 25 us -> 24.8 us (level)
  waiting for transfers between devices: 6.37 us -> 5.27 us
  starting transfers between devices: 9.29 us -> 10.2 us
    ppermute x6, starting transfers between devices: 4.11 us -> 5.82 us  [swapped(): lax.ppermute(x, 'head', [(i, i ^ mask) for i in range(lax.axis_size('head...]
    ppermute x3, waiting for transfers between devices: 2.88 us -> 1.66 us  [sent(): return lax.ppermute(x, ('ctx', 'head'), moves)]
    ppermute x3, starting transfers between devices: 5.18 us -> 4.34 us  [sent(): return lax.ppermute(x, ('ctx', 'head'), moves)]
where the time goes in v10:
time: 24.8 us; the launch traced here: 24.6 us
  starting transfers between devices  10.2 us (41%)
  Pallas kernels  8.23 us (33%)
  waiting for transfers between devices  5.27 us (21%)
  other arithmetic  0.54 us (2%)
  local copies, waits for them, and re-layouts  0.26 us (1%)
    ppermute x6, starting transfers between devices, swapped(): lax.ppermute(x, 'head', [(i, i ^ mask) for i in range(lax.axis_size('head...  5.82 us
    ppermute x3, starting transfers between devices, sent(): return lax.ppermute(x, ('ctx', 'head'), moves)  4.34 us
    ppermute x6, waiting for transfers between devices, swapped(): lax.ppermute(x, 'head', [(i, i ^ mask) for i in range(lax.axis_size('head...  3.61 us
    pallas_call x3, Pallas kernels, block_outputs(): pl.pallas_call(functools.partial(value_kernel, inputs=len(parts), flip=fl...  3.01 us
    pallas_call x2, Pallas kernels, begin(): pl.pallas_call(kernel, in_specs=[pl.BlockSpec(memory_space=pltpu.HBM)] *...  2.28 us
    pallas_call x2, Pallas kernels, block_weights(): pl.pallas_call(functools.partial(score_kernel, inputs=len(parts)) if len(...  1.91 us
    ppermute x3, waiting for transfers between devices, sent(): return lax.ppermute(x, ('ctx', 'head'), moves)  1.66 us
    pallas_call x1, Pallas kernels, join_pieces(): pl.pallas_call(functools.partial(join_kernel, share=share, width=width),...  0.82 us
  transfers between devices with their start and end apart: 9, of which 5 were waited for; matrix products, arithmetic and copies ran while one was open for 3% of the time, Pallas kernels for 26%

profile of v10, /device:TPU:0, one launch (start us, length us, event | category | flops | bytes accessed | tf_op | source)
XLA Modules:
  0.0 24.6 jit_solution(188617400279088832)
XLA Ops:
  0.0 1.0 %key_kernel.1._.rest_0_ = bf16[8,128,128]{2,1,0:T(8,128)(2,1)S(1)} custom-call(s32[2,2,8]{2,1,0:T(2,128)} %index_hbm.3, f32[2,16]{1,0:T(2,128)} %table_hbm.3, bf16[2,1024,128]{2,1,0:T(8,128)(2,1)} %codes_hbm.2), custom_call_target="tpu_custom_call" | custom-call | tf_op jit(solution)/shard_map/key_kernel/pallas_call | solution.py:122
  1.0 2.5 %collective-permute-start = (bf16[8,128,128]{2,1,0:T(8,128)(2,1)S(1)}, bf16[8,128,128]{2,1,0:T(8,128)(2,1)S(1)}, u32[]{:S(2)}, u32[]{:S(2)}) collective-permute-start(bf16[8,128,128]{2,1,0:T(8,128)(2,1)S(1)} %key_kernel.1._.rest_0_), channel_id=1, source_target_pairs={{5,0},{13,1},{7,2},{15,3},{8,4},{0,5},{10,6},{2,7},{4,8},{12,9},{6... | collective-permute-start | bytes 786440 | tf_op jit(solution)/shard_map/ppermute | solution.py:44
  3.6 1.3 %half_kernel.1 = (bf16[4,128,128]{2,1,0:T(8,128)(2,1)S(1)}, bf16[4,128,128]{2,1,0:T(8,128)(2,1)S(1)}, bf16[128,8,128]{2,1,0:T(8,128)(2,1)S(1)}, s32[128]{0:T(128)S(1)}, s32[8,4,8]{2,1,0:T(4,128)S(1)}) custom-call(s32[2,2,8]{2,1,0:T(2,128)} %index_hbm.3, f32[2,16]{1,0:T(2,128)} %table_hbm.3, bf16[2,1024,128]{2,1,0:T(8,128)(2,1)} %codes_hbm.3, ...), custom_call_target="tpu_custom_call" | custom-call | tf_op jit(solution)/shard_map/half_kernel/pallas_call | solution.py:122
  4.8 0.1 collective-permute-start.3
  4.9 1.7 %collective-permute-start.6 = (bf16[4,128,128]{2,1,0:T(8,128)(2,1)S(1)}, bf16[4,128,128]{2,1,0:T(8,128)(2,1)S(1)}, u32[]{:S(2)}, u32[]{:S(2)}) collective-permute-start(bf16[4,128,128]{2,1,0:T(8,128)(2,1)S(1)} %get-tuple-element.39.rest_4_), channel_id=1, source_target_pairs={{5,0},{13,1},{7,2},{15,3},{8,4},{0,5},{10,6},{2,7},{4,8},{12,9},{6... | collective-permute-start | bytes 393224 | tf_op jit(solution)/shard_map/ppermute | solution.py:44
  6.9 0.1 convert_element_type.35
  7.0 0.3 %fusion = (f32[128,128]{1,0:T(8,128)S(1)}, f32[128,128]{1,0:T(8,128)S(1)}) fusion(f32[128]{0:T(128)S(1)} %get-tuple-element.56, f32[128]{0:T(128)S(1)} %get-tuple-element.57, f32[128]{0:T(128)S(1)} %convert_element_type.35), kind=kLoop, calls=%fused_computation.3 | loop fusion | flops 32768 | bytes 132608 | tf_op jit(solution)/shard_map/mul | solution.py:381
  7.3 0.2 turn_queries.1
  7.6 1.7 %collective-permute-done.rest_1_ = bf16[8,128,128]{2,1,0:T(8,128)(2,1)S(1)} collective-permute-done((bf16[8,128,128]{2,1,0:T(8,128)(2,1)S(1)}, bf16[8,128,128]{2,1,0:T(8,128)(2,1)S(1)}, u32[]{:S(2)}, u32[]{:S(2)}) %collective-permute-start) | collective-permute-done | bytes 262176 | tf_op jit(solution)/shard_map/ppermute | solution.py:44
  9.2 2.7 %collective-permute-start.1 = (bf16[8,80,128]{2,1,0:T(8,128)(2,1)S(1)}, bf16[8,80,128]{2,1,0:T(8,128)(2,1)S(1)}, u32[]{:S(2)}, u32[]{:S(2)}) collective-permute-start(bf16[8,80,128]{2,1,0:T(8,128)(2,1)S(1)} %get-tuple-element.27), channel_id=1, source_target_pairs={{0,1},{1,0},{2,3},{3,2},{4,5},{5,4},{6,7},{7,6},{8,9},{9,8},{10,11... | collective-permute-start | bytes 491528 | tf_op jit(solution)/shard_map/ppermute | solution.py:52
  12.0 1.0 %collective-permute-done.1.queries_ref = bf16[8,80,128]{2,1,0:T(8,128)(2,1)S(1)} collective-permute-done((bf16[8,80,128]{2,1,0:T(8,128)(2,1)S(1)}, bf16[8,80,128]{2,1,0:T(8,128)(2,1)S(1)}, u32[]{:S(2)}, u32[]{:S(2)}) %collective-permute-start.1) | collective-permute-done | bytes 163872 | tf_op jit(solution)/shard_map/ppermute | solution.py:52
  13.0 0.4 %collective-permute-done.2.rest_2_ = bf16[8,128,128]{2,1,0:T(8,128)(2,1)S(1)} collective-permute-done((bf16[8,128,128]{2,1,0:T(8,128)(2,1)S(1)}, bf16[8,128,128]{2,1,0:T(8,128)(2,1)S(1)}, u32[]{:S(2)}, u32[]{:S(2)}) %collective-permute-start.2) | collective-permute-done | bytes 262176 | tf_op jit(solution)/shard_map/ppermute | solution.py:52
  13.4 1.1 %block_weights.2 = (bf16[8,64,1024]{2,1,0:T(8,128)(2,1)S(1)}, f32[8,64,128]{2,1,0:T(8,128)S(1)}, bf16[24,128,128]{2,1,0:T(8,128)(2,1)S(1)}) custom-call(s32[8,8]{1,0:T(8,128)S(1)} %get-tuple-element.49.slots_ref, bf16[8,64,128]{2,1,0:T(8,128)(2,1)S(1)} %get-tuple-element.28.queries_ref, bf16[8,128,128]{2,1,0:T(8,128)(2,1)S(1)} %key_kernel.1._.rest_0_, ...), custom_call_target="tpu_custom_call" | custom-call | tf_op jit(solution)/shard_map/block_weights/pallas_call | solution.py:226
  14.5 0.3 %collective-permute-start.4 = (bf16[4,128,128]{2,1,0:T(8,128)(2,1)S(1)}, bf16[4,128,128]{2,1,0:T(8,128)(2,1)S(1)}, u32[]{:S(2)}, u32[]{:S(2)}) collective-permute-start(bf16[4,128,128]{2,1,0:T(8,128)(2,1)S(1)} %collective-permute-done.3.rest_5_), channel_id=1, source_target_pairs={{0,1},{1,0},{2,3},{3,2},{4,5},{5,4},{6,7},{7,6},{8,9},{9,8},{10,11... | collective-permute-start | bytes 393224 | tf_op jit(solution)/shard_map/ppermute | solution.py:52
  14.9 0.8 %block_weights.3 = (bf16[8,64,1024]{2,1,0:T(8,128)(2,1)S(1)}, f32[8,64,128]{2,1,0:T(8,128)S(1)}) custom-call(s32[8,8]{1,0:T(8,128)S(1)} %get-tuple-element.48.slots_ref, bf16[8,80,128]{2,1,0:T(8,128)(2,1)S(1)} %collective-permute-done.1.queries_ref, bf16[24,128,128]{2,1,0:T(8,128)(2,1)S(1)} %get-tuple-element.31.store), custom_call_target="tpu_custom_call" | custom-call | tf_op jit(solution)/shard_map/block_weights/pallas_call | solution.py:226
  15.7 0.2 collective-permute-done.4.rest_6_
  15.9 1.1 %block_outputs.3 = (bf16[32,1024]{1,0:T(8,128)(2,1)S(1)}, bf16[32,1024]{1,0:T(8,128)(2,1)S(1)}) custom-call(s32[16,8]{1,0:T(8,128)S(1)} %multiply_add_fusion.1.slots_ref, bf16[8,64,1024]{2,1,0:T(8,128)(2,1)S(1)} %get-tuple-element.30.rest_0_, bf16[8,64,1024]{2,1,0:T(8,128)(2,1)S(1)} %get-tuple-element.32.rest_1_, ...), custom_call_target="tpu_custom_call" | custom-call | tf_op jit(solution)/shard_map/block_outputs/pallas_call | solution.py:278
  17.0 0.3 %collective-permute-start.7 = (bf16[4,128,128]{2,1,0:T(8,128)(2,1)S(1)}, bf16[4,128,128]{2,1,0:T(8,128)(2,1)S(1)}, u32[]{:S(2)}, u32[]{:S(2)}) collective-permute-start(bf16[4,128,128]{2,1,0:T(8,128)(2,1)S(1)} %collective-permute-done.6.rest_5_), channel_id=1, source_target_pairs={{0,1},{1,0},{2,3},{3,2},{4,5},{5,4},{6,7},{7,6},{8,9},{9,8},{10,11... | collective-permute-start | bytes 393224 | tf_op jit(solution)/shard_map/ppermute | solution.py:52
  17.3 1.4 %collective-permute-start.5 = (bf16[32,1024]{1,0:T(8,128)(2,1)S(1)}, bf16[32,1024]{1,0:T(8,128)(2,1)S(1)}, u32[]{:S(2)}, u32[]{:S(2)}) collective-permute-start(bf16[32,1024]{1,0:T(8,128)(2,1)S(1)} %get-tuple-element.38), channel_id=1, source_target_pairs={{0,3},{1,2},{2,1},{3,0},{4,7},{5,6},{6,5},{7,4},{8,11},{9,10},{10,... | collective-permute-start | bytes 196616 | tf_op jit(solution)/shard_map/ppermute | solution.py:52
  18.7 1.0 %block_outputs.5 = bf16[32,1024]{1,0:T(8,128)(2,1)S(1)} custom-call(s32[16,8]{1,0:T(8,128)S(1)} %get-tuple-element.41.slots_ref, bf16[8,64,1024]{2,1,0:T(8,128)(2,1)S(1)} %get-tuple-element.30.rest_0_, bf16[8,64,1024]{2,1,0:T(8,128)(2,1)S(1)} %get-tuple-element.32.rest_1_, f32[8,64,128]{2,1,0:T(8,128)S(1)} %get-tuple-element.33.rest_2_, ...), custom_call_target="tpu_custom_call" | custom-call | tf_op jit(solution)/shard_map/block_outputs/pallas_call | solution.py:278
  19.7 1.1 %collective-permute-start.8 = (bf16[32,1024]{1,0:T(8,128)(2,1)S(1)}, bf16[32,1024]{1,0:T(8,128)(2,1)S(1)}, u32[]{:S(2)}, u32[]{:S(2)}) collective-permute-start(bf16[32,1024]{1,0:T(8,128)(2,1)S(1)} %block_outputs.5), channel_id=1, source_target_pairs={{0,3},{1,2},{2,1},{3,0},{4,7},{5,6},{6,5},{7,4},{8,11},{9,10},{10,... | collective-permute-start | bytes 196616 | tf_op jit(solution)/shard_map/ppermute | solution.py:52
  20.8 1.0 %block_outputs.4.refs_2_ = bf16[32,1024]{1,0:T(8,128)(2,1)S(1)} custom-call(s32[16,8]{1,0:T(8,128)S(1)} %get-tuple-element.41.slots_ref, bf16[8,64,1024]{2,1,0:T(8,128)(2,1)S(1)} %get-tuple-element.30.rest_0_, bf16[8,64,1024]{2,1,0:T(8,128)(2,1)S(1)} %get-tuple-element.32.rest_1_, f32[8,64,128]{2,1,0:T(8,128)S(1)} %get-tuple-element.33.rest_2_, ...), custom_call_target="tpu_custom_call" | custom-call | tf_op jit(solution)/shard_map/block_outputs/pallas_call | solution.py:278
  21.8 2.0 %collective-permute-done.8.refs_3_ = bf16[32,1024]{1,0:T(8,128)(2,1)S(1)} collective-permute-done((bf16[32,1024]{1,0:T(8,128)(2,1)S(1)}, bf16[32,1024]{1,0:T(8,128)(2,1)S(1)}, u32[]{:S(2)}, u32[]{:S(2)}) %collective-permute-start.8) | collective-permute-done | bytes 65568 | tf_op jit(solution)/shard_map/ppermute | solution.py:52
  23.8 0.8 %join_pieces.1 = bf16[32,4096]{1,0:T(8,128)(2,1)} custom-call(bf16[32,1024]{1,0:T(8,128)(2,1)S(1)} %get-tuple-element.37.refs_0_, bf16[32,1024]{1,0:T(8,128)(2,1)S(1)} %collective-permute-done.5.refs_1_, bf16[32,1024]{1,0:T(8,128)(2,1)S(1)} %block_outputs.4.refs_2_, bf16[32,1024]{1,0:T(8,128)(2,1)S(1)} %collective-permute-done.8.refs_3_), custom_call_target="tpu_custom_call" | custom-call | tf_op jit(solution)/shard_map/join_pieces/pallas_call | solution.py:320
  (24 shorter events, 0.5 us)
Async XLA Ops:
  1.0 8.2 %collective-permute-start = (bf16[8,128,128]{2,1,0:T(8,128)(2,1)S(1)}, bf16[8,128,128]{2,1,0:T(8,128)(2,1)S(1)}, u32[]{:S(2)}, u32[]{:S(2)}) collective-permute-start(bf16[8,128,128]{2,1,0:T(8,128)(2,1)S(1)} %key_kernel.1._.rest_0_), channel_id=1, source_target_pairs={{5,0},{13,1},{7,2},{15,3},{8,4},{0,5},{10,6},{2,7},{4,8},{12,9},{6... | collective-permute-start | bytes 786440 | tf_op jit(solution)/shard_map/ppermute | solution.py:44
  4.8 9.7 %collective-permute-start.3 = (bf16[4,128,128]{2,1,0:T(8,128)(2,1)S(1)}, bf16[4,128,128]{2,1,0:T(8,128)(2,1)S(1)}, u32[]{:S(2)}, u32[]{:S(2)}) collective-permute-start(bf16[4,128,128]{2,1,0:T(8,128)(2,1)S(1)} %get-tuple-element.35.rest_4_), channel_id=1, source_target_pairs={{5,0},{13,1},{7,2},{15,3},{8,4},{0,5},{10,6},{2,7},{4,8},{12,9},{6... | collective-permute-start | bytes 393224 | tf_op jit(solution)/shard_map/ppermute | solution.py:44
  4.9 12.1 %collective-permute-start.6 = (bf16[4,128,128]{2,1,0:T(8,128)(2,1)S(1)}, bf16[4,128,128]{2,1,0:T(8,128)(2,1)S(1)}, u32[]{:S(2)}, u32[]{:S(2)}) collective-permute-start(bf16[4,128,128]{2,1,0:T(8,128)(2,1)S(1)} %get-tuple-element.39.rest_4_), channel_id=1, source_target_pairs={{5,0},{13,1},{7,2},{15,3},{8,4},{0,5},{10,6},{2,7},{4,8},{12,9},{6... | collective-permute-start | bytes 393224 | tf_op jit(solution)/shard_map/ppermute | solution.py:44
  9.2 3.7 %collective-permute-start.1 = (bf16[8,80,128]{2,1,0:T(8,128)(2,1)S(1)}, bf16[8,80,128]{2,1,0:T(8,128)(2,1)S(1)}, u32[]{:S(2)}, u32[]{:S(2)}) collective-permute-start(bf16[8,80,128]{2,1,0:T(8,128)(2,1)S(1)} %get-tuple-element.27), channel_id=1, source_target_pairs={{0,1},{1,0},{2,3},{3,2},{4,5},{5,4},{6,7},{7,6},{8,9},{9,8},{10,11... | collective-permute-start | bytes 491528 | tf_op jit(solution)/shard_map/ppermute | solution.py:52
  11.9 1.5 %collective-permute-start.2 = (bf16[8,128,128]{2,1,0:T(8,128)(2,1)S(1)}, bf16[8,128,128]{2,1,0:T(8,128)(2,1)S(1)}, u32[]{:S(2)}, u32[]{:S(2)}) collective-permute-start(bf16[8,128,128]{2,1,0:T(8,128)(2,1)S(1)} %collective-permute-done.rest_1_), channel_id=1, source_target_pairs={{0,1},{1,0},{2,3},{3,2},{4,5},{5,4},{6,7},{7,6},{8,9},{9,8},{10,11... | collective-permute-start | bytes 786440 | tf_op jit(solution)/shard_map/ppermute | solution.py:52
  14.5 1.4 %collective-permute-start.4 = (bf16[4,128,128]{2,1,0:T(8,128)(2,1)S(1)}, bf16[4,128,128]{2,1,0:T(8,128)(2,1)S(1)}, u32[]{:S(2)}, u32[]{:S(2)}) collective-permute-start(bf16[4,128,128]{2,1,0:T(8,128)(2,1)S(1)} %collective-permute-done.3.rest_5_), channel_id=1, source_target_pairs={{0,1},{1,0},{2,3},{3,2},{4,5},{5,4},{6,7},{7,6},{8,9},{9,8},{10,11... | collective-permute-start | bytes 393224 | tf_op jit(solution)/shard_map/ppermute | solution.py:52
  17.0 1.7 %collective-permute-start.7 = (bf16[4,128,128]{2,1,0:T(8,128)(2,1)S(1)}, bf16[4,128,128]{2,1,0:T(8,128)(2,1)S(1)}, u32[]{:S(2)}, u32[]{:S(2)}) collective-permute-start(bf16[4,128,128]{2,1,0:T(8,128)(2,1)S(1)} %collective-permute-done.6.rest_5_), channel_id=1, source_target_pairs={{0,1},{1,0},{2,3},{3,2},{4,5},{5,4},{6,7},{7,6},{8,9},{9,8},{10,11... | collective-permute-start | bytes 393224 | tf_op jit(solution)/shard_map/ppermute | solution.py:52
  17.3 4.5 %collective-permute-start.5 = (bf16[32,1024]{1,0:T(8,128)(2,1)S(1)}, bf16[32,1024]{1,0:T(8,128)(2,1)S(1)}, u32[]{:S(2)}, u32[]{:S(2)}) collective-permute-start(bf16[32,1024]{1,0:T(8,128)(2,1)S(1)} %get-tuple-element.38), channel_id=1, source_target_pairs={{0,3},{1,2},{2,1},{3,0},{4,7},{5,6},{6,5},{7,4},{8,11},{9,10},{10,... | collective-permute-start | bytes 196616 | tf_op jit(solution)/shard_map/ppermute | solution.py:52
  19.7 4.1 %collective-permute-start.8 = (bf16[32,1024]{1,0:T(8,128)(2,1)S(1)}, bf16[32,1024]{1,0:T(8,128)(2,1)S(1)}, u32[]{:S(2)}, u32[]{:S(2)}) collective-permute-start(bf16[32,1024]{1,0:T(8,128)(2,1)S(1)} %block_outputs.5), channel_id=1, source_target_pairs={{0,3},{1,2},{2,1},{3,0},{4,7},{5,6},{6,5},{7,4},{8,11},{9,10},{10,... | collective-permute-start | bytes 196616 | tf_op jit(solution)/shard_map/ppermute | solution.py:52

commit v11 on v10

--- a/solution.py
+++ b/solution.py
@@ -343,21 +343,23 @@
     groups = head_count // share
 
     (keys,) = begin(key_kernel, scale_index, scale_table, key_codes, 1)
-    *values, queries, positions, block_lists = begin(
+    *values, brought, positions, block_lists = begin(
         half_kernel,
         scale_index,
         scale_table,
         value_codes,
         2,
         keys,
-        others=(queries, positions, block_lists),
-    )
+        others=(queries.reshape(-1, head_width), positions, block_lists),
+    )
+    queries = brought.reshape(queries.shape)
     far_keys = keys
     key_parts = []
     for _ in range(reach_hops):
         far_keys = sent(far_keys, share, pairs)
         key_parts.append(far_keys)
     own_lists = lax.dynamic_index_in_dim(block_lists, cycle_place, 1, keepdims=False)
+
     def ordered(x):
         cut = x.reshape((groups, share, rows_dev // head_count) + x.shape[1:])
         taken = [

time: 24.8 us -> 24.8 us (level)
  no operation moved by 1% of the time
where the time goes in v11:
time: 24.8 us; the launch traced here: 24.6 us
  starting transfers between devices  10.2 us (41%)
  Pallas kernels  8.23 us (33%)
  waiting for transfers between devices  5.27 us (21%)
  other arithmetic  0.54 us (2%)
  local copies, waits for them, and re-layouts  0.26 us (1%)
    ppermute x6, starting transfers between devices, swapped(): lax.ppermute(x, 'head', [(i, i ^ mask) for i in range(lax.axis_size('head...  5.82 us
    ppermute x3, starting transfers between devices, sent(): return lax.ppermute(x, ('ctx', 'head'), moves)  4.34 us
    ppermute x6, waiting for transfers between devices, swapped(): lax.ppermute(x, 'head', [(i, i ^ mask) for i in range(lax.axis_size('head...  3.61 us
    pallas_call x3, Pallas kernels, block_outputs(): pl.pallas_call(functools.partial(value_kernel, inputs=len(parts), flip=fl...  3.01 us
    pallas_call x2, Pallas kernels, begin(): pl.pallas_call(kernel, in_specs=[pl.BlockSpec(memory_space=pltpu.HBM)] *...  2.28 us
    pallas_call x2, Pallas kernels, block_weights(): pl.pallas_call(functools.partial(score_kernel, inputs=len(parts)) if len(...  1.91 us
    ppermute x3, waiting for transfers between devices, sent(): return lax.ppermute(x, ('ctx', 'head'), moves)  1.66 us
    pallas_call x1, Pallas kernels, join_pieces(): pl.pallas_call(functools.partial(join_kernel, share=share, width=width),...  0.82 us
  transfers between devices with their start and end apart: 9, of which 5 were waited for; matrix products, arithmetic and copies ran while one was open for 3% of the time, Pallas kernels for 26%

profile of v11, /device:TPU:0, one launch (start us, length us, event | category | flops | bytes accessed | tf_op | source)
XLA Modules:
  0.0 24.6 jit_solution(188617400279088832)
XLA Ops:
  0.0 1.0 %key_kernel.1._.rest_0_ = bf16[8,128,128]{2,1,0:T(8,128)(2,1)S(1)} custom-call(s32[2,2,8]{2,1,0:T(2,128)} %index_hbm.3, f32[2,16]{1,0:T(2,128)} %table_hbm.3, bf16[2,1024,128]{2,1,0:T(8,128)(2,1)} %codes_hbm.2), custom_call_target="tpu_custom_call" | custom-call | tf_op jit(solution)/shard_map/key_kernel/pallas_call | solution.py:122
  1.0 2.5 %collective-permute-start = (bf16[8,128,128]{2,1,0:T(8,128)(2,1)S(1)}, bf16[8,128,128]{2,1,0:T(8,128)(2,1)S(1)}, u32[]{:S(2)}, u32[]{:S(2)}) collective-permute-start(bf16[8,128,128]{2,1,0:T(8,128)(2,1)S(1)} %key_kernel.1._.rest_0_), channel_id=1, source_target_pairs={{5,0},{13,1},{7,2},{15,3},{8,4},{0,5},{10,6},{2,7},{4,8},{12,9},{6... | collective-permute-start | bytes 786440 | tf_op jit(solution)/shard_map/ppermute | solution.py:44
  3.6 1.3 %half_kernel.1 = (bf16[4,128,128]{2,1,0:T(8,128)(2,1)S(1)}, bf16[4,128,128]{2,1,0:T(8,128)(2,1)S(1)}, bf16[1024,128]{1,0:T(8,128)(2,1)S(1)}, s32[128]{0:T(128)S(1)}, s32[8,4,8]{2,1,0:T(4,128)S(1)}) custom-call(s32[2,2,8]{2,1,0:T(2,128)} %index_hbm.3, f32[2,16]{1,0:T(2,128)} %table_hbm.3, bf16[2,1024,128]{2,1,0:T(8,128)(2,1)} %codes_hbm.3, ...), custom_call_target="tpu_custom_call" | custom-call | tf_op jit(solution)/shard_map/half_kernel/pallas_call | solution.py:122
  4.8 0.1 collective-permute-start.3
  4.9 1.7 %collective-permute-start.6 = (bf16[4,128,128]{2,1,0:T(8,128)(2,1)S(1)}, bf16[4,128,128]{2,1,0:T(8,128)(2,1)S(1)}, u32[]{:S(2)}, u32[]{:S(2)}) collective-permute-start(bf16[4,128,128]{2,1,0:T(8,128)(2,1)S(1)} %get-tuple-element.39.rest_4_), channel_id=1, source_target_pairs={{5,0},{13,1},{7,2},{15,3},{8,4},{0,5},{10,6},{2,7},{4,8},{12,9},{6... | collective-permute-start | bytes 393224 | tf_op jit(solution)/shard_map/ppermute | solution.py:44
  6.9 0.1 convert_element_type.35
  7.0 0.3 %fusion = (f32[128,128]{1,0:T(8,128)S(1)}, f32[128,128]{1,0:T(8,128)S(1)}) fusion(f32[128]{0:T(128)S(1)} %get-tuple-element.56, f32[128]{0:T(128)S(1)} %get-tuple-element.57, f32[128]{0:T(128)S(1)} %convert_element_type.35), kind=kLoop, calls=%fused_computation.3 | loop fusion | flops 32768 | bytes 132608 | tf_op jit(solution)/shard_map/mul | solution.py:383
  7.3 0.2 turn_queries.1
  7.6 1.7 %collective-permute-done.rest_1_ = bf16[8,128,128]{2,1,0:T(8,128)(2,1)S(1)} collective-permute-done((bf16[8,128,128]{2,1,0:T(8,128)(2,1)S(1)}, bf16[8,128,128]{2,1,0:T(8,128)(2,1)S(1)}, u32[]{:S(2)}, u32[]{:S(2)}) %collective-permute-start) | collective-permute-done | bytes 262176 | tf_op jit(solution)/shard_map/ppermute | solution.py:44
  9.2 2.7 %collective-permute-start.1 = (bf16[8,80,128]{2,1,0:T(8,128)(2,1)S(1)}, bf16[8,80,128]{2,1,0:T(8,128)(2,1)S(1)}, u32[]{:S(2)}, u32[]{:S(2)}) collective-permute-start(bf16[8,80,128]{2,1,0:T(8,128)(2,1)S(1)} %get-tuple-element.27), channel_id=1, source_target_pairs={{0,1},{1,0},{2,3},{3,2},{4,5},{5,4},{6,7},{7,6},{8,9},{9,8},{10,11... | collective-permute-start | bytes 491528 | tf_op jit(solution)/shard_map/ppermute | solution.py:52
  12.0 1.0 %collective-permute-done.1.queries_ref = bf16[8,80,128]{2,1,0:T(8,128)(2,1)S(1)} collective-permute-done((bf16[8,80,128]{2,1,0:T(8,128)(2,1)S(1)}, bf16[8,80,128]{2,1,0:T(8,128)(2,1)S(1)}, u32[]{:S(2)}, u32[]{:S(2)}) %collective-permute-start.1) | collective-permute-done | bytes 163872 | tf_op jit(solution)/shard_map/ppermute | solution.py:52
  13.0 0.4 %collective-permute-done.2.rest_2_ = bf16[8,128,128]{2,1,0:T(8,128)(2,1)S(1)} collective-permute-done((bf16[8,128,128]{2,1,0:T(8,128)(2,1)S(1)}, bf16[8,128,128]{2,1,0:T(8,128)(2,1)S(1)}, u32[]{:S(2)}, u32[]{:S(2)}) %collective-permute-start.2) | collective-permute-done | bytes 262176 | tf_op jit(solution)/shard_map/ppermute | solution.py:52
  13.4 1.1 %block_weights.2 = (bf16[8,64,1024]{2,1,0:T(8,128)(2,1)S(1)}, f32[8,64,128]{2,1,0:T(8,128)S(1)}, bf16[24,128,128]{2,1,0:T(8,128)(2,1)S(1)}) custom-call(s32[8,8]{1,0:T(8,128)S(1)} %get-tuple-element.49.slots_ref, bf16[8,64,128]{2,1,0:T(8,128)(2,1)S(1)} %get-tuple-element.28.queries_ref, bf16[8,128,128]{2,1,0:T(8,128)(2,1)S(1)} %key_kernel.1._.rest_0_, ...), custom_call_target="tpu_custom_call" | custom-call | tf_op jit(solution)/shard_map/block_weights/pallas_call | solution.py:226
  14.5 0.3 %collective-permute-start.4 = (bf16[4,128,128]{2,1,0:T(8,128)(2,1)S(1)}, bf16[4,128,128]{2,1,0:T(8,128)(2,1)S(1)}, u32[]{:S(2)}, u32[]{:S(2)}) collective-permute-start(bf16[4,128,128]{2,1,0:T(8,128)(2,1)S(1)} %collective-permute-done.3.rest_5_), channel_id=1, source_target_pairs={{0,1},{1,0},{2,3},{3,2},{4,5},{5,4},{6,7},{7,6},{8,9},{9,8},{10,11... | collective-permute-start | bytes 393224 | tf_op jit(solution)/shard_map/ppermute | solution.py:52
  14.9 0.8 %block_weights.3 = (bf16[8,64,1024]{2,1,0:T(8,128)(2,1)S(1)}, f32[8,64,128]{2,1,0:T(8,128)S(1)}) custom-call(s32[8,8]{1,0:T(8,128)S(1)} %get-tuple-element.48.slots_ref, bf16[8,80,128]{2,1,0:T(8,128)(2,1)S(1)} %collective-permute-done.1.queries_ref, bf16[24,128,128]{2,1,0:T(8,128)(2,1)S(1)} %get-tuple-element.31.store), custom_call_target="tpu_custom_call" | custom-call | tf_op jit(solution)/shard_map/block_weights/pallas_call | solution.py:226
  15.7 0.2 collective-permute-done.4.rest_6_
  15.9 1.1 %block_outputs.3 = (bf16[32,1024]{1,0:T(8,128)(2,1)S(1)}, bf16[32,1024]{1,0:T(8,128)(2,1)S(1)}) custom-call(s32[16,8]{1,0:T(8,128)S(1)} %multiply_add_fusion.1.slots_ref, bf16[8,64,1024]{2,1,0:T(8,128)(2,1)S(1)} %get-tuple-element.30.rest_0_, bf16[8,64,1024]{2,1,0:T(8,128)(2,1)S(1)} %get-tuple-element.32.rest_1_, ...), custom_call_target="tpu_custom_call" | custom-call | tf_op jit(solution)/shard_map/block_outputs/pallas_call | solution.py:278
  17.0 0.3 %collective-permute-start.7 = (bf16[4,128,128]{2,1,0:T(8,128)(2,1)S(1)}, bf16[4,128,128]{2,1,0:T(8,128)(2,1)S(1)}, u32[]{:S(2)}, u32[]{:S(2)}) collective-permute-start(bf16[4,128,128]{2,1,0:T(8,128)(2,1)S(1)} %collective-permute-done.6.rest_5_), channel_id=1, source_target_pairs={{0,1},{1,0},{2,3},{3,2},{4,5},{5,4},{6,7},{7,6},{8,9},{9,8},{10,11... | collective-permute-start | bytes 393224 | tf_op jit(solution)/shard_map/ppermute | solution.py:52
  17.3 1.4 %collective-permute-start.5 = (bf16[32,1024]{1,0:T(8,128)(2,1)S(1)}, bf16[32,1024]{1,0:T(8,128)(2,1)S(1)}, u32[]{:S(2)}, u32[]{:S(2)}) collective-permute-start(bf16[32,1024]{1,0:T(8,128)(2,1)S(1)} %get-tuple-element.38), channel_id=1, source_target_pairs={{0,3},{1,2},{2,1},{3,0},{4,7},{5,6},{6,5},{7,4},{8,11},{9,10},{10,... | collective-permute-start | bytes 196616 | tf_op jit(solution)/shard_map/ppermute | solution.py:52
  18.7 1.0 %block_outputs.5 = bf16[32,1024]{1,0:T(8,128)(2,1)S(1)} custom-call(s32[16,8]{1,0:T(8,128)S(1)} %get-tuple-element.41.slots_ref, bf16[8,64,1024]{2,1,0:T(8,128)(2,1)S(1)} %get-tuple-element.30.rest_0_, bf16[8,64,1024]{2,1,0:T(8,128)(2,1)S(1)} %get-tuple-element.32.rest_1_, f32[8,64,128]{2,1,0:T(8,128)S(1)} %get-tuple-element.33.rest_2_, ...), custom_call_target="tpu_custom_call" | custom-call | tf_op jit(solution)/shard_map/block_outputs/pallas_call | solution.py:278
  19.7 1.1 %collective-permute-start.8 = (bf16[32,1024]{1,0:T(8,128)(2,1)S(1)}, bf16[32,1024]{1,0:T(8,128)(2,1)S(1)}, u32[]{:S(2)}, u32[]{:S(2)}) collective-permute-start(bf16[32,1024]{1,0:T(8,128)(2,1)S(1)} %block_outputs.5), channel_id=1, source_target_pairs={{0,3},{1,2},{2,1},{3,0},{4,7},{5,6},{6,5},{7,4},{8,11},{9,10},{10,... | collective-permute-start | bytes 196616 | tf_op jit(solution)/shard_map/ppermute | solution.py:52
  20.8 1.0 %block_outputs.4.refs_2_ = bf16[32,1024]{1,0:T(8,128)(2,1)S(1)} custom-call(s32[16,8]{1,0:T(8,128)S(1)} %get-tuple-element.41.slots_ref, bf16[8,64,1024]{2,1,0:T(8,128)(2,1)S(1)} %get-tuple-element.30.rest_0_, bf16[8,64,1024]{2,1,0:T(8,128)(2,1)S(1)} %get-tuple-element.32.rest_1_, f32[8,64,128]{2,1,0:T(8,128)S(1)} %get-tuple-element.33.rest_2_, ...), custom_call_target="tpu_custom_call" | custom-call | tf_op jit(solution)/shard_map/block_outputs/pallas_call | solution.py:278
  21.8 2.0 %collective-permute-done.8.refs_3_ = bf16[32,1024]{1,0:T(8,128)(2,1)S(1)} collective-permute-done((bf16[32,1024]{1,0:T(8,128)(2,1)S(1)}, bf16[32,1024]{1,0:T(8,128)(2,1)S(1)}, u32[]{:S(2)}, u32[]{:S(2)}) %collective-permute-start.8) | collective-permute-done | bytes 65568 | tf_op jit(solution)/shard_map/ppermute | solution.py:52
  23.8 0.8 %join_pieces.1 = bf16[32,4096]{1,0:T(8,128)(2,1)} custom-call(bf16[32,1024]{1,0:T(8,128)(2,1)S(1)} %get-tuple-element.37.refs_0_, bf16[32,1024]{1,0:T(8,128)(2,1)S(1)} %collective-permute-done.5.refs_1_, bf16[32,1024]{1,0:T(8,128)(2,1)S(1)} %block_outputs.4.refs_2_, bf16[32,1024]{1,0:T(8,128)(2,1)S(1)} %collective-permute-done.8.refs_3_), custom_call_target="tpu_custom_call" | custom-call | tf_op jit(solution)/shard_map/join_pieces/pallas_call | solution.py:320
  (24 shorter events, 0.5 us)
Async XLA Ops:
  1.0 8.2 %collective-permute-start = (bf16[8,128,128]{2,1,0:T(8,128)(2,1)S(1)}, bf16[8,128,128]{2,1,0:T(8,128)(2,1)S(1)}, u32[]{:S(2)}, u32[]{:S(2)}) collective-permute-start(bf16[8,128,128]{2,1,0:T(8,128)(2,1)S(1)} %key_kernel.1._.rest_0_), channel_id=1, source_target_pairs={{5,0},{13,1},{7,2},{15,3},{8,4},{0,5},{10,6},{2,7},{4,8},{12,9},{6... | collective-permute-start | bytes 786440 | tf_op jit(solution)/shard_map/ppermute | solution.py:44
  4.8 9.7 %collective-permute-start.3 = (bf16[4,128,128]{2,1,0:T(8,128)(2,1)S(1)}, bf16[4,128,128]{2,1,0:T(8,128)(2,1)S(1)}, u32[]{:S(2)}, u32[]{:S(2)}) collective-permute-start(bf16[4,128,128]{2,1,0:T(8,128)(2,1)S(1)} %get-tuple-element.35.rest_4_), channel_id=1, source_target_pairs={{5,0},{13,1},{7,2},{15,3},{8,4},{0,5},{10,6},{2,7},{4,8},{12,9},{6... | collective-permute-start | bytes 393224 | tf_op jit(solution)/shard_map/ppermute | solution.py:44
  4.9 12.1 %collective-permute-start.6 = (bf16[4,128,128]{2,1,0:T(8,128)(2,1)S(1)}, bf16[4,128,128]{2,1,0:T(8,128)(2,1)S(1)}, u32[]{:S(2)}, u32[]{:S(2)}) collective-permute-start(bf16[4,128,128]{2,1,0:T(8,128)(2,1)S(1)} %get-tuple-element.39.rest_4_), channel_id=1, source_target_pairs={{5,0},{13,1},{7,2},{15,3},{8,4},{0,5},{10,6},{2,7},{4,8},{12,9},{6... | collective-permute-start | bytes 393224 | tf_op jit(solution)/shard_map/ppermute | solution.py:44
  9.2 3.7 %collective-permute-start.1 = (bf16[8,80,128]{2,1,0:T(8,128)(2,1)S(1)}, bf16[8,80,128]{2,1,0:T(8,128)(2,1)S(1)}, u32[]{:S(2)}, u32[]{:S(2)}) collective-permute-start(bf16[8,80,128]{2,1,0:T(8,128)(2,1)S(1)} %get-tuple-element.27), channel_id=1, source_target_pairs={{0,1},{1,0},{2,3},{3,2},{4,5},{5,4},{6,7},{7,6},{8,9},{9,8},{10,11... | collective-permute-start | bytes 491528 | tf_op jit(solution)/shard_map/ppermute | solution.py:52
  11.9 1.5 %collective-permute-start.2 = (bf16[8,128,128]{2,1,0:T(8,128)(2,1)S(1)}, bf16[8,128,128]{2,1,0:T(8,128)(2,1)S(1)}, u32[]{:S(2)}, u32[]{:S(2)}) collective-permute-start(bf16[8,128,128]{2,1,0:T(8,128)(2,1)S(1)} %collective-permute-done.rest_1_), channel_id=1, source_target_pairs={{0,1},{1,0},{2,3},{3,2},{4,5},{5,4},{6,7},{7,6},{8,9},{9,8},{10,11... | collective-permute-start | bytes 786440 | tf_op jit(solution)/shard_map/ppermute | solution.py:52
  14.5 1.4 %collective-permute-start.4 = (bf16[4,128,128]{2,1,0:T(8,128)(2,1)S(1)}, bf16[4,128,128]{2,1,0:T(8,128)(2,1)S(1)}, u32[]{:S(2)}, u32[]{:S(2)}) collective-permute-start(bf16[4,128,128]{2,1,0:T(8,128)(2,1)S(1)} %collective-permute-done.3.rest_5_), channel_id=1, source_target_pairs={{0,1},{1,0},{2,3},{3,2},{4,5},{5,4},{6,7},{7,6},{8,9},{9,8},{10,11... | collective-permute-start | bytes 393224 | tf_op jit(solution)/shard_map/ppermute | solution.py:52
  17.0 1.7 %collective-permute-start.7 = (bf16[4,128,128]{2,1,0:T(8,128)(2,1)S(1)}, bf16[4,128,128]{2,1,0:T(8,128)(2,1)S(1)}, u32[]{:S(2)}, u32[]{:S(2)}) collective-permute-start(bf16[4,128,128]{2,1,0:T(8,128)(2,1)S(1)} %collective-permute-done.6.rest_5_), channel_id=1, source_target_pairs={{0,1},{1,0},{2,3},{3,2},{4,5},{5,4},{6,7},{7,6},{8,9},{9,8},{10,11... | collective-permute-start | bytes 393224 | tf_op jit(solution)/shard_map/ppermute | solution.py:52
  17.3 4.5 %collective-permute-start.5 = (bf16[32,1024]{1,0:T(8,128)(2,1)S(1)}, bf16[32,1024]{1,0:T(8,128)(2,1)S(1)}, u32[]{:S(2)}, u32[]{:S(2)}) collective-permute-start(bf16[32,1024]{1,0:T(8,128)(2,1)S(1)} %get-tuple-element.38), channel_id=1, source_target_pairs={{0,3},{1,2},{2,1},{3,0},{4,7},{5,6},{6,5},{7,4},{8,11},{9,10},{10,... | collective-permute-start | bytes 196616 | tf_op jit(solution)/shard_map/ppermute | solution.py:52
  19.7 4.1 %collective-permute-start.8 = (bf16[32,1024]{1,0:T(8,128)(2,1)S(1)}, bf16[32,1024]{1,0:T(8,128)(2,1)S(1)}, u32[]{:S(2)}, u32[]{:S(2)}) collective-permute-start(bf16[32,1024]{1,0:T(8,128)(2,1)S(1)} %block_outputs.5), channel_id=1, source_target_pairs={{0,3},{1,2},{2,1},{3,0},{4,7},{5,6},{6,5},{7,4},{8,11},{9,10},{10,... | collective-permute-start | bytes 196616 | tf_op jit(solution)/shard_map/ppermute | solution.py:52

commit v12 on v11

--- a/solution.py
+++ b/solution.py
@@ -293,15 +293,17 @@
 
 
 def join_kernel(*refs, share, width):
-    *pieces, out_ref = refs
+    *pieces, out_hbm, held, left = refs
     place = lax.axis_index("head")
     chips = len(pieces) // 2
-    rows = out_ref.shape[0]
+    rows = held.shape[0]
     pairs = pieces[0].shape[1] // width // share
+    size = 2 * pairs * width
     low = lower_half((rows, width))
+    copies = []
     for n in range(chips):
         for part in range(share):
-            column = jnp.bitwise_xor(place, across(n, share) ^ part) * (2 * pairs * width)
+            base = (n * share + part) * size
             for pair in range(pairs):
                 at = (part * pairs + pair) * width
                 first, second = (
@@ -311,17 +313,32 @@
                 even = jnp.where(low, first, second)
                 odd = pltpu.roll(jnp.where(low, second, first), width // 2, 1)
                 for m, out in enumerate((even, odd)):
-                    to = pl.multiple_of(column + (2 * pair + m) * width, width)
-                    out_ref[:, pl.ds(to, width)] = out.astype(jnp.bfloat16)
+                    to = base + (2 * pair + m) * width
+                    held[:, to : to + width] = out.astype(jnp.bfloat16)
+            column = jnp.bitwise_xor(place, across(n, share) ^ part) * size
+            copy = pltpu.make_async_copy(
+                held.at[:, pl.ds(base, size)],
+                out_hbm.at[:, pl.ds(pl.multiple_of(column, size), size)],
+                left.at[n * share + part],
+            )
+            copy.start()
+            copies.append(copy)
+    for copy in copies:
+        copy.wait()
 
 
 def join_pieces(pieces, share, width):
-    rows, across = pieces[0].shape
+    rows, columns = pieces[0].shape
+    shape = (rows, columns * len(pieces))
     return pl.pallas_call(
         functools.partial(join_kernel, share=share, width=width),
         in_specs=[in_vmem] * len(pieces),
-        out_specs=in_vmem,
-        out_shape=jax.ShapeDtypeStruct((rows, across * len(pieces)), jnp.bfloat16),
+        out_specs=pl.BlockSpec(memory_space=pltpu.HBM),
+        out_shape=jax.ShapeDtypeStruct(shape, jnp.bfloat16),
+        scratch_shapes=[
+            pltpu.VMEM(shape, jnp.bfloat16),
+            pltpu.SemaphoreType.DMA((len(pieces) // 2 * share,)),
+        ],
         compiler_params=granted,
         name="join_pieces",
     )(*pieces)

time: 24.8 us -> 24.8 us (level)
  no operation moved by 1% of the time
where the time goes in v12:
time: 24.8 us; the launch traced here: 24.6 us
  starting transfers between devices  10.2 us (41%)
  Pallas kernels  8.22 us (33%)
  waiting for transfers between devices  5.27 us (21%)
  other arithmetic  0.54 us (2%)
  local copies, waits for them, and re-layouts  0.26 us (1%)
    ppermute x6, starting transfers between devices, swapped(): lax.ppermute(x, 'head', [(i, i ^ mask) for i in range(lax.axis_size('head...  5.82 us
    ppermute x3, starting transfers between devices, sent(): return lax.ppermute(x, ('ctx', 'head'), moves)  4.34 us
    ppermute x6, waiting for transfers between devices, swapped(): lax.ppermute(x, 'head', [(i, i ^ mask) for i in range(lax.axis_size('head...  3.61 us
    pallas_call x3, Pallas kernels, block_outputs(): pl.pallas_call(functools.partial(value_kernel, inputs=len(parts), flip=fl...  3.01 us
    pallas_call x2, Pallas kernels, begin(): pl.pallas_call(kernel, in_specs=[pl.BlockSpec(memory_space=pltpu.HBM)] *...  2.28 us
    pallas_call x2, Pallas kernels, block_weights(): pl.pallas_call(functools.partial(score_kernel, inputs=len(parts)) if len(...  1.91 us
    ppermute x3, waiting for transfers between devices, sent(): return lax.ppermute(x, ('ctx', 'head'), moves)  1.66 us
    pallas_call x1, Pallas kernels, join_pieces(): pl.pallas_call(functools.partial(join_kernel, share=share, width=width),...  0.81 us
  transfers between devices with their start and end apart: 9, of which 5 were waited for; matrix products, arithmetic and copies ran while one was open for 3% of the time, Pallas kernels for 26%

profile of v12, /device:TPU:0, one launch (start us, length us, event | category | flops | bytes accessed | tf_op | source)
XLA Modules:
  0.0 24.6 jit_solution(10231259043213003057)
XLA Ops:
  0.0 1.0 %key_kernel.1._.rest_0_ = bf16[8,128,128]{2,1,0:T(8,128)(2,1)S(1)} custom-call(s32[2,2,8]{2,1,0:T(2,128)} %index_hbm.3, f32[2,16]{1,0:T(2,128)} %table_hbm.3, bf16[2,1024,128]{2,1,0:T(8,128)(2,1)} %codes_hbm.2), custom_call_target="tpu_custom_call" | custom-call | tf_op jit(solution)/shard_map/key_kernel/pallas_call | solution.py:122
  1.0 2.5 %collective-permute-start = (bf16[8,128,128]{2,1,0:T(8,128)(2,1)S(1)}, bf16[8,128,128]{2,1,0:T(8,128)(2,1)S(1)}, u32[]{:S(2)}, u32[]{:S(2)}) collective-permute-start(bf16[8,128,128]{2,1,0:T(8,128)(2,1)S(1)} %key_kernel.1._.rest_0_), channel_id=1, source_target_pairs={{5,0},{13,1},{7,2},{15,3},{8,4},{0,5},{10,6},{2,7},{4,8},{12,9},{6... | collective-permute-start | bytes 786440 | tf_op jit(solution)/shard_map/ppermute | solution.py:44
  3.6 1.3 %half_kernel.1 = (bf16[4,128,128]{2,1,0:T(8,128)(2,1)S(1)}, bf16[4,128,128]{2,1,0:T(8,128)(2,1)S(1)}, bf16[1024,128]{1,0:T(8,128)(2,1)S(1)}, s32[128]{0:T(128)S(1)}, s32[8,4,8]{2,1,0:T(4,128)S(1)}) custom-call(s32[2,2,8]{2,1,0:T(2,128)} %index_hbm.3, f32[2,16]{1,0:T(2,128)} %table_hbm.3, bf16[2,1024,128]{2,1,0:T(8,128)(2,1)} %codes_hbm.3, ...), custom_call_target="tpu_custom_call" | custom-call | tf_op jit(solution)/shard_map/half_kernel/pallas_call | solution.py:122
  4.8 0.1 collective-permute-start.3
  4.9 1.7 %collective-permute-start.6 = (bf16[4,128,128]{2,1,0:T(8,128)(2,1)S(1)}, bf16[4,128,128]{2,1,0:T(8,128)(2,1)S(1)}, u32[]{:S(2)}, u32[]{:S(2)}) collective-permute-start(bf16[4,128,128]{2,1,0:T(8,128)(2,1)S(1)} %get-tuple-element.39.rest_4_), channel_id=1, source_target_pairs={{5,0},{13,1},{7,2},{15,3},{8,4},{0,5},{10,6},{2,7},{4,8},{12,9},{6... | collective-permute-start | bytes 393224 | tf_op jit(solution)/shard_map/ppermute | solution.py:44
  6.9 0.1 convert_element_type.35
  7.0 0.3 %fusion = (f32[128,128]{1,0:T(8,128)S(1)}, f32[128,128]{1,0:T(8,128)S(1)}) fusion(f32[128]{0:T(128)S(1)} %get-tuple-element.56, f32[128]{0:T(128)S(1)} %get-tuple-element.57, f32[128]{0:T(128)S(1)} %convert_element_type.35), kind=kLoop, calls=%fused_computation.3 | loop fusion | flops 32768 | bytes 132608 | tf_op jit(solution)/shard_map/mul | solution.py:400
  7.3 0.2 turn_queries.1
  7.6 1.7 %collective-permute-done.rest_1_ = bf16[8,128,128]{2,1,0:T(8,128)(2,1)S(1)} collective-permute-done((bf16[8,128,128]{2,1,0:T(8,128)(2,1)S(1)}, bf16[8,128,128]{2,1,0:T(8,128)(2,1)S(1)}, u32[]{:S(2)}, u32[]{:S(2)}) %collective-permute-start) | collective-permute-done | bytes 262176 | tf_op jit(solution)/shard_map/ppermute | solution.py:44
  9.2 2.7 %collective-permute-start.1 = (bf16[8,80,128]{2,1,0:T(8,128)(2,1)S(1)}, bf16[8,80,128]{2,1,0:T(8,128)(2,1)S(1)}, u32[]{:S(2)}, u32[]{:S(2)}) collective-permute-start(bf16[8,80,128]{2,1,0:T(8,128)(2,1)S(1)} %get-tuple-element.27), channel_id=1, source_target_pairs={{0,1},{1,0},{2,3},{3,2},{4,5},{5,4},{6,7},{7,6},{8,9},{9,8},{10,11... | collective-permute-start | bytes 491528 | tf_op jit(solution)/shard_map/ppermute | solution.py:52
  12.0 1.0 %collective-permute-done.1.queries_ref = bf16[8,80,128]{2,1,0:T(8,128)(2,1)S(1)} collective-permute-done((bf16[8,80,128]{2,1,0:T(8,128)(2,1)S(1)}, bf16[8,80,128]{2,1,0:T(8,128)(2,1)S(1)}, u32[]{:S(2)}, u32[]{:S(2)}) %collective-permute-start.1) | collective-permute-done | bytes 163872 | tf_op jit(solution)/shard_map/ppermute | solution.py:52
  13.0 0.4 %collective-permute-done.2.rest_2_ = bf16[8,128,128]{2,1,0:T(8,128)(2,1)S(1)} collective-permute-done((bf16[8,128,128]{2,1,0:T(8,128)(2,1)S(1)}, bf16[8,128,128]{2,1,0:T(8,128)(2,1)S(1)}, u32[]{:S(2)}, u32[]{:S(2)}) %collective-permute-start.2) | collective-permute-done | bytes 262176 | tf_op jit(solution)/shard_map/ppermute | solution.py:52
  13.4 1.1 %block_weights.2 = (bf16[8,64,1024]{2,1,0:T(8,128)(2,1)S(1)}, f32[8,64,128]{2,1,0:T(8,128)S(1)}, bf16[24,128,128]{2,1,0:T(8,128)(2,1)S(1)}) custom-call(s32[8,8]{1,0:T(8,128)S(1)} %get-tuple-element.49.slots_ref, bf16[8,64,128]{2,1,0:T(8,128)(2,1)S(1)} %get-tuple-element.28.queries_ref, bf16[8,128,128]{2,1,0:T(8,128)(2,1)S(1)} %key_kernel.1._.rest_0_, ...), custom_call_target="tpu_custom_call" | custom-call | tf_op jit(solution)/shard_map/block_weights/pallas_call | solution.py:226
  14.5 0.3 %collective-permute-start.4 = (bf16[4,128,128]{2,1,0:T(8,128)(2,1)S(1)}, bf16[4,128,128]{2,1,0:T(8,128)(2,1)S(1)}, u32[]{:S(2)}, u32[]{:S(2)}) collective-permute-start(bf16[4,128,128]{2,1,0:T(8,128)(2,1)S(1)} %collective-permute-done.3.rest_5_), channel_id=1, source_target_pairs={{0,1},{1,0},{2,3},{3,2},{4,5},{5,4},{6,7},{7,6},{8,9},{9,8},{10,11... | collective-permute-start | bytes 393224 | tf_op jit(solution)/shard_map/ppermute | solution.py:52
  14.9 0.8 %block_weights.3 = (bf16[8,64,1024]{2,1,0:T(8,128)(2,1)S(1)}, f32[8,64,128]{2,1,0:T(8,128)S(1)}) custom-call(s32[8,8]{1,0:T(8,128)S(1)} %get-tuple-element.48.slots_ref, bf16[8,80,128]{2,1,0:T(8,128)(2,1)S(1)} %collective-permute-done.1.queries_ref, bf16[24,128,128]{2,1,0:T(8,128)(2,1)S(1)} %get-tuple-element.31.store), custom_call_target="tpu_custom_call" | custom-call | tf_op jit(solution)/shard_map/block_weights/pallas_call | solution.py:226
  15.7 0.2 collective-permute-done.4.rest_6_
  15.9 1.1 %block_outputs.3 = (bf16[32,1024]{1,0:T(8,128)(2,1)S(1)}, bf16[32,1024]{1,0:T(8,128)(2,1)S(1)}) custom-call(s32[16,8]{1,0:T(8,128)S(1)} %multiply_add_fusion.1.slots_ref, bf16[8,64,1024]{2,1,0:T(8,128)(2,1)S(1)} %get-tuple-element.30.rest_0_, bf16[8,64,1024]{2,1,0:T(8,128)(2,1)S(1)} %get-tuple-element.32.rest_1_, ...), custom_call_target="tpu_custom_call" | custom-call | tf_op jit(solution)/shard_map/block_outputs/pallas_call | solution.py:278
  17.0 0.3 %collective-permute-start.7 = (bf16[4,128,128]{2,1,0:T(8,128)(2,1)S(1)}, bf16[4,128,128]{2,1,0:T(8,128)(2,1)S(1)}, u32[]{:S(2)}, u32[]{:S(2)}) collective-permute-start(bf16[4,128,128]{2,1,0:T(8,128)(2,1)S(1)} %collective-permute-done.6.rest_5_), channel_id=1, source_target_pairs={{0,1},{1,0},{2,3},{3,2},{4,5},{5,4},{6,7},{7,6},{8,9},{9,8},{10,11... | collective-permute-start | bytes 393224 | tf_op jit(solution)/shard_map/ppermute | solution.py:52
  17.3 1.4 %collective-permute-start.5 = (bf16[32,1024]{1,0:T(8,128)(2,1)S(1)}, bf16[32,1024]{1,0:T(8,128)(2,1)S(1)}, u32[]{:S(2)}, u32[]{:S(2)}) collective-permute-start(bf16[32,1024]{1,0:T(8,128)(2,1)S(1)} %get-tuple-element.38), channel_id=1, source_target_pairs={{0,3},{1,2},{2,1},{3,0},{4,7},{5,6},{6,5},{7,4},{8,11},{9,10},{10,... | collective-permute-start | bytes 196616 | tf_op jit(solution)/shard_map/ppermute | solution.py:52
  18.7 1.0 %block_outputs.5 = bf16[32,1024]{1,0:T(8,128)(2,1)S(1)} custom-call(s32[16,8]{1,0:T(8,128)S(1)} %get-tuple-element.41.slots_ref, bf16[8,64,1024]{2,1,0:T(8,128)(2,1)S(1)} %get-tuple-element.30.rest_0_, bf16[8,64,1024]{2,1,0:T(8,128)(2,1)S(1)} %get-tuple-element.32.rest_1_, f32[8,64,128]{2,1,0:T(8,128)S(1)} %get-tuple-element.33.rest_2_, ...), custom_call_target="tpu_custom_call" | custom-call | tf_op jit(solution)/shard_map/block_outputs/pallas_call | solution.py:278
  19.7 1.1 %collective-permute-start.8 = (bf16[32,1024]{1,0:T(8,128)(2,1)S(1)}, bf16[32,1024]{1,0:T(8,128)(2,1)S(1)}, u32[]{:S(2)}, u32[]{:S(2)}) collective-permute-start(bf16[32,1024]{1,0:T(8,128)(2,1)S(1)} %block_outputs.5), channel_id=1, source_target_pairs={{0,3},{1,2},{2,1},{3,0},{4,7},{5,6},{6,5},{7,4},{8,11},{9,10},{10,... | collective-permute-start | bytes 196616 | tf_op jit(solution)/shard_map/ppermute | solution.py:52
  20.8 1.0 %block_outputs.4.refs_2_ = bf16[32,1024]{1,0:T(8,128)(2,1)S(1)} custom-call(s32[16,8]{1,0:T(8,128)S(1)} %get-tuple-element.41.slots_ref, bf16[8,64,1024]{2,1,0:T(8,128)(2,1)S(1)} %get-tuple-element.30.rest_0_, bf16[8,64,1024]{2,1,0:T(8,128)(2,1)S(1)} %get-tuple-element.32.rest_1_, f32[8,64,128]{2,1,0:T(8,128)S(1)} %get-tuple-element.33.rest_2_, ...), custom_call_target="tpu_custom_call" | custom-call | tf_op jit(solution)/shard_map/block_outputs/pallas_call | solution.py:278
  21.8 2.0 %collective-permute-done.8.refs_3_ = bf16[32,1024]{1,0:T(8,128)(2,1)S(1)} collective-permute-done((bf16[32,1024]{1,0:T(8,128)(2,1)S(1)}, bf16[32,1024]{1,0:T(8,128)(2,1)S(1)}, u32[]{:S(2)}, u32[]{:S(2)}) %collective-permute-start.8) | collective-permute-done | bytes 65568 | tf_op jit(solution)/shard_map/ppermute | solution.py:52
  23.8 0.8 %join_pieces.1 = bf16[32,4096]{1,0:T(8,128)(2,1)} custom-call(bf16[32,1024]{1,0:T(8,128)(2,1)S(1)} %get-tuple-element.37.refs_0_, bf16[32,1024]{1,0:T(8,128)(2,1)S(1)} %collective-permute-done.5.refs_1_, bf16[32,1024]{1,0:T(8,128)(2,1)S(1)} %block_outputs.4.refs_2_, bf16[32,1024]{1,0:T(8,128)(2,1)S(1)} %collective-permute-done.8.refs_3_), custom_call_target="tpu_custom_call" | custom-call | tf_op jit(solution)/shard_map/join_pieces/pallas_call | solution.py:333
  (24 shorter events, 0.5 us)
Async XLA Ops:
  1.0 8.2 %collective-permute-start = (bf16[8,128,128]{2,1,0:T(8,128)(2,1)S(1)}, bf16[8,128,128]{2,1,0:T(8,128)(2,1)S(1)}, u32[]{:S(2)}, u32[]{:S(2)}) collective-permute-start(bf16[8,128,128]{2,1,0:T(8,128)(2,1)S(1)} %key_kernel.1._.rest_0_), channel_id=1, source_target_pairs={{5,0},{13,1},{7,2},{15,3},{8,4},{0,5},{10,6},{2,7},{4,8},{12,9},{6... | collective-permute-start | bytes 786440 | tf_op jit(solution)/shard_map/ppermute | solution.py:44
  4.8 9.7 %collective-permute-start.3 = (bf16[4,128,128]{2,1,0:T(8,128)(2,1)S(1)}, bf16[4,128,128]{2,1,0:T(8,128)(2,1)S(1)}, u32[]{:S(2)}, u32[]{:S(2)}) collective-permute-start(bf16[4,128,128]{2,1,0:T(8,128)(2,1)S(1)} %get-tuple-element.35.rest_4_), channel_id=1, source_target_pairs={{5,0},{13,1},{7,2},{15,3},{8,4},{0,5},{10,6},{2,7},{4,8},{12,9},{6... | collective-permute-start | bytes 393224 | tf_op jit(solution)/shard_map/ppermute | solution.py:44
  4.9 12.1 %collective-permute-start.6 = (bf16[4,128,128]{2,1,0:T(8,128)(2,1)S(1)}, bf16[4,128,128]{2,1,0:T(8,128)(2,1)S(1)}, u32[]{:S(2)}, u32[]{:S(2)}) collective-permute-start(bf16[4,128,128]{2,1,0:T(8,128)(2,1)S(1)} %get-tuple-element.39.rest_4_), channel_id=1, source_target_pairs={{5,0},{13,1},{7,2},{15,3},{8,4},{0,5},{10,6},{2,7},{4,8},{12,9},{6... | collective-permute-start | bytes 393224 | tf_op jit(solution)/shard_map/ppermute | solution.py:44
  9.2 3.7 %collective-permute-start.1 = (bf16[8,80,128]{2,1,0:T(8,128)(2,1)S(1)}, bf16[8,80,128]{2,1,0:T(8,128)(2,1)S(1)}, u32[]{:S(2)}, u32[]{:S(2)}) collective-permute-start(bf16[8,80,128]{2,1,0:T(8,128)(2,1)S(1)} %get-tuple-element.27), channel_id=1, source_target_pairs={{0,1},{1,0},{2,3},{3,2},{4,5},{5,4},{6,7},{7,6},{8,9},{9,8},{10,11... | collective-permute-start | bytes 491528 | tf_op jit(solution)/shard_map/ppermute | solution.py:52
  11.9 1.5 %collective-permute-start.2 = (bf16[8,128,128]{2,1,0:T(8,128)(2,1)S(1)}, bf16[8,128,128]{2,1,0:T(8,128)(2,1)S(1)}, u32[]{:S(2)}, u32[]{:S(2)}) collective-permute-start(bf16[8,128,128]{2,1,0:T(8,128)(2,1)S(1)} %collective-permute-done.rest_1_), channel_id=1, source_target_pairs={{0,1},{1,0},{2,3},{3,2},{4,5},{5,4},{6,7},{7,6},{8,9},{9,8},{10,11... | collective-permute-start | bytes 786440 | tf_op jit(solution)/shard_map/ppermute | solution.py:52
  14.5 1.4 %collective-permute-start.4 = (bf16[4,128,128]{2,1,0:T(8,128)(2,1)S(1)}, bf16[4,128,128]{2,1,0:T(8,128)(2,1)S(1)}, u32[]{:S(2)}, u32[]{:S(2)}) collective-permute-start(bf16[4,128,128]{2,1,0:T(8,128)(2,1)S(1)} %collective-permute-done.3.rest_5_), channel_id=1, source_target_pairs={{0,1},{1,0},{2,3},{3,2},{4,5},{5,4},{6,7},{7,6},{8,9},{9,8},{10,11... | collective-permute-start | bytes 393224 | tf_op jit(solution)/shard_map/ppermute | solution.py:52
  17.0 1.7 %collective-permute-start.7 = (bf16[4,128,128]{2,1,0:T(8,128)(2,1)S(1)}, bf16[4,128,128]{2,1,0:T(8,128)(2,1)S(1)}, u32[]{:S(2)}, u32[]{:S(2)}) collective-permute-start(bf16[4,128,128]{2,1,0:T(8,128)(2,1)S(1)} %collective-permute-done.6.rest_5_), channel_id=1, source_target_pairs={{0,1},{1,0},{2,3},{3,2},{4,5},{5,4},{6,7},{7,6},{8,9},{9,8},{10,11... | collective-permute-start | bytes 393224 | tf_op jit(solution)/shard_map/ppermute | solution.py:52
  17.3 4.5 %collective-permute-start.5 = (bf16[32,1024]{1,0:T(8,128)(2,1)S(1)}, bf16[32,1024]{1,0:T(8,128)(2,1)S(1)}, u32[]{:S(2)}, u32[]{:S(2)}) collective-permute-start(bf16[32,1024]{1,0:T(8,128)(2,1)S(1)} %get-tuple-element.38), channel_id=1, source_target_pairs={{0,3},{1,2},{2,1},{3,0},{4,7},{5,6},{6,5},{7,4},{8,11},{9,10},{10,... | collective-permute-start | bytes 196616 | tf_op jit(solution)/shard_map/ppermute | solution.py:52
  19.7 4.1 %collective-permute-start.8 = (bf16[32,1024]{1,0:T(8,128)(2,1)S(1)}, bf16[32,1024]{1,0:T(8,128)(2,1)S(1)}, u32[]{:S(2)}, u32[]{:S(2)}) collective-permute-start(bf16[32,1024]{1,0:T(8,128)(2,1)S(1)} %block_outputs.5), channel_id=1, source_target_pairs={{0,3},{1,2},{2,1},{3,0},{4,7},{5,6},{6,5},{7,4},{8,11},{9,10},{10,... | collective-permute-start | bytes 196616 | tf_op jit(solution)/shard_map/ppermute | solution.py:52

commit v13 on v12

--- a/solution.py
+++ b/solution.py
@@ -11,7 +11,7 @@
 GROUP = 16
 BLOCK = 128
 ROW_TILE = 16
-ABREAST = 2
+ABREAST = 4
 ROPE_BASE = 500000.0
 VMEM_GRANT = 16 * 2**20
 

time: 24.8 us -> 24.8 us (level)
  no operation moved by 1% of the time
where the time goes in v13:
time: 24.8 us; the launch traced here: 24.6 us
  starting transfers between devices  10.2 us (41%)
  Pallas kernels  8.22 us (33%)
  waiting for transfers between devices  5.27 us (21%)
  other arithmetic  0.54 us (2%)
  local copies, waits for them, and re-layouts  0.26 us (1%)
    ppermute x6, starting transfers between devices, swapped(): lax.ppermute(x, 'head', [(i, i ^ mask) for i in range(lax.axis_size('head...  5.82 us
    ppermute x3, starting transfers between devices, sent(): return lax.ppermute(x, ('ctx', 'head'), moves)  4.34 us
    ppermute x6, waiting for transfers between devices, swapped(): lax.ppermute(x, 'head', [(i, i ^ mask) for i in range(lax.axis_size('head...  3.61 us
    pallas_call x3, Pallas kernels, block_outputs(): pl.pallas_call(functools.partial(value_kernel, inputs=len(parts), flip=fl...  3.01 us
    pallas_call x2, Pallas kernels, begin(): pl.pallas_call(kernel, in_specs=[pl.BlockSpec(memory_space=pltpu.HBM)] *...  2.28 us
    pallas_call x2, Pallas kernels, block_weights(): pl.pallas_call(functools.partial(score_kernel, inputs=len(parts)) if len(...  1.91 us
    ppermute x3, waiting for transfers between devices, sent(): return lax.ppermute(x, ('ctx', 'head'), moves)  1.66 us
    pallas_call x1, Pallas kernels, join_pieces(): pl.pallas_call(functools.partial(join_kernel, share=share, width=width),...  0.81 us
  transfers between devices with their start and end apart: 9, of which 5 were waited for; matrix products, arithmetic and copies ran while one was open for 3% of the time, Pallas kernels for 26%

profile of v13, /device:TPU:0, one launch (start us, length us, event | category | flops | bytes accessed | tf_op | source)
XLA Modules:
  0.0 24.6 jit_solution(10231259043213003057)
XLA Ops:
  0.0 1.0 %key_kernel.1._.rest_0_ = bf16[8,128,128]{2,1,0:T(8,128)(2,1)S(1)} custom-call(s32[2,2,8]{2,1,0:T(2,128)} %index_hbm.3, f32[2,16]{1,0:T(2,128)} %table_hbm.3, bf16[2,1024,128]{2,1,0:T(8,128)(2,1)} %codes_hbm.2), custom_call_target="tpu_custom_call" | custom-call | tf_op jit(solution)/shard_map/key_kernel/pallas_call | solution.py:122
  1.0 2.5 %collective-permute-start = (bf16[8,128,128]{2,1,0:T(8,128)(2,1)S(1)}, bf16[8,128,128]{2,1,0:T(8,128)(2,1)S(1)}, u32[]{:S(2)}, u32[]{:S(2)}) collective-permute-start(bf16[8,128,128]{2,1,0:T(8,128)(2,1)S(1)} %key_kernel.1._.rest_0_), channel_id=1, source_target_pairs={{5,0},{13,1},{7,2},{15,3},{8,4},{0,5},{10,6},{2,7},{4,8},{12,9},{6... | collective-permute-start | bytes 786440 | tf_op jit(solution)/shard_map/ppermute | solution.py:44
  3.6 1.3 %half_kernel.1 = (bf16[4,128,128]{2,1,0:T(8,128)(2,1)S(1)}, bf16[4,128,128]{2,1,0:T(8,128)(2,1)S(1)}, bf16[1024,128]{1,0:T(8,128)(2,1)S(1)}, s32[128]{0:T(128)S(1)}, s32[8,4,8]{2,1,0:T(4,128)S(1)}) custom-call(s32[2,2,8]{2,1,0:T(2,128)} %index_hbm.3, f32[2,16]{1,0:T(2,128)} %table_hbm.3, bf16[2,1024,128]{2,1,0:T(8,128)(2,1)} %codes_hbm.3, ...), custom_call_target="tpu_custom_call" | custom-call | tf_op jit(solution)/shard_map/half_kernel/pallas_call | solution.py:122
  4.8 0.1 collective-permute-start.3
  4.9 1.7 %collective-permute-start.6 = (bf16[4,128,128]{2,1,0:T(8,128)(2,1)S(1)}, bf16[4,128,128]{2,1,0:T(8,128)(2,1)S(1)}, u32[]{:S(2)}, u32[]{:S(2)}) collective-permute-start(bf16[4,128,128]{2,1,0:T(8,128)(2,1)S(1)} %get-tuple-element.39.rest_4_), channel_id=1, source_target_pairs={{5,0},{13,1},{7,2},{15,3},{8,4},{0,5},{10,6},{2,7},{4,8},{12,9},{6... | collective-permute-start | bytes 393224 | tf_op jit(solution)/shard_map/ppermute | solution.py:44
  6.9 0.1 convert_element_type.35
  7.0 0.3 %fusion = (f32[128,128]{1,0:T(8,128)S(1)}, f32[128,128]{1,0:T(8,128)S(1)}) fusion(f32[128]{0:T(128)S(1)} %get-tuple-element.56, f32[128]{0:T(128)S(1)} %get-tuple-element.57, f32[128]{0:T(128)S(1)} %convert_element_type.35), kind=kLoop, calls=%fused_computation.3 | loop fusion | flops 32768 | bytes 132608 | tf_op jit(solution)/shard_map/mul | solution.py:400
  7.3 0.2 turn_queries.1
  7.6 1.7 %collective-permute-done.rest_1_ = bf16[8,128,128]{2,1,0:T(8,128)(2,1)S(1)} collective-permute-done((bf16[8,128,128]{2,1,0:T(8,128)(2,1)S(1)}, bf16[8,128,128]{2,1,0:T(8,128)(2,1)S(1)}, u32[]{:S(2)}, u32[]{:S(2)}) %collective-permute-start) | collective-permute-done | bytes 262176 | tf_op jit(solution)/shard_map/ppermute | solution.py:44
  9.2 2.7 %collective-permute-start.1 = (bf16[8,80,128]{2,1,0:T(8,128)(2,1)S(1)}, bf16[8,80,128]{2,1,0:T(8,128)(2,1)S(1)}, u32[]{:S(2)}, u32[]{:S(2)}) collective-permute-start(bf16[8,80,128]{2,1,0:T(8,128)(2,1)S(1)} %get-tuple-element.27), channel_id=1, source_target_pairs={{0,1},{1,0},{2,3},{3,2},{4,5},{5,4},{6,7},{7,6},{8,9},{9,8},{10,11... | collective-permute-start | bytes 491528 | tf_op jit(solution)/shard_map/ppermute | solution.py:52
  12.0 1.0 %collective-permute-done.1.queries_ref = bf16[8,80,128]{2,1,0:T(8,128)(2,1)S(1)} collective-permute-done((bf16[8,80,128]{2,1,0:T(8,128)(2,1)S(1)}, bf16[8,80,128]{2,1,0:T(8,128)(2,1)S(1)}, u32[]{:S(2)}, u32[]{:S(2)}) %collective-permute-start.1) | collective-permute-done | bytes 163872 | tf_op jit(solution)/shard_map/ppermute | solution.py:52
  13.0 0.4 %collective-permute-done.2.rest_2_ = bf16[8,128,128]{2,1,0:T(8,128)(2,1)S(1)} collective-permute-done((bf16[8,128,128]{2,1,0:T(8,128)(2,1)S(1)}, bf16[8,128,128]{2,1,0:T(8,128)(2,1)S(1)}, u32[]{:S(2)}, u32[]{:S(2)}) %collective-permute-start.2) | collective-permute-done | bytes 262176 | tf_op jit(solution)/shard_map/ppermute | solution.py:52
  13.4 1.1 %block_weights.2 = (bf16[8,64,1024]{2,1,0:T(8,128)(2,1)S(1)}, f32[8,64,128]{2,1,0:T(8,128)S(1)}, bf16[24,128,128]{2,1,0:T(8,128)(2,1)S(1)}) custom-call(s32[8,8]{1,0:T(8,128)S(1)} %get-tuple-element.49.slots_ref, bf16[8,64,128]{2,1,0:T(8,128)(2,1)S(1)} %get-tuple-element.28.queries_ref, bf16[8,128,128]{2,1,0:T(8,128)(2,1)S(1)} %key_kernel.1._.rest_0_, ...), custom_call_target="tpu_custom_call" | custom-call | tf_op jit(solution)/shard_map/block_weights/pallas_call | solution.py:226
  14.5 0.3 %collective-permute-start.4 = (bf16[4,128,128]{2,1,0:T(8,128)(2,1)S(1)}, bf16[4,128,128]{2,1,0:T(8,128)(2,1)S(1)}, u32[]{:S(2)}, u32[]{:S(2)}) collective-permute-start(bf16[4,128,128]{2,1,0:T(8,128)(2,1)S(1)} %collective-permute-done.3.rest_5_), channel_id=1, source_target_pairs={{0,1},{1,0},{2,3},{3,2},{4,5},{5,4},{6,7},{7,6},{8,9},{9,8},{10,11... | collective-permute-start | bytes 393224 | tf_op jit(solution)/shard_map/ppermute | solution.py:52
  14.9 0.8 %block_weights.3 = (bf16[8,64,1024]{2,1,0:T(8,128)(2,1)S(1)}, f32[8,64,128]{2,1,0:T(8,128)S(1)}) custom-call(s32[8,8]{1,0:T(8,128)S(1)} %get-tuple-element.48.slots_ref, bf16[8,80,128]{2,1,0:T(8,128)(2,1)S(1)} %collective-permute-done.1.queries_ref, bf16[24,128,128]{2,1,0:T(8,128)(2,1)S(1)} %get-tuple-element.31.store), custom_call_target="tpu_custom_call" | custom-call | tf_op jit(solution)/shard_map/block_weights/pallas_call | solution.py:226
  15.7 0.2 collective-permute-done.4.rest_6_
  15.9 1.1 %block_outputs.3 = (bf16[32,1024]{1,0:T(8,128)(2,1)S(1)}, bf16[32,1024]{1,0:T(8,128)(2,1)S(1)}) custom-call(s32[16,8]{1,0:T(8,128)S(1)} %multiply_add_fusion.1.slots_ref, bf16[8,64,1024]{2,1,0:T(8,128)(2,1)S(1)} %get-tuple-element.30.rest_0_, bf16[8,64,1024]{2,1,0:T(8,128)(2,1)S(1)} %get-tuple-element.32.rest_1_, ...), custom_call_target="tpu_custom_call" | custom-call | tf_op jit(solution)/shard_map/block_outputs/pallas_call | solution.py:278
  17.0 0.3 %collective-permute-start.7 = (bf16[4,128,128]{2,1,0:T(8,128)(2,1)S(1)}, bf16[4,128,128]{2,1,0:T(8,128)(2,1)S(1)}, u32[]{:S(2)}, u32[]{:S(2)}) collective-permute-start(bf16[4,128,128]{2,1,0:T(8,128)(2,1)S(1)} %collective-permute-done.6.rest_5_), channel_id=1, source_target_pairs={{0,1},{1,0},{2,3},{3,2},{4,5},{5,4},{6,7},{7,6},{8,9},{9,8},{10,11... | collective-permute-start | bytes 393224 | tf_op jit(solution)/shard_map/ppermute | solution.py:52
  17.3 1.4 %collective-permute-start.5 = (bf16[32,1024]{1,0:T(8,128)(2,1)S(1)}, bf16[32,1024]{1,0:T(8,128)(2,1)S(1)}, u32[]{:S(2)}, u32[]{:S(2)}) collective-permute-start(bf16[32,1024]{1,0:T(8,128)(2,1)S(1)} %get-tuple-element.38), channel_id=1, source_target_pairs={{0,3},{1,2},{2,1},{3,0},{4,7},{5,6},{6,5},{7,4},{8,11},{9,10},{10,... | collective-permute-start | bytes 196616 | tf_op jit(solution)/shard_map/ppermute | solution.py:52
  18.7 1.0 %block_outputs.5 = bf16[32,1024]{1,0:T(8,128)(2,1)S(1)} custom-call(s32[16,8]{1,0:T(8,128)S(1)} %get-tuple-element.41.slots_ref, bf16[8,64,1024]{2,1,0:T(8,128)(2,1)S(1)} %get-tuple-element.30.rest_0_, bf16[8,64,1024]{2,1,0:T(8,128)(2,1)S(1)} %get-tuple-element.32.rest_1_, f32[8,64,128]{2,1,0:T(8,128)S(1)} %get-tuple-element.33.rest_2_, ...), custom_call_target="tpu_custom_call" | custom-call | tf_op jit(solution)/shard_map/block_outputs/pallas_call | solution.py:278
  19.7 1.1 %collective-permute-start.8 = (bf16[32,1024]{1,0:T(8,128)(2,1)S(1)}, bf16[32,1024]{1,0:T(8,128)(2,1)S(1)}, u32[]{:S(2)}, u32[]{:S(2)}) collective-permute-start(bf16[32,1024]{1,0:T(8,128)(2,1)S(1)} %block_outputs.5), channel_id=1, source_target_pairs={{0,3},{1,2},{2,1},{3,0},{4,7},{5,6},{6,5},{7,4},{8,11},{9,10},{10,... | collective-permute-start | bytes 196616 | tf_op jit(solution)/shard_map/ppermute | solution.py:52
  20.8 1.0 %block_outputs.4.refs_2_ = bf16[32,1024]{1,0:T(8,128)(2,1)S(1)} custom-call(s32[16,8]{1,0:T(8,128)S(1)} %get-tuple-element.41.slots_ref, bf16[8,64,1024]{2,1,0:T(8,128)(2,1)S(1)} %get-tuple-element.30.rest_0_, bf16[8,64,1024]{2,1,0:T(8,128)(2,1)S(1)} %get-tuple-element.32.rest_1_, f32[8,64,128]{2,1,0:T(8,128)S(1)} %get-tuple-element.33.rest_2_, ...), custom_call_target="tpu_custom_call" | custom-call | tf_op jit(solution)/shard_map/block_outputs/pallas_call | solution.py:278
  21.8 2.0 %collective-permute-done.8.refs_3_ = bf16[32,1024]{1,0:T(8,128)(2,1)S(1)} collective-permute-done((bf16[32,1024]{1,0:T(8,128)(2,1)S(1)}, bf16[32,1024]{1,0:T(8,128)(2,1)S(1)}, u32[]{:S(2)}, u32[]{:S(2)}) %collective-permute-start.8) | collective-permute-done | bytes 65568 | tf_op jit(solution)/shard_map/ppermute | solution.py:52
  23.8 0.8 %join_pieces.1 = bf16[32,4096]{1,0:T(8,128)(2,1)} custom-call(bf16[32,1024]{1,0:T(8,128)(2,1)S(1)} %get-tuple-element.37.refs_0_, bf16[32,1024]{1,0:T(8,128)(2,1)S(1)} %collective-permute-done.5.refs_1_, bf16[32,1024]{1,0:T(8,128)(2,1)S(1)} %block_outputs.4.refs_2_, bf16[32,1024]{1,0:T(8,128)(2,1)S(1)} %collective-permute-done.8.refs_3_), custom_call_target="tpu_custom_call" | custom-call | tf_op jit(solution)/shard_map/join_pieces/pallas_call | solution.py:333
  (24 shorter events, 0.5 us)
Async XLA Ops:
  1.0 8.2 %collective-permute-start = (bf16[8,128,128]{2,1,0:T(8,128)(2,1)S(1)}, bf16[8,128,128]{2,1,0:T(8,128)(2,1)S(1)}, u32[]{:S(2)}, u32[]{:S(2)}) collective-permute-start(bf16[8,128,128]{2,1,0:T(8,128)(2,1)S(1)} %key_kernel.1._.rest_0_), channel_id=1, source_target_pairs={{5,0},{13,1},{7,2},{15,3},{8,4},{0,5},{10,6},{2,7},{4,8},{12,9},{6... | collective-permute-start | bytes 786440 | tf_op jit(solution)/shard_map/ppermute | solution.py:44
  4.8 9.7 %collective-permute-start.3 = (bf16[4,128,128]{2,1,0:T(8,128)(2,1)S(1)}, bf16[4,128,128]{2,1,0:T(8,128)(2,1)S(1)}, u32[]{:S(2)}, u32[]{:S(2)}) collective-permute-start(bf16[4,128,128]{2,1,0:T(8,128)(2,1)S(1)} %get-tuple-element.35.rest_4_), channel_id=1, source_target_pairs={{5,0},{13,1},{7,2},{15,3},{8,4},{0,5},{10,6},{2,7},{4,8},{12,9},{6... | collective-permute-start | bytes 393224 | tf_op jit(solution)/shard_map/ppermute | solution.py:44
  4.9 12.1 %collective-permute-start.6 = (bf16[4,128,128]{2,1,0:T(8,128)(2,1)S(1)}, bf16[4,128,128]{2,1,0:T(8,128)(2,1)S(1)}, u32[]{:S(2)}, u32[]{:S(2)}) collective-permute-start(bf16[4,128,128]{2,1,0:T(8,128)(2,1)S(1)} %get-tuple-element.39.rest_4_), channel_id=1, source_target_pairs={{5,0},{13,1},{7,2},{15,3},{8,4},{0,5},{10,6},{2,7},{4,8},{12,9},{6... | collective-permute-start | bytes 393224 | tf_op jit(solution)/shard_map/ppermute | solution.py:44
  9.2 3.7 %collective-permute-start.1 = (bf16[8,80,128]{2,1,0:T(8,128)(2,1)S(1)}, bf16[8,80,128]{2,1,0:T(8,128)(2,1)S(1)}, u32[]{:S(2)}, u32[]{:S(2)}) collective-permute-start(bf16[8,80,128]{2,1,0:T(8,128)(2,1)S(1)} %get-tuple-element.27), channel_id=1, source_target_pairs={{0,1},{1,0},{2,3},{3,2},{4,5},{5,4},{6,7},{7,6},{8,9},{9,8},{10,11... | collective-permute-start | bytes 491528 | tf_op jit(solution)/shard_map/ppermute | solution.py:52
  11.9 1.5 %collective-permute-start.2 = (bf16[8,128,128]{2,1,0:T(8,128)(2,1)S(1)}, bf16[8,128,128]{2,1,0:T(8,128)(2,1)S(1)}, u32[]{:S(2)}, u32[]{:S(2)}) collective-permute-start(bf16[8,128,128]{2,1,0:T(8,128)(2,1)S(1)} %collective-permute-done.rest_1_), channel_id=1, source_target_pairs={{0,1},{1,0},{2,3},{3,2},{4,5},{5,4},{6,7},{7,6},{8,9},{9,8},{10,11... | collective-permute-start | bytes 786440 | tf_op jit(solution)/shard_map/ppermute | solution.py:52
  14.5 1.4 %collective-permute-start.4 = (bf16[4,128,128]{2,1,0:T(8,128)(2,1)S(1)}, bf16[4,128,128]{2,1,0:T(8,128)(2,1)S(1)}, u32[]{:S(2)}, u32[]{:S(2)}) collective-permute-start(bf16[4,128,128]{2,1,0:T(8,128)(2,1)S(1)} %collective-permute-done.3.rest_5_), channel_id=1, source_target_pairs={{0,1},{1,0},{2,3},{3,2},{4,5},{5,4},{6,7},{7,6},{8,9},{9,8},{10,11... | collective-permute-start | bytes 393224 | tf_op jit(solution)/shard_map/ppermute | solution.py:52
  17.0 1.7 %collective-permute-start.7 = (bf16[4,128,128]{2,1,0:T(8,128)(2,1)S(1)}, bf16[4,128,128]{2,1,0:T(8,128)(2,1)S(1)}, u32[]{:S(2)}, u32[]{:S(2)}) collective-permute-start(bf16[4,128,128]{2,1,0:T(8,128)(2,1)S(1)} %collective-permute-done.6.rest_5_), channel_id=1, source_target_pairs={{0,1},{1,0},{2,3},{3,2},{4,5},{5,4},{6,7},{7,6},{8,9},{9,8},{10,11... | collective-permute-start | bytes 393224 | tf_op jit(solution)/shard_map/ppermute | solution.py:52
  17.3 4.5 %collective-permute-start.5 = (bf16[32,1024]{1,0:T(8,128)(2,1)S(1)}, bf16[32,1024]{1,0:T(8,128)(2,1)S(1)}, u32[]{:S(2)}, u32[]{:S(2)}) collective-permute-start(bf16[32,1024]{1,0:T(8,128)(2,1)S(1)} %get-tuple-element.38), channel_id=1, source_target_pairs={{0,3},{1,2},{2,1},{3,0},{4,7},{5,6},{6,5},{7,4},{8,11},{9,10},{10,... | collective-permute-start | bytes 196616 | tf_op jit(solution)/shard_map/ppermute | solution.py:52
  19.7 4.1 %collective-permute-start.8 = (bf16[32,1024]{1,0:T(8,128)(2,1)S(1)}, bf16[32,1024]{1,0:T(8,128)(2,1)S(1)}, u32[]{:S(2)}, u32[]{:S(2)}) collective-permute-start(bf16[32,1024]{1,0:T(8,128)(2,1)S(1)} %block_outputs.5), channel_id=1, source_target_pairs={{0,3},{1,2},{2,1},{3,0},{4,7},{5,6},{6,5},{7,4},{8,11},{9,10},{10,... | collective-permute-start | bytes 196616 | tf_op jit(solution)/shard_map/ppermute | solution.py:52
